TPU v7x, 512 devices: a whole 4x4x16 slice. The times are simulated.
512 devices in a mesh: row: 32 (over z_lo, x), col: 16 (over z_hi, y, core).
Axes of the slice: x: 4, y: 4, z: 16 (z_hi: 2, z_lo: 8; z = z_hi * 8 + z_lo), core: 2. Of those that a mesh axis runs over, the one named last changes fastest.
Arguments:
- amplitudes: bfloat16 [12, 1024, 1024], P(None, 'row', 'col'), may hold values from -6 to 6
- cycle_vertex: bfloat16 [12, 1024, 1024], P(None, 'row', 'col'), may hold values from -0.1875 to 0.1875
- occupied_irrep: int32 [12], replicated, may hold values from 0 to 7
- virtual_irrep: int32 [1024], replicated, may hold values from 0 to 7
Outputs:
- residual: bfloat16 [12, 1024, 12288], P(None, 'row', 'col')
Inputs may be any that keep to these rules, and one draw needn't show every extreme that they name: `occupied_irrep`: D2h irrep labels; the product of two irreps is the bitwise exclusive or of their labels. `virtual_irrep`: D2h irrep labels; the product of two irreps is the bitwise exclusive or of their labels.
All inputs are finite; a program needn't handle non-finite values.
Results may differ from a plain program's by a relative error of at most 0.01.
Values may be sent and summed in bfloat16 or wider, within the bound.
No kernel may reach another device: no remote copies, remote signals or barrier semaphores. Data moves between devices by JAX's collectives and lax.ppermute only.
A program may use at most 64 MiB of HBM per device.

v0:
```python
import jax
import jax.numpy as jnp
from jax import lax
from jax.sharding import PartitionSpec as P


def swap_residual(block):
    row_count = lax.axis_size("row")
    leading, width_a, width_b, trailing = block.shape
    factor = width_b // width_a
    stride = width_a // row_count
    sectioned = block.reshape(leading, width_a, factor, row_count, stride, trailing)
    sectioned = lax.all_to_all(sectioned, "row", split_axis=3, concat_axis=1, tiled=True)
    sectioned = sectioned.reshape(leading, width_a * row_count, factor * stride, trailing)
    sectioned = lax.all_to_all(sectioned, "col", split_axis=1, concat_axis=2, tiled=True)
    sectioned = sectioned.reshape(leading, width_b, row_count, stride, trailing)
    sectioned = lax.all_to_all(sectioned, "row", split_axis=2, concat_axis=2, tiled=True)
    return jnp.swapaxes(sectioned.reshape(leading, width_b, width_a, trailing), 1, 2)


def on_device(amplitudes, cycle_vertex, occupied_irrep, virtual_irrep):
    leading, width_a, width_b = amplitudes.shape
    irrep_a = lax.dynamic_slice_in_dim(virtual_irrep, lax.axis_index("row") * width_a, width_a)
    irrep_b = lax.dynamic_slice_in_dim(virtual_irrep, lax.axis_index("col") * width_b, width_b)
    product_irrep = jnp.bitwise_xor(
        occupied_irrep[:, None, None, None], occupied_irrep[None, None, None, :]
    )
    product_irrep = jnp.bitwise_xor(product_irrep, irrep_a[None, :, None, None])
    product_irrep = jnp.bitwise_xor(product_irrep, irrep_b[None, None, :, None])
    allowed = (product_irrep == 0).astype(jnp.float32)
    gathered = lax.all_gather(amplitudes, "col", axis=2, tiled=True)
    direct = jnp.einsum(
        "iac,jcb->iabj",
        gathered,
        lax.all_gather(cycle_vertex, "row", axis=1, tiled=True),
        preferred_element_type=jnp.float32,
    )
    paired = (direct - jnp.swapaxes(direct, 0, 3)).astype(jnp.bfloat16)
    mirrored = swap_residual(paired)
    result = allowed * (paired.astype(jnp.float32) - mirrored.astype(jnp.float32))
    return result.astype(jnp.bfloat16).reshape(leading, width_a, width_b * leading)


def solution(mesh):
    return jax.shard_map(
        on_device,
        mesh=mesh,
        in_specs=(P(None, "row", "col"), P(None, "row", "col"), P(), P()),
        out_specs=P(None, "row", "col"),
        check_vma=False,
    )
```

profile of v0, /device:TPU:8, one launch (start us, length us, event | category | flops | bytes accessed | tf_op | source)
XLA Modules:
  0.0 513.6 jit_solution(3895624791044629457)
XLA Ops:
  6.5 0.7 all-gather.2.cloned.1.call-update
  7.3 1.1 copy.33
  8.4 104.5 %all_gather.7 = bf16[12,32,1024]{1,0,2:T(8,128)(2,1)} all-gather(bf16[12,32,64]{1,0,2:T(8,128)(2,1)S(1)} %copy.33), channel_id=1, replica_groups=mesh['row'=32,'col'=16] {'col'}, dimensions={2}, use_global_device_ids=true | all-gather | bytes 835584 | tf_op jit(solution)/shard_map/all_gather | solution.py:31
  112.9 4.4 copy.34
  117.3 122.6 %all-gather.2.cloned.1.call-done = bf16[12,1024,64]{2,1,0:T(8,128)(2,1)} async-done(((bf16[12,32,64]{2,1,0:T(8,128)(2,1)}), bf16[12,1024,64]{2,1,0:T(8,128)(2,1)}) %all-gather.2.cloned.1.call-update) | async-done | bytes 1572880 | tf_op jit(solution)/shard_map/all_gather | solution.py:35
  239.9 3.3 fusion
  243.2 1.4 copy-done
  244.7 0.3 fusion.5
  245.0 1.1 reshape.53
  246.1 5.4 %copy.36 = bf16[12,32,2,32,1,12]{1,2,5,0,4,3:T(2,128)(2,1)} copy(bf16[12,32,2,32,1,12]{3,2,1,5,0,4:T(2,128)(2,1)S(1)} %reshape.53) | data formatting | bytes 1179648 | tf_op jit(solution)/shard_map/reshape | solution.py:12
  251.5 5.7 %reshape.60 = bf16[32,2,4608]{2,1,0:T(2,128)(2,1)S(1)} reshape(bf16[32,1,12,12,2,32]{5,4,3,2,1,0:T(2,128)(2,1)} %bitcast.54) | data formatting | bytes 1179648
  257.2 33.0 %all_to_all.35 = bf16[32,2,4608]{2,1,0:T(2,128)(2,1)S(1)} all-to-all(bf16[32,2,4608]{2,1,0:T(2,128)(2,1)S(1)} %reshape.60), channel_id=1, replica_groups=mesh['row'=32,'col'=16] {'row'}, dimensions={0} | all-to-all | bytes 1179648 | tf_op jit(solution)/shard_map/all_to_all | solution.py:13
  290.2 1.3 reshape.61
  291.5 3.1 bitcast_bitcast_fusion
  294.6 16.8 %copy.46 = bf16[12,32,32,2,1,1,12]{6,3,0,2,1,5,4:T(2,128)(2,1)} copy(bf16[12,32,32,2,1,1,12]{2,3,6,0,1,5,4:T(2,128)(2,1)} %bitcast_bitcast_fusion) | data formatting | bytes 1179648 | tf_op jit(solution)/shard_map/reshape | solution.py:14
  311.4 17.5 %reshape.62 = bf16[16,2,9216]{2,1,0:T(2,128)(2,1)S(1)} reshape(bf16[1024,12,2,12]{3,2,1,0:T(2,128)(2,1)} %bitcast.53) | data formatting | bytes 1179648
  328.9 77.4 %all_to_all.36 = bf16[16,2,9216]{2,1,0:T(2,128)(2,1)S(1)} all-to-all(bf16[16,2,9216]{2,1,0:T(2,128)(2,1)S(1)} %reshape.62), channel_id=1, replica_groups=mesh['row'=32,'col'=16] {'col'}, dimensions={0} | all-to-all | bytes 1179648 | tf_op jit(solution)/shard_map/all_to_all | solution.py:15
  406.4 15.6 %reshape.63 = bf16[1024,12,2,12]{3,2,1,0:T(2,128)(2,1)} reshape(bf16[16,2,9216]{2,1,0:T(2,128)(2,1)S(1)} %all_to_all.36) | data formatting | bytes 1179648
  422.0 14.9 %copy.47 = bf16[12,16,64,2,12]{2,1,3,4,0:T(8,128)(2,1)S(1)} copy(bf16[12,16,64,2,12]{4,3,0,2,1:T(2,128)(2,1)} %bitcast.52) | data formatting | bytes 1179648 | tf_op jit(solution)/shard_map/all_to_all | solution.py:15
  436.9 1.1 copy.40
  438.0 1.7 copy.54
  439.6 2.9 reshape.64
  442.6 17.0 %all-to-all-start.2 = ((bf16[32,2,4608]{2,1,0:T(2,128)(2,1)}), bf16[32,2,4608]{2,1,0:T(2,128)(2,1)S(1)}, u32[]{:S(2)}, u32[]{:S(2)}) async-start(bf16[32,2,4608]{2,1,0:T(2,128)(2,1)} %reshape.64), calls=%async_computation.2 | async-start | bytes 1179648 | tf_op jit(solution)/shard_map/all_to_all | solution.py:17
  459.6 0.8 dynamic_slice.7
  460.4 0.8 dynamic_slice.6
  461.2 0.1 broadcast_xor_fusion
  461.3 31.0 %all-to-all-done.2 = bf16[32,2,4608]{2,1,0:T(2,128)(2,1)S(1)} async-done(((bf16[32,2,4608]{2,1,0:T(2,128)(2,1)}), bf16[32,2,4608]{2,1,0:T(2,128)(2,1)S(1)}, u32[]{:S(2)}, u32[]{:S(2)}) %all-to-all-start.2) | async-done | bytes 589856 | tf_op jit(solution)/shard_map/all_to_all | solution.py:17
  492.3 1.8 reshape.65
  494.1 3.8 fusion.4
  498.0 3.6 copy.43
  501.6 2.5 reshape.56
  504.1 2.7 copy.44
  (7 shorter events, 0.1 us)
Async XLA Ops:
  6.5 233.4 %all-gather.2.cloned.1.call-start = ((), (), s32[]{:S(2)}) async-start(), calls=%async_computation.3 | async-start | bytes 3244032 | tf_op jit(solution)/shard_map/all_gather | solution.py:35
  243.2 1.5 copy-start
  439.6 21.5 %copy-start.2 = (s32[12]{0:T(128)S(1)}, s32[12]{0:T(128)}, u32[]{:S(2)}) copy-start(s32[12]{0:T(128)} %param.6) | copy-start | bytes 148
  439.6 54.5 %copy-start.1 = (f32[12,64,12,32]{1,3,2,0:T(8,128)S(1)}, f32[12,64,12,32]{1,3,2,0:T(8,128)}, u32[]{:S(2)}) copy-start(f32[12,64,12,32]{1,3,2,0:T(8,128)} %copy-done) | copy-start | bytes 3538948
  442.6 49.7 %all-to-all-start.2 = ((bf16[32,2,4608]{2,1,0:T(2,128)(2,1)}), bf16[32,2,4608]{2,1,0:T(2,128)(2,1)S(1)}, u32[]{:S(2)}, u32[]{:S(2)}) async-start(bf16[32,2,4608]{2,1,0:T(2,128)(2,1)} %reshape.64), calls=%async_computation.2 | async-start | bytes 1179648 | tf_op jit(solution)/shard_map/all_to_all | solution.py:17
Sparse Core Ops, SparseCore 0:
  9.4 230.4 all-gather.1
where the time goes:
time: 515 us; the launch traced here: 514 us
  blocking collectives  215 us (42%)
  waiting for transfers between devices  154 us (30%)
  local copies, waits for them, and re-layouts  106 us (21%)
  starting transfers between devices  17 us (3%)
  between operations  13.5 us (3%)
    all_gather x1, waiting for transfers between devices, on_device(): lax.all_gather(cycle_vertex, 'row', axis=1, tiled=True)  123 us
    all_gather x1, blocking collectives, on_device(): gathered = lax.all_gather(amplitudes, 'col', axis=2, tiled=True)  105 us
    all_to_all x1, blocking collectives, swap_residual(): lax.all_to_all(sectioned, 'col', split_axis=1, concat_axis=2, tiled=True)  77.4 us
    unnamed x13, local copies, waits for them, and re-layouts  47.5 us
    all_to_all x1, blocking collectives, swap_residual(): lax.all_to_all(sectioned, 'row', split_axis=3, concat_axis=1, tiled=True)  33 us
    all_to_all x1, waiting for transfers between devices, swap_residual(): lax.all_to_all(sectioned, 'row', split_axis=2, concat_axis=2, tiled=True)  31 us
    all_to_all x1, starting transfers between devices, swap_residual(): lax.all_to_all(sectioned, 'row', split_axis=2, concat_axis=2, tiled=True)  17 us
    reshape x1, local copies, waits for them, and re-layouts, swap_residual(): sectioned.reshape(leading, width_a * row_count, factor * stride, trailing)  16.8 us
  transfers between devices with their start and end apart: 2, of which 2 were waited for; matrix products, arithmetic and copies ran while one was open for 1% of the time, Pallas kernels for 0%

commit v1 on v0

v1 whole, which is shorter than its diff:
```python
import functools

import jax
import jax.numpy as jnp
from jax import lax
from jax.experimental import pallas as pl
from jax.experimental.pallas import tpu as pltpu
from jax.sharding import PartitionSpec as P

Z, X, H, YC = 8, 4, 2, 8
OCC, WA, WB = 12, 32, 64
HALF = 32
GROUPS = OCC // 4
SIDE = OCC * 32
TILES = 17
VMEM_LIMIT = 48 * 1024 * 1024


def z_groups():
    return [[z * X + x for z in range(Z)] for x in range(X)]


def x_groups():
    return [[z * X + x for x in range(X)] for z in range(Z)]


def yc_groups():
    return [[h * YC + k for k in range(YC)] for h in range(H)]


def h_swap():
    return [(h * YC + k, (1 - h) * YC + k) for h in range(H) for k in range(YC)]


def mirror_perm(step):
    rows, cols = Z * X, H * YC
    return [
        (r * cols + c, (2 * c + (step + r) % 2) * cols + r // 2)
        for r in range(rows)
        for c in range(cols)
    ]


def slot_of(shape):
    return lax.broadcasted_iota(jnp.int32, shape, 1) // HALF


def crossed(load, i, group):
    slot = slot_of((32, 128))
    out = None
    for s in range(4):
        piece = load(4 * group + s, i // 4)
        shift = (s - i % 4) % 4
        if shift:
            piece = pltpu.roll(piece, shift * HALF, 1)
        out = piece if out is None else jnp.where(slot == s, piece, out)
    return out


def full_tiles():
    return [(i, g) for i in range(OCC) for g in range(i // 4 + 1, GROUPS)]


def pack_kernel(a_ref, w_ref, a_out, w_out):
    for i in range(OCC // 2):
        a_out[32 * i : 32 * i + 32, :] = jnp.concatenate([a_ref[i], a_ref[i + 6]], axis=1)
    for g in range(GROUPS):
        block = [w_ref[4 * g + s].astype(jnp.float32) for s in range(4)]
        for half in range(2):
            cut = jnp.concatenate(
                [b[:, HALF * half : HALF * half + HALF] for b in block], axis=1
            ).astype(jnp.bfloat16)
            lane = half * SIDE + 128 * g
            for copy in range(Z):
                w_out[copy, :, lane : lane + 128] = cut


def pack(amplitudes, cycle_vertex):
    return pl.pallas_call(
        pack_kernel,
        out_shape=(
            jax.ShapeDtypeStruct((192, 128), jnp.bfloat16),
            jax.ShapeDtypeStruct((Z, 32, 2 * SIDE), jnp.bfloat16),
        ),
        compiler_params=pltpu.CompilerParams(vmem_limit_bytes=VMEM_LIMIT),
        name="pack",
    )(amplitudes, cycle_vertex)


def pair_kernel(row_ref, a_ref, w_ref, paired_ref, send0_ref, send1_ref, w_own, lhs, prod, turned, sem):
    copies = [pltpu.make_async_copy(w_ref.at[x], w_own.at[:, x], sem.at[x]) for x in range(X)]
    for copy in copies:
        copy.start()
    for z in range(Z):
        h, y = z // 4, z % 4
        first = a_ref[2 * y, h]
        second = a_ref[2 * y + 1, h]
        lhs[:192, 128 * z : 128 * z + 128] = jnp.concatenate([first[:, :64], second[:, :64]], axis=1)
        lhs[192:, 128 * z : 128 * z + 128] = jnp.concatenate([first[:, 64:], second[:, 64:]], axis=1)
    for copy in copies:
        copy.wait()
    prod[...] = jnp.dot(
        lhs[...], w_own[...].reshape(Z * X * 32, 2 * SIDE), preferred_element_type=jnp.float32
    )
    slot = slot_of((32, 128))
    flip = row_ref[0]
    for half in range(2):
        lane = half * SIDE

        def load(j, group):
            return prod[32 * j : 32 * j + 32, lane + 128 * group : lane + 128 * group + 128]

        for i in range(OCC):
            for g in range(GROUPS):
                paired_ref[half, 32 * i : 32 * i + 32, 128 * g : 128 * g + 128] = (
                    load(i, g) - crossed(load, i, g)
                ).astype(jnp.bfloat16)
        turned[...] = paired_ref[half].astype(jnp.float32).T

        def tile(i, group):
            return turned[32 * i : 32 * i + 32, 128 * group : 128 * group + 128]

        out = [tile(i, g) for i, g in full_tiles()]
        for q in range(GROUPS):
            out.append(jnp.where(slot == 0, pltpu.roll(tile(4 * q + 2, q), HALF, 1), tile(4 * q, q)))
        out.append(jnp.where(slot < 2, pltpu.roll(tile(5, 1), 2 * HALF, 1), tile(1, 0)))
        out.append(tile(9, 2))
        packed = jnp.concatenate(out, axis=0).astype(jnp.bfloat16)

        @pl.when(flip == half)
        def _():
            send0_ref[...] = packed

        @pl.when(flip != half)
        def _():
            send1_ref[...] = packed


def pair(row, a_all, w_all):
    vmem = pl.BlockSpec(memory_space=pltpu.VMEM)
    send = jax.ShapeDtypeStruct((TILES * 32, 128), jnp.bfloat16)
    return pl.pallas_call(
        pair_kernel,
        out_shape=(jax.ShapeDtypeStruct((2, SIDE, SIDE), jnp.bfloat16), send, send),
        in_specs=[pl.BlockSpec(memory_space=pltpu.SMEM), vmem, pl.BlockSpec(memory_space=pl.ANY)],
        out_specs=(vmem, vmem, vmem),
        scratch_shapes=[
            pltpu.VMEM((Z, X, 32, 2 * SIDE), jnp.bfloat16),
            pltpu.VMEM((SIDE, Z * 128), jnp.bfloat16),
            pltpu.VMEM((SIDE, 2 * SIDE), jnp.float32),
            pltpu.VMEM((SIDE, SIDE), jnp.float32),
            pltpu.SemaphoreType.DMA((X,)),
        ],
        compiler_params=pltpu.CompilerParams(vmem_limit_bytes=VMEM_LIMIT),
        name="pair",
    )(row, a_all, w_all)


def finish_kernel(row_ref, paired_ref, get0_ref, get1_ref, row_key, col_key, order, out_ref, upper, whole):
    slot = slot_of((32, 128))
    flip = row_ref[0]
    for half in range(2):
        def got(t):
            rows = slice(32 * t, 32 * t + 32)
            return jnp.where(flip == half, get0_ref[rows, :], get1_ref[rows, :]).astype(jnp.float32)

        def put(i, group, mirrored, floor):
            rows, lanes = slice(32 * i, 32 * i + 32), slice(128 * group, 128 * group + 128)
            diff = paired_ref[half, rows, lanes].astype(jnp.float32) + mirrored
            if floor >= 0:
                diff = jnp.where(slot > floor, diff, 0.0)
            upper[rows, lanes] = diff

        for t, (i, g) in enumerate(full_tiles()):
            put(i, g, got(t), -1)
        last = [got(15), got(16)]
        for q in range(GROUPS):
            piece = got(12 + q)
            put(4 * q, q, piece, 0)
            put(4 * q + 2, q, pltpu.roll(piece, 3 * HALF, 1), 2)
            put(4 * q + 1, q, (last[0], pltpu.roll(last[0], 2 * HALF, 1), last[1])[q], 1)
            upper[32 * (4 * q + 3) : 32 * (4 * q + 4), 128 * q : 128 * q + 128] = jnp.zeros((32, 128), jnp.float32)

        def load(j, group):
            return upper[32 * j : 32 * j + 32, 128 * group : 128 * group + 128]

        for i in range(OCC):
            rows = slice(32 * i, 32 * i + 32)
            for g in range(GROUPS):
                lanes = slice(128 * g, 128 * g + 128)
                if g > i // 4:
                    value = load(i, g)
                elif g < i // 4:
                    value = -crossed(load, i, g)
                else:
                    value = load(i, g) - crossed(load, i, g)
                allowed = row_key[rows, :] == col_key[half : half + 1, lanes]
                whole[rows, lanes] = jnp.where(allowed, value, 0.0).astype(jnp.bfloat16)
        out_ref[:, SIDE * half : SIDE * half + SIDE] = jnp.dot(
            whole[...], order[...], preferred_element_type=jnp.float32
        ).astype(jnp.bfloat16)


def finish(row, paired, get0, get1, row_key, col_key, order):
    vmem = pl.BlockSpec(memory_space=pltpu.VMEM)
    return pl.pallas_call(
        finish_kernel,
        out_shape=jax.ShapeDtypeStruct((SIDE, 2 * SIDE), jnp.bfloat16),
        in_specs=[pl.BlockSpec(memory_space=pltpu.SMEM)] + [vmem] * 6,
        out_specs=vmem,
        scratch_shapes=[
            pltpu.VMEM((SIDE, SIDE), jnp.float32),
            pltpu.VMEM((SIDE, SIDE), jnp.bfloat16),
        ],
        compiler_params=pltpu.CompilerParams(vmem_limit_bytes=VMEM_LIMIT),
        name="finish",
    )(row, paired, get0, get1, row_key, col_key, order)


def on_device(amplitudes, cycle_vertex, occupied_irrep, virtual_irrep):
    r, c = lax.axis_index("row"), lax.axis_index("col")
    flip = (r % 2).astype(jnp.int32).reshape(1)
    a_own, w_own = pack(amplitudes, cycle_vertex)
    w_z = lax.all_to_all(w_own, "row", 0, 0, tiled=True, axis_index_groups=z_groups())
    w_all = lax.all_to_all(
        jnp.broadcast_to(w_z[None], (X, Z, 32, 2 * SIDE)),
        "row", 0, 0, tiled=True, axis_index_groups=x_groups(),
    )
    a_far = lax.ppermute(a_own, "col", h_swap())
    low = c < YC
    a_two = jnp.stack([jnp.where(low, a_own, a_far), jnp.where(low, a_far, a_own)])
    a_all = lax.all_to_all(
        jnp.broadcast_to(a_two[None], (YC, H, 192, 128)),
        "col", 0, 0, tiled=True, axis_index_groups=yc_groups(),
    )
    paired, send0, send1 = pair(flip, a_all, w_all)
    get0 = lax.ppermute(send0, ("row", "col"), mirror_perm(0))
    get1 = lax.ppermute(send1, ("row", "col"), mirror_perm(1))
    irrep_a = lax.dynamic_slice_in_dim(virtual_irrep, r * WA, WA)
    irrep_b = lax.dynamic_slice_in_dim(virtual_irrep, c * WB, WB)
    row_key = (occupied_irrep[:, None] ^ irrep_a[None, :]).reshape(SIDE, 1)
    row_key = jnp.broadcast_to(row_key, (SIDE, 128))
    col_key = (occupied_irrep[None, :, None] ^ irrep_b.reshape(2, 1, HALF)).reshape(2, SIDE)
    source = jnp.arange(SIDE)
    order = ((source % HALF) * OCC + source // HALF)[:, None] == jnp.arange(SIDE)[None, :]
    result = finish(flip, paired, get0, get1, row_key, col_key, order.astype(jnp.bfloat16))
    return result.reshape(OCC, WA, WB * OCC)


def solution(mesh):
    return jax.shard_map(
        on_device,
        mesh=mesh,
        in_specs=(P(None, "row", "col"), P(None, "row", "col"), P(), P()),
        out_specs=P(None, "row", "col"),
        check_vma=False,
    )
```

time: 515 us -> 126 us (0.24)
  the two profiles are of different devices: /device:TPU:8 before, /device:TPU:128 now
where the time goes in v1:
time: 126 us
  waiting for transfers between devices  46.2 us (37%)
  blocking collectives  44.7 us (35%)
  starting transfers between devices  25.1 us (20%)
  local copies, waits for them, and re-layouts  5.3 us (4%)
  Pallas kernels  4.43 us (4%)
    all_to_all x1, blocking collectives, on_device(): lax.all_to_all(w_own, 'row', 0, 0, tiled=True, axis_index_groups=z_groups())  26.7 us
    ppermute x1, waiting for transfers between devices, on_device(): get0 = lax.ppermute(send0, ('row', 'col'), mirror_perm(0))  20.5 us
    all_to_all x1, blocking collectives, on_device(): lax.all_to_all(jnp.broadcast_to(a_two[None], (YC, H, 192, 128)), 'col', 0...  18.1 us
    all_to_all x1, waiting for transfers between devices, on_device(): lax.all_to_all(jnp.broadcast_to(w_z[None], (X, Z, 32, 2 * SIDE)), 'row',...  18 us
    ppermute x1, starting transfers between devices, on_device(): a_far = lax.ppermute(a_own, 'col', h_swap())  10.9 us
    ppermute x1, starting transfers between devices, on_device(): get0 = lax.ppermute(send0, ('row', 'col'), mirror_perm(0))  5.12 us
    ppermute x1, waiting for transfers between devices, on_device(): a_far = lax.ppermute(a_own, 'col', h_swap())  5.05 us
    ppermute x1, starting transfers between devices, on_device(): get1 = lax.ppermute(send1, ('row', 'col'), mirror_perm(1))  4.63 us
  transfers between devices with their start and end apart: 4, of which 4 were waited for; matrix products, arithmetic and copies ran while one was open for 2% of the time, Pallas kernels for 0%

profile of v1, /device:TPU:128, one launch (start us, length us, event | category | flops | bytes accessed | tf_op | source)
XLA Modules:
  0.0 126.1 jit_solution(5209280188713478511)
XLA Ops:
  0.0 0.0 copy-start
  0.0 0.9 copy-done
  0.9 0.0 copy-start.1
  0.9 0.9 copy-done.1
  1.8 0.1 pack.1
  1.9 10.9 %collective-permute-start = (bf16[192,128]{1,0:T(8,128)(2,1)S(1)}, bf16[192,128]{1,0:T(8,128)(2,1)S(1)}, u32[]{:S(2)}, u32[]{:S(2)}) collective-permute-start(bf16[192,128]{1,0:T(8,128)(2,1)S(1)} %get-tuple-element.10), channel_id=1, source_target_pairs={{0,8},{1,9},{2,10},{3,11},{4,12},{5,13},{6,14},{7,15},{8,0},{9,1},... | collective-permute-start | bytes 147464 | tf_op jit(solution)/shard_map/ppermute | solution.py:229
  12.9 5.0 %collective-permute-done = bf16[192,128]{1,0:T(8,128)(2,1)S(1)} collective-permute-done((bf16[192,128]{1,0:T(8,128)(2,1)S(1)}, bf16[192,128]{1,0:T(8,128)(2,1)S(1)}, u32[]{:S(2)}, u32[]{:S(2)}) %collective-permute-start) | collective-permute-done | bytes 49184 | tf_op jit(solution)/shard_map/ppermute | solution.py:229
  17.9 0.1 broadcast_in_dim.6
  18.1 18.1 %all_to_all.15.a_ref = bf16[8,2,192,128]{3,2,1,0:T(8,128)(2,1)S(1)} all-to-all(bf16[8,2,192,128]{3,2,1,0:T(8,128)(2,1)S(1)} %broadcast_in_dim.6), channel_id=1, replica_groups={{0,1,2,3,4,5,6,7},{8,9,10,11,12,13,14,15},{16,17,18,19,20,21,22,23},{24..., dimensions={0} | all-to-all | bytes 1572864 | tf_op jit(solution)/shard_map/all_to_all | solution.py:232
  36.2 26.7 %all_to_all.16 = bf16[8,32,768]{2,1,0:T(8,128)(2,1)S(1)} all-to-all(bf16[8,32,768]{2,1,0:T(8,128)(2,1)S(1)} %get-tuple-element.11), channel_id=1, replica_groups={{0,64,128,192,256,320,384,448},{16,80,144,208,272,336,400,464},{32,96,1..., dimensions={0} | all-to-all | bytes 786432 | tf_op jit(solution)/shard_map/all_to_all | solution.py:224
  62.8 1.3 %broadcast_in_dim.7 = bf16[4,8,32,768]{3,2,1,0:T(8,128)(2,1)} broadcast(bf16[8,32,768]{2,1,0:T(8,128)(2,1)S(1)} %all_to_all.16), dimensions={1,2,3} | broadcast | bytes 1966080 | tf_op jit(solution)/shard_map/broadcast_in_dim | solution.py:226
  64.2 0.0 copy-start.2
  64.2 4.4 %all-to-all-start.2 = ((bf16[4,8,32,768]{3,2,1,0:T(8,128)(2,1)}), bf16[4,8,32,768]{3,2,1,0:T(8,128)(2,1)S(1)}, u32[]{:S(2)}, u32[]{:S(2)}) async-start(bf16[4,8,32,768]{3,2,1,0:T(8,128)(2,1)} %broadcast_in_dim.7), calls=%async_computation.2 | async-start | bytes 3145728 | tf_op jit(solution)/shard_map/all_to_all | solution.py:225
  68.6 0.8 dynamic_slice.6
  69.4 0.1 xor.42
  69.4 0.0 copy-done.2
  69.4 0.1 xor.39
  69.5 0.1 xor.40
  69.6 0.8 dynamic_slice.7
  70.4 0.1 xor.45
  70.5 0.1 xor.47
  70.5 0.1 fusion.order
  70.7 18.0 %all-to-all-done.2.w_ref = bf16[4,8,32,768]{3,2,1,0:T(8,128)(2,1)S(1)} async-done(((bf16[4,8,32,768]{3,2,1,0:T(8,128)(2,1)}), bf16[4,8,32,768]{3,2,1,0:T(8,128)(2,1)S(1)}, u32[]{:S(2)}, u32[]{:S(2)}) %all-to-all-start.2) | async-done | bytes 1572896 | tf_op jit(solution)/shard_map/all_to_all | solution.py:225
  88.7 2.4 %pair.1 = (bf16[2,384,384]{2,1,0:T(8,128)(2,1)S(1)}, bf16[544,128]{1,0:T(8,128)(2,1)S(1)}, bf16[544,128]{1,0:T(8,128)(2,1)S(1)}) custom-call(s32[1]{0:T(128)} %bitcast.row_ref, bf16[8,2,192,128]{3,2,1,0:T(8,128)(2,1)S(1)} %all_to_all.15.a_ref, bf16[4,8,32,768]{3,2,1,0:T(8,128)(2,1)S(1)} %all-to-all-done.2.w_ref), custom_call_target="tpu_custom_call" | custom-call | tf_op jit(solution)/shard_map/pair/pallas_call | solution.py:142
  91.1 5.1 %collective-permute-start.1 = (bf16[544,128]{1,0:T(8,128)(2,1)S(1)}, bf16[544,128]{1,0:T(8,128)(2,1)S(1)}, u32[]{:S(2)}, u32[]{:S(2)}) collective-permute-start(bf16[544,128]{1,0:T(8,128)(2,1)S(1)} %get-tuple-element.13), channel_id=1, source_target_pairs={{0,0},{1,32},{2,64},{3,96},{4,128},{5,160},{6,192},{7,224},{8,256}... | collective-permute-start | bytes 417800 | tf_op jit(solution)/shard_map/ppermute | solution.py:237
  96.2 4.6 %collective-permute-start.2 = (bf16[544,128]{1,0:T(8,128)(2,1)S(1)}, bf16[544,128]{1,0:T(8,128)(2,1)S(1)}, u32[]{:S(2)}, u32[]{:S(2)}) collective-permute-start(bf16[544,128]{1,0:T(8,128)(2,1)S(1)} %get-tuple-element.14), channel_id=1, source_target_pairs={{0,16},{1,48},{2,80},{3,112},{4,144},{5,176},{6,208},{7,240},{8,27... | collective-permute-start | bytes 417800 | tf_op jit(solution)/shard_map/ppermute | solution.py:238
  100.9 20.5 %collective-permute-done.1.get0_ref = bf16[544,128]{1,0:T(8,128)(2,1)S(1)} collective-permute-done((bf16[544,128]{1,0:T(8,128)(2,1)S(1)}, bf16[544,128]{1,0:T(8,128)(2,1)S(1)}, u32[]{:S(2)}, u32[]{:S(2)}) %collective-permute-start.1) | collective-permute-done | bytes 139296 | tf_op jit(solution)/shard_map/ppermute | solution.py:237
  121.3 2.7 %collective-permute-done.2.get1_ref = bf16[544,128]{1,0:T(8,128)(2,1)S(1)} collective-permute-done((bf16[544,128]{1,0:T(8,128)(2,1)S(1)}, bf16[544,128]{1,0:T(8,128)(2,1)S(1)}, u32[]{:S(2)}, u32[]{:S(2)}) %collective-permute-start.2) | collective-permute-done | bytes 139296 | tf_op jit(solution)/shard_map/ppermute | solution.py:238
  124.0 0.1 broadcast_in_dim.8.row_key
  124.1 1.9 %finish.1 = bf16[384,768]{1,0:T(8,128)(2,1)} custom-call(s32[1]{0:T(128)} %bitcast.row_ref, bf16[2,384,384]{2,1,0:T(8,128)(2,1)S(1)} %get-tuple-element.12.paired_ref, bf16[544,128]{1,0:T(8,128)(2,1)S(1)} %collective-permute-done.1.get0_ref, bf16[544,128]{1,0:T(8,128)(2,1)S(1)} %collective-permute-done.2.get1_ref, s32[384,128]{1,0:T(8,128)S(1)} %broadcast_in_dim.8.row_key, ...), custom_call_target="tpu_custom_call" | custom-call | tf_op jit(solution)/shard_map/finish/pallas_call | solution.py:206
  (7 shorter events, 0.0 us)
Async XLA Ops:
  0.0 0.9 copy-start
  0.9 0.9 copy-start.1
  1.9 16.0 %collective-permute-start = (bf16[192,128]{1,0:T(8,128)(2,1)S(1)}, bf16[192,128]{1,0:T(8,128)(2,1)S(1)}, u32[]{:S(2)}, u32[]{:S(2)}) collective-permute-start(bf16[192,128]{1,0:T(8,128)(2,1)S(1)} %get-tuple-element.10), channel_id=1, source_target_pairs={{0,8},{1,9},{2,10},{3,11},{4,12},{5,13},{6,14},{7,15},{8,0},{9,1},... | collective-permute-start | bytes 147464 | tf_op jit(solution)/shard_map/ppermute | solution.py:229
  64.2 5.3 %copy-start.2 = (s32[12]{0:T(128)S(1)}, s32[12]{0:T(128)}, u32[]{:S(2)}) copy-start(s32[12]{0:T(128)} %param.6) | copy-start | bytes 148
  64.2 24.5 %all-to-all-start.2 = ((bf16[4,8,32,768]{3,2,1,0:T(8,128)(2,1)}), bf16[4,8,32,768]{3,2,1,0:T(8,128)(2,1)S(1)}, u32[]{:S(2)}, u32[]{:S(2)}) async-start(bf16[4,8,32,768]{3,2,1,0:T(8,128)(2,1)} %broadcast_in_dim.7), calls=%async_computation.2 | async-start | bytes 3145728 | tf_op jit(solution)/shard_map/all_to_all | solution.py:225
  91.1 30.2 %collective-permute-start.1 = (bf16[544,128]{1,0:T(8,128)(2,1)S(1)}, bf16[544,128]{1,0:T(8,128)(2,1)S(1)}, u32[]{:S(2)}, u32[]{:S(2)}) collective-permute-start(bf16[544,128]{1,0:T(8,128)(2,1)S(1)} %get-tuple-element.13), channel_id=1, source_target_pairs={{0,0},{1,32},{2,64},{3,96},{4,128},{5,160},{6,192},{7,224},{8,256}... | collective-permute-start | bytes 417800 | tf_op jit(solution)/shard_map/ppermute | solution.py:237
  96.2 27.8 %collective-permute-start.2 = (bf16[544,128]{1,0:T(8,128)(2,1)S(1)}, bf16[544,128]{1,0:T(8,128)(2,1)S(1)}, u32[]{:S(2)}, u32[]{:S(2)}) collective-permute-start(bf16[544,128]{1,0:T(8,128)(2,1)S(1)} %get-tuple-element.14), channel_id=1, source_target_pairs={{0,16},{1,48},{2,80},{3,112},{4,144},{5,176},{6,208},{7,240},{8,27... | collective-permute-start | bytes 417800 | tf_op jit(solution)/shard_map/ppermute | solution.py:238

commit v2 on v1

--- a/solution.py
+++ b/solution.py
@@ -30,6 +30,17 @@
 
 def h_swap():
     return [(h * YC + k, (1 - h) * YC + k) for h in range(H) for k in range(YC)]
+
+
+def y_shift(step):
+    return [
+        (h * YC + y * 2 + k, h * YC + (y + step) % 4 * 2 + k)
+        for h in range(H) for y in range(4) for k in range(2)
+    ]
+
+
+def core_swap():
+    return [(c, c ^ 1) for c in range(H * YC)]
 
 
 def mirror_perm(step):
@@ -87,20 +98,23 @@
     )(amplitudes, cycle_vertex)
 
 
-def pair_kernel(row_ref, a_ref, w_ref, paired_ref, send0_ref, send1_ref, w_own, lhs, prod, turned, sem):
+def pair_kernel(row_ref, own_ref, far_ref, w_ref, paired_ref, send0_ref, send1_ref, w_own, lhs, prod, turned, sem):
     copies = [pltpu.make_async_copy(w_ref.at[x], w_own.at[:, x], sem.at[x]) for x in range(X)]
     for copy in copies:
         copy.start()
-    for z in range(Z):
-        h, y = z // 4, z % 4
-        first = a_ref[2 * y, h]
-        second = a_ref[2 * y + 1, h]
-        lhs[:192, 128 * z : 128 * z + 128] = jnp.concatenate([first[:, :64], second[:, :64]], axis=1)
-        lhs[192:, 128 * z : 128 * z + 128] = jnp.concatenate([first[:, 64:], second[:, 64:]], axis=1)
+    core, y = row_ref[1], row_ref[2]
+    for step in range(4):
+        for h in range(H):
+            mine, other = own_ref[step, h], far_ref[step, h]
+            first = jnp.where(core == 0, mine, other)
+            second = jnp.where(core == 0, other, mine)
+            z = h * 4 + lax.rem(y + 4 - step, 4)
+            lhs[z, :192] = jnp.concatenate([first[:, :64], second[:, :64]], axis=1)
+            lhs[z, 192:] = jnp.concatenate([first[:, 64:], second[:, 64:]], axis=1)
     for copy in copies:
         copy.wait()
     prod[...] = jnp.dot(
-        lhs[...], w_own[...].reshape(Z * X * 32, 2 * SIDE), preferred_element_type=jnp.float32
+        jnp.concatenate([lhs[z] for z in range(Z)], axis=1), w_own[...].reshape(Z * X * 32, 2 * SIDE), preferred_element_type=jnp.float32
     )
     slot = slot_of((32, 128))
     flip = row_ref[0]
@@ -136,24 +150,24 @@
             send1_ref[...] = packed
 
 
-def pair(row, a_all, w_all):
+def pair(row, a_mine, a_other, w_all):
     vmem = pl.BlockSpec(memory_space=pltpu.VMEM)
     send = jax.ShapeDtypeStruct((TILES * 32, 128), jnp.bfloat16)
     return pl.pallas_call(
         pair_kernel,
         out_shape=(jax.ShapeDtypeStruct((2, SIDE, SIDE), jnp.bfloat16), send, send),
-        in_specs=[pl.BlockSpec(memory_space=pltpu.SMEM), vmem, pl.BlockSpec(memory_space=pl.ANY)],
+        in_specs=[pl.BlockSpec(memory_space=pltpu.SMEM), vmem, vmem, pl.BlockSpec(memory_space=pl.ANY)],
         out_specs=(vmem, vmem, vmem),
         scratch_shapes=[
             pltpu.VMEM((Z, X, 32, 2 * SIDE), jnp.bfloat16),
-            pltpu.VMEM((SIDE, Z * 128), jnp.bfloat16),
+            pltpu.VMEM((Z, SIDE, 128), jnp.bfloat16),
             pltpu.VMEM((SIDE, 2 * SIDE), jnp.float32),
             pltpu.VMEM((SIDE, SIDE), jnp.float32),
             pltpu.SemaphoreType.DMA((X,)),
         ],
         compiler_params=pltpu.CompilerParams(vmem_limit_bytes=VMEM_LIMIT),
         name="pair",
-    )(row, a_all, w_all)
+    )(row, a_mine, a_other, w_all)
 
 
 def finish_kernel(row_ref, paired_ref, get0_ref, get1_ref, row_key, col_key, order, out_ref, upper, whole):
@@ -219,21 +233,20 @@
 
 def on_device(amplitudes, cycle_vertex, occupied_irrep, virtual_irrep):
     r, c = lax.axis_index("row"), lax.axis_index("col")
-    flip = (r % 2).astype(jnp.int32).reshape(1)
+    place = jnp.stack([r % 2, c % 2, c // 2 % 4]).astype(jnp.int32)
     a_own, w_own = pack(amplitudes, cycle_vertex)
     w_z = lax.all_to_all(w_own, "row", 0, 0, tiled=True, axis_index_groups=z_groups())
+    a_far = lax.ppermute(a_own, "col", h_swap())
+    low = c < YC
+    a_two = jnp.stack([jnp.where(low, a_own, a_far), jnp.where(low, a_far, a_own)])
+    w_z, a_two = lax.optimization_barrier((w_z, a_two))
     w_all = lax.all_to_all(
         jnp.broadcast_to(w_z[None], (X, Z, 32, 2 * SIDE)),
         "row", 0, 0, tiled=True, axis_index_groups=x_groups(),
     )
-    a_far = lax.ppermute(a_own, "col", h_swap())
-    low = c < YC
-    a_two = jnp.stack([jnp.where(low, a_own, a_far), jnp.where(low, a_far, a_own)])
-    a_all = lax.all_to_all(
-        jnp.broadcast_to(a_two[None], (YC, H, 192, 128)),
-        "col", 0, 0, tiled=True, axis_index_groups=yc_groups(),
-    )
-    paired, send0, send1 = pair(flip, a_all, w_all)
+    a_mine = jnp.stack([a_two] + [lax.ppermute(a_two, "col", y_shift(s)) for s in (1, 2, 3)])
+    a_other = lax.ppermute(a_mine, "col", core_swap())
+    paired, send0, send1 = pair(place, a_mine, a_other, w_all)
     get0 = lax.ppermute(send0, ("row", "col"), mirror_perm(0))
     get1 = lax.ppermute(send1, ("row", "col"), mirror_perm(1))
     irrep_a = lax.dynamic_slice_in_dim(virtual_irrep, r * WA, WA)
@@ -243,7 +256,7 @@
     col_key = (occupied_irrep[None, :, None] ^ irrep_b.reshape(2, 1, HALF)).reshape(2, SIDE)
     source = jnp.arange(SIDE)
     order = ((source % HALF) * OCC + source // HALF)[:, None] == jnp.arange(SIDE)[None, :]
-    result = finish(flip, paired, get0, get1, row_key, col_key, order.astype(jnp.bfloat16))
+    result = finish(place, paired, get0, get1, row_key, col_key, order.astype(jnp.bfloat16))
     return result.reshape(OCC, WA, WB * OCC)
 
 

time: 126 us -> 106 us (0.84)
  the two profiles are of different devices: /device:TPU:128 before, /device:TPU:161 now
where the time goes in v2:
time: 106 us; the launch traced here: 105 us
  starting transfers between devices  51.6 us (49%)
  waiting for transfers between devices  41.5 us (39%)
  Pallas kernels  6.25 us (6%)
  local copies, waits for them, and re-layouts  5.18 us (5%)
    ppermute x1, waiting for transfers between devices, on_device(): get0 = lax.ppermute(send0, ('row', 'col'), mirror_perm(0))  18.1 us
    ppermute x1, waiting for transfers between devices, on_device(): a_far = lax.ppermute(a_own, 'col', h_swap())  17.8 us
    ppermute x3, starting transfers between devices, on_device(): lax.ppermute(a_two, 'col', y_shift(s))  10.7 us
    all_to_all x1, starting transfers between devices, on_device(): lax.all_to_all(w_own, 'row', 0, 0, tiled=True, axis_index_groups=z_groups())  10.3 us
    ppermute x1, starting transfers between devices, on_device(): get1 = lax.ppermute(send1, ('row', 'col'), mirror_perm(1))  8.85 us
    ppermute x1, starting transfers between devices, on_device(): a_far = lax.ppermute(a_own, 'col', h_swap())  7.93 us
    ppermute x1, starting transfers between devices, on_device(): a_other = lax.ppermute(a_mine, 'col', core_swap())  5.58 us
    ppermute x1, starting transfers between devices, on_device(): get0 = lax.ppermute(send0, ('row', 'col'), mirror_perm(0))  4.19 us
  transfers between devices with their start and end apart: 9, of which 4 were waited for; matrix products, arithmetic and copies ran while one was open for 2% of the time, Pallas kernels for 0%

profile of v2, /device:TPU:161, one launch (start us, length us, event | category | flops | bytes accessed | tf_op | source)
XLA Modules:
  0.0 105.1 jit_solution(2105093232122823727)
XLA Ops:
  0.0 0.9 copy-done
  0.9 0.9 copy-done.1
  1.8 0.9 pack.1
  2.7 10.3 %all-to-all-start = ((bf16[8,32,768]{2,1,0:T(8,128)(2,1)}), bf16[8,32,768]{2,1,0:T(8,128)(2,1)S(1)}, u32[]{:S(2)}, u32[]{:S(2)}) async-start(bf16[8,32,768]{2,1,0:T(8,128)(2,1)} %get-tuple-element.12), calls=%async_computation | async-start | bytes 786432 | tf_op jit(solution)/shard_map/all_to_all | solution.py:238
  12.9 7.9 %collective-permute-start = (bf16[192,128]{1,0:T(8,128)(2,1)S(1)}, bf16[192,128]{1,0:T(8,128)(2,1)S(1)}, u32[]{:S(2)}, u32[]{:S(2)}) collective-permute-start(bf16[192,128]{1,0:T(8,128)(2,1)S(1)} %get-tuple-element.13), channel_id=1, source_target_pairs={{0,8},{1,9},{2,10},{3,11},{4,12},{5,13},{6,14},{7,15},{8,0},{9,1},... | collective-permute-start | bytes 147464 | tf_op jit(solution)/shard_map/ppermute | solution.py:239
  20.9 17.8 %collective-permute-done = bf16[192,128]{1,0:T(8,128)(2,1)S(1)} collective-permute-done((bf16[192,128]{1,0:T(8,128)(2,1)S(1)}, bf16[192,128]{1,0:T(8,128)(2,1)S(1)}, u32[]{:S(2)}, u32[]{:S(2)}) %collective-permute-start) | collective-permute-done | bytes 49184 | tf_op jit(solution)/shard_map/ppermute | solution.py:239
  38.7 0.0 all-to-all-done
  38.7 1.4 %broadcast_in_dim.4 = bf16[4,8,32,768]{3,2,1,0:T(8,128)(2,1)} broadcast(bf16[8,32,768]{2,1,0:T(8,128)(2,1)S(1)} %all-to-all-done), dimensions={1,2,3} | broadcast | bytes 1966080 | tf_op jit(solution)/shard_map/broadcast_in_dim | solution.py:244
  40.1 4.1 %all-to-all-start.1 = ((bf16[4,8,32,768]{3,2,1,0:T(8,128)(2,1)}), bf16[4,8,32,768]{3,2,1,0:T(8,128)(2,1)S(1)}, u32[]{:S(2)}, u32[]{:S(2)}) async-start(bf16[4,8,32,768]{3,2,1,0:T(8,128)(2,1)} %broadcast_in_dim.4), calls=%async_computation.1 | async-start | bytes 3145728 | tf_op jit(solution)/shard_map/all_to_all | solution.py:243
  44.2 3.2 %collective-permute-start.1 = (bf16[2,192,128]{2,1,0:T(8,128)(2,1)S(1)}, bf16[2,192,128]{2,1,0:T(8,128)(2,1)S(1)}, u32[]{:S(2)}, u32[]{:S(2)}) collective-permute-start(bf16[2,192,128]{2,1,0:T(8,128)(2,1)S(1)} %pad_maximum_fusion.1), channel_id=1, source_target_pairs={{0,2},{1,3},{2,4},{3,5},{4,6},{5,7},{6,0},{7,1},{8,10},{9,11},{10,... | collective-permute-start | bytes 294920 | tf_op jit(solution)/shard_map/ppermute | solution.py:247
  47.4 4.5 %collective-permute-start.2 = (bf16[2,192,128]{2,1,0:T(8,128)(2,1)S(1)}, bf16[2,192,128]{2,1,0:T(8,128)(2,1)S(1)}, u32[]{:S(2)}, u32[]{:S(2)}) collective-permute-start(bf16[2,192,128]{2,1,0:T(8,128)(2,1)S(1)} %pad_maximum_fusion.1), channel_id=1, source_target_pairs={{0,4},{1,5},{2,6},{3,7},{4,0},{5,1},{6,2},{7,3},{8,12},{9,13},{10,... | collective-permute-start | bytes 294920 | tf_op jit(solution)/shard_map/ppermute | solution.py:247
  52.0 3.0 %collective-permute-start.3 = (bf16[2,192,128]{2,1,0:T(8,128)(2,1)S(1)}, bf16[2,192,128]{2,1,0:T(8,128)(2,1)S(1)}, u32[]{:S(2)}, u32[]{:S(2)}) collective-permute-start(bf16[2,192,128]{2,1,0:T(8,128)(2,1)S(1)} %pad_maximum_fusion.1), channel_id=1, source_target_pairs={{0,6},{1,7},{2,0},{3,1},{4,2},{5,3},{6,4},{7,5},{8,14},{9,15},{10,... | collective-permute-start | bytes 294920 | tf_op jit(solution)/shard_map/ppermute | solution.py:247
  55.0 0.0 collective-permute-done.1
  55.0 2.8 %collective-permute-done.3 = bf16[2,192,128]{2,1,0:T(8,128)(2,1)S(1)} collective-permute-done((bf16[2,192,128]{2,1,0:T(8,128)(2,1)S(1)}, bf16[2,192,128]{2,1,0:T(8,128)(2,1)S(1)}, u32[]{:S(2)}, u32[]{:S(2)}) %collective-permute-start.3) | collective-permute-done | bytes 98336 | tf_op jit(solution)/shard_map/ppermute | solution.py:247
  57.8 0.1 pad_maximum_fusion.own_ref
  57.9 5.6 %collective-permute-start.4 = (bf16[4,2,192,128]{3,2,1,0:T(8,128)(2,1)S(1)}, bf16[4,2,192,128]{3,2,1,0:T(8,128)(2,1)S(1)}, u32[]{:S(2)}, u32[]{:S(2)}) collective-permute-start(bf16[4,2,192,128]{3,2,1,0:T(8,128)(2,1)S(1)} %pad_maximum_fusion.own_ref), channel_id=1, source_target_pairs={{0,1},{1,0},{2,3},{3,2},{4,5},{5,4},{6,7},{7,6},{8,9},{9,8},{10,11... | collective-permute-start | bytes 1179656 | tf_op jit(solution)/shard_map/ppermute | solution.py:248
  63.5 0.1 pad_add_fusion.row_ref
  63.5 0.8 dynamic_slice.7
  64.3 0.1 xor.45
  64.4 0.1 xor.47
  64.5 0.1 xor.39
  64.5 0.1 xor.40
  64.6 0.8 dynamic_slice.6
  65.4 0.1 xor.42
  65.5 0.1 fusion.order
  65.6 2.9 %pair.1 = (bf16[2,384,384]{2,1,0:T(8,128)(2,1)S(1)}, bf16[544,128]{1,0:T(8,128)(2,1)S(1)}, bf16[544,128]{1,0:T(8,128)(2,1)S(1)}) custom-call(s32[3]{0:T(128)S(1)} %pad_add_fusion.row_ref, bf16[4,2,192,128]{3,2,1,0:T(8,128)(2,1)S(1)} %pad_maximum_fusion.own_ref, bf16[4,2,192,128]{3,2,1,0:T(8,128)(2,1)S(1)} %collective-permute-done.4.far_ref, ...), custom_call_target="tpu_custom_call" | custom-call | tf_op jit(solution)/shard_map/pair/pallas_call | solution.py:156
  68.6 4.2 %collective-permute-start.5 = (bf16[544,128]{1,0:T(8,128)(2,1)S(1)}, bf16[544,128]{1,0:T(8,128)(2,1)S(1)}, u32[]{:S(2)}, u32[]{:S(2)}) collective-permute-start(bf16[544,128]{1,0:T(8,128)(2,1)S(1)} %get-tuple-element.17), channel_id=1, source_target_pairs={{0,0},{1,32},{2,64},{3,96},{4,128},{5,160},{6,192},{7,224},{8,256}... | collective-permute-start | bytes 417800 | tf_op jit(solution)/shard_map/ppermute | solution.py:250
  72.8 8.9 %collective-permute-start.6 = (bf16[544,128]{1,0:T(8,128)(2,1)S(1)}, bf16[544,128]{1,0:T(8,128)(2,1)S(1)}, u32[]{:S(2)}, u32[]{:S(2)}) collective-permute-start(bf16[544,128]{1,0:T(8,128)(2,1)S(1)} %get-tuple-element.18), channel_id=1, source_target_pairs={{0,16},{1,48},{2,80},{3,112},{4,144},{5,176},{6,208},{7,240},{8,27... | collective-permute-start | bytes 417800 | tf_op jit(solution)/shard_map/ppermute | solution.py:251
  81.6 18.1 %collective-permute-done.5.get0_ref = bf16[544,128]{1,0:T(8,128)(2,1)S(1)} collective-permute-done((bf16[544,128]{1,0:T(8,128)(2,1)S(1)}, bf16[544,128]{1,0:T(8,128)(2,1)S(1)}, u32[]{:S(2)}, u32[]{:S(2)}) %collective-permute-start.5) | collective-permute-done | bytes 139296 | tf_op jit(solution)/shard_map/ppermute | solution.py:250
  99.8 2.7 %collective-permute-done.6.get1_ref = bf16[544,128]{1,0:T(8,128)(2,1)S(1)} collective-permute-done((bf16[544,128]{1,0:T(8,128)(2,1)S(1)}, bf16[544,128]{1,0:T(8,128)(2,1)S(1)}, u32[]{:S(2)}, u32[]{:S(2)}) %collective-permute-start.6) | collective-permute-done | bytes 139296 | tf_op jit(solution)/shard_map/ppermute | solution.py:251
  102.5 0.1 broadcast_in_dim.5.row_key
  102.6 2.5 %finish.1 = bf16[384,768]{1,0:T(8,128)(2,1)} custom-call(s32[3]{0:T(128)S(1)} %pad_add_fusion.row_ref, bf16[2,384,384]{2,1,0:T(8,128)(2,1)S(1)} %get-tuple-element.16.paired_ref, bf16[544,128]{1,0:T(8,128)(2,1)S(1)} %collective-permute-done.5.get0_ref, bf16[544,128]{1,0:T(8,128)(2,1)S(1)} %collective-permute-done.6.get1_ref, ...), custom_call_target="tpu_custom_call" | custom-call | tf_op jit(solution)/shard_map/finish/pallas_call | solution.py:220
  (14 shorter events, 0.1 us)
Async XLA Ops:
  0.0 0.9 copy-start
  0.9 0.9 copy-start.1
  2.7 36.0 %all-to-all-start = ((bf16[8,32,768]{2,1,0:T(8,128)(2,1)}), bf16[8,32,768]{2,1,0:T(8,128)(2,1)S(1)}, u32[]{:S(2)}, u32[]{:S(2)}) async-start(bf16[8,32,768]{2,1,0:T(8,128)(2,1)} %get-tuple-element.12), calls=%async_computation | async-start | bytes 786432 | tf_op jit(solution)/shard_map/all_to_all | solution.py:238
  12.9 25.8 %collective-permute-start = (bf16[192,128]{1,0:T(8,128)(2,1)S(1)}, bf16[192,128]{1,0:T(8,128)(2,1)S(1)}, u32[]{:S(2)}, u32[]{:S(2)}) collective-permute-start(bf16[192,128]{1,0:T(8,128)(2,1)S(1)} %get-tuple-element.13), channel_id=1, source_target_pairs={{0,8},{1,9},{2,10},{3,11},{4,12},{5,13},{6,14},{7,15},{8,0},{9,1},... | collective-permute-start | bytes 147464 | tf_op jit(solution)/shard_map/ppermute | solution.py:239
  40.1 24.4 %copy-start.2 = (s32[12]{0:T(128)S(1)}, s32[12]{0:T(128)}, u32[]{:S(2)}) copy-start(s32[12]{0:T(128)} %param.6) | copy-start | bytes 148
  40.1 25.5 %all-to-all-start.1 = ((bf16[4,8,32,768]{3,2,1,0:T(8,128)(2,1)}), bf16[4,8,32,768]{3,2,1,0:T(8,128)(2,1)S(1)}, u32[]{:S(2)}, u32[]{:S(2)}) async-start(bf16[4,8,32,768]{3,2,1,0:T(8,128)(2,1)} %broadcast_in_dim.4), calls=%async_computation.1 | async-start | bytes 3145728 | tf_op jit(solution)/shard_map/all_to_all | solution.py:243
  44.2 10.8 %collective-permute-start.1 = (bf16[2,192,128]{2,1,0:T(8,128)(2,1)S(1)}, bf16[2,192,128]{2,1,0:T(8,128)(2,1)S(1)}, u32[]{:S(2)}, u32[]{:S(2)}) collective-permute-start(bf16[2,192,128]{2,1,0:T(8,128)(2,1)S(1)} %pad_maximum_fusion.1), channel_id=1, source_target_pairs={{0,2},{1,3},{2,4},{3,5},{4,6},{5,7},{6,0},{7,1},{8,10},{9,11},{10,... | collective-permute-start | bytes 294920 | tf_op jit(solution)/shard_map/ppermute | solution.py:247
  47.4 7.6 %collective-permute-start.2 = (bf16[2,192,128]{2,1,0:T(8,128)(2,1)S(1)}, bf16[2,192,128]{2,1,0:T(8,128)(2,1)S(1)}, u32[]{:S(2)}, u32[]{:S(2)}) collective-permute-start(bf16[2,192,128]{2,1,0:T(8,128)(2,1)S(1)} %pad_maximum_fusion.1), channel_id=1, source_target_pairs={{0,4},{1,5},{2,6},{3,7},{4,0},{5,1},{6,2},{7,3},{8,12},{9,13},{10,... | collective-permute-start | bytes 294920 | tf_op jit(solution)/shard_map/ppermute | solution.py:247
  52.0 5.8 %collective-permute-start.3 = (bf16[2,192,128]{2,1,0:T(8,128)(2,1)S(1)}, bf16[2,192,128]{2,1,0:T(8,128)(2,1)S(1)}, u32[]{:S(2)}, u32[]{:S(2)}) collective-permute-start(bf16[2,192,128]{2,1,0:T(8,128)(2,1)S(1)} %pad_maximum_fusion.1), channel_id=1, source_target_pairs={{0,6},{1,7},{2,0},{3,1},{4,2},{5,3},{6,4},{7,5},{8,14},{9,15},{10,... | collective-permute-start | bytes 294920 | tf_op jit(solution)/shard_map/ppermute | solution.py:247
  57.9 7.7 %collective-permute-start.4 = (bf16[4,2,192,128]{3,2,1,0:T(8,128)(2,1)S(1)}, bf16[4,2,192,128]{3,2,1,0:T(8,128)(2,1)S(1)}, u32[]{:S(2)}, u32[]{:S(2)}) collective-permute-start(bf16[4,2,192,128]{3,2,1,0:T(8,128)(2,1)S(1)} %pad_maximum_fusion.own_ref), channel_id=1, source_target_pairs={{0,1},{1,0},{2,3},{3,2},{4,5},{5,4},{6,7},{7,6},{8,9},{9,8},{10,11... | collective-permute-start | bytes 1179656 | tf_op jit(solution)/shard_map/ppermute | solution.py:248
  68.6 31.2 %collective-permute-start.5 = (bf16[544,128]{1,0:T(8,128)(2,1)S(1)}, bf16[544,128]{1,0:T(8,128)(2,1)S(1)}, u32[]{:S(2)}, u32[]{:S(2)}) collective-permute-start(bf16[544,128]{1,0:T(8,128)(2,1)S(1)} %get-tuple-element.17), channel_id=1, source_target_pairs={{0,0},{1,32},{2,64},{3,96},{4,128},{5,160},{6,192},{7,224},{8,256}... | collective-permute-start | bytes 417800 | tf_op jit(solution)/shard_map/ppermute | solution.py:250
  72.8 29.7 %collective-permute-start.6 = (bf16[544,128]{1,0:T(8,128)(2,1)S(1)}, bf16[544,128]{1,0:T(8,128)(2,1)S(1)}, u32[]{:S(2)}, u32[]{:S(2)}) collective-permute-start(bf16[544,128]{1,0:T(8,128)(2,1)S(1)} %get-tuple-element.18), channel_id=1, source_target_pairs={{0,16},{1,48},{2,80},{3,112},{4,144},{5,176},{6,208},{7,240},{8,27... | collective-permute-start | bytes 417800 | tf_op jit(solution)/shard_map/ppermute | solution.py:251

commit v3 on v0

v3 whole, which is shorter than its diff:
```python
import jax
import jax.numpy as jnp
from jax import lax
from jax.experimental import pallas as pl
from jax.experimental.pallas import tpu as pltpu
from jax.sharding import PartitionSpec as P

Q, S, X = 2, 4, 4
H, Y, CORE = 2, 4, 2
ROWS, COLS = Q * S * X, H * Y * CORE
OCC, WA, WB = 12, 32, 64
HALF = 32
GROUPS = OCC // 4
SIDE = OCC * 32
TILES = 17
STEPS = (0, 1, 3, 2)
VMEM = pl.BlockSpec(memory_space=pltpu.VMEM)
SMEM = pl.BlockSpec(memory_space=pltpu.SMEM)
HBM = pl.BlockSpec(memory_space=pltpu.HBM)
PARAMS = pltpu.CompilerParams(vmem_limit_bytes=48 * 1024 * 1024)


def bf16(*shape):
    return jax.ShapeDtypeStruct(shape, jnp.bfloat16)


def s_shift(step):
    return [(r, r // 16 * 16 + (r // X % S + step) % S * X + r % X) for r in range(ROWS)]


def q_swap():
    return [(r, r ^ (S * X)) for r in range(ROWS)]


def x_groups():
    return [[z * X + x for x in range(X)] for z in range(Q * S)]


def h_swap():
    return [(c, c ^ (Y * CORE)) for c in range(COLS)]


def y_swap(step):
    return [(c, c ^ (2 if step == 1 else 6)) for c in range(COLS)]


def core_swap():
    return [(c, c ^ 1) for c in range(COLS)]


def mirror_perm(step):
    return [
        (r * COLS + c, (2 * c + (step + r) % 2) * COLS + r // 2)
        for r in range(ROWS) for c in range(COLS)
    ]


def slot_of(shape):
    return lax.broadcasted_iota(jnp.int32, shape, 1) // HALF


def crossed(load, i, group):
    slot = slot_of((32, 128))
    out = None
    for s in range(4):
        piece = load(4 * group + s, i // 4)
        shift = (s - i % 4) % 4
        if shift:
            piece = pltpu.roll(piece, shift * HALF, 1)
        out = piece if out is None else jnp.where(slot == s, piece, out)
    return out


def full_tiles():
    return [(i, g) for i in range(OCC) for g in range(i // 4 + 1, GROUPS)]


def pack_kernel(a_hbm, w_hbm, a_out, w_out, a_ref, w_ref, sem):
    copies = [pltpu.make_async_copy(w_hbm, w_ref, sem.at[0]), pltpu.make_async_copy(a_hbm, a_ref, sem.at[1])]
    for copy in copies:
        copy.start()
    for copy in copies:
        copy.wait()
    for i in range(OCC // 2):
        a_out[32 * i : 32 * i + 32, :] = jnp.concatenate([a_ref[i], a_ref[i + 6]], axis=1)
    for g in range(GROUPS):
        block = [w_ref[4 * g + s].astype(jnp.float32) for s in range(4)]
        for half in range(2):
            cut = jnp.concatenate([b[:, HALF * half : HALF * half + HALF] for b in block], axis=1)
            lane = half * SIDE + 128 * g
            w_out[:, lane : lane + 128] = cut.astype(jnp.bfloat16)


def pack(amplitudes, cycle_vertex):
    return pl.pallas_call(
        pack_kernel,
        out_shape=(bf16(192, 128), bf16(32, 2 * SIDE)),
        in_specs=[HBM, HBM],
        out_specs=(VMEM, VMEM),
        scratch_shapes=[
            pltpu.VMEM(amplitudes.shape, jnp.bfloat16),
            pltpu.VMEM(cycle_vertex.shape, jnp.bfloat16),
            pltpu.SemaphoreType.DMA((2,)),
        ],
        compiler_params=PARAMS,
        name="pack",
    )(amplitudes, cycle_vertex)


def keys_kernel(place_ref, occ_ref, virt_ref, row_key, col_key, order):
    r, c = place_ref[5], place_ref[6]

    def cut(first):
        line = jnp.broadcast_to(virt_ref[pl.ds(first // 128, 1), :], (8, 128))
        return pltpu.roll(line, lax.rem(128 - lax.rem(first, 128), 128), 1)

    down = jnp.broadcast_to(cut(WA * r)[:1], (128, 128)).T[:32]
    for i in range(OCC):
        row_key[32 * i : 32 * i + 32, :] = down ^ occ_ref[i]
    slot = slot_of((8, 128))
    for half in range(2):
        line = cut(WB * c + HALF * half)
        wide = line
        for s in range(1, 4):
            wide = jnp.where(slot == s, pltpu.roll(line, s * HALF, 1), wide)
        for g in range(GROUPS):
            label = jnp.full((8, 128), occ_ref[4 * g], jnp.int32)
            for s in range(1, 4):
                label = jnp.where(slot == s, occ_ref[4 * g + s], label)
            col_key[half : half + 1, 128 * g : 128 * g + 128] = (wide ^ label)[:1]
    source = lax.broadcasted_iota(jnp.int32, (SIDE, SIDE), 0)
    target = lax.broadcasted_iota(jnp.int32, (SIDE, SIDE), 1)
    hit = (source % HALF) * OCC + source // HALF == target
    order[...] = jnp.where(hit, 1.0, 0.0).astype(jnp.bfloat16)


def keys(place, occupied_irrep, virtual_irrep):
    return pl.pallas_call(
        keys_kernel,
        out_shape=(
            jax.ShapeDtypeStruct((SIDE, 128), jnp.int32),
            jax.ShapeDtypeStruct((2, SIDE), jnp.int32),
            bf16(SIDE, SIDE),
        ),
        in_specs=[SMEM, SMEM, VMEM],
        out_specs=(VMEM, VMEM, VMEM),
        compiler_params=PARAMS,
        name="keys",
    )(place, occupied_irrep, virtual_irrep.reshape(8, 128))


def paired_half(half, lhs, w_ref, paired_ref, send_ref, prod, turned):
    lanes = pl.ds(pl.multiple_of(half * SIDE, 128), SIDE)
    prod[...] = jnp.dot(
        jnp.concatenate([lhs[p] for p in range(Q * S)], axis=1),
        jnp.concatenate([w_ref[x, k, q, :, lanes] for k in range(S) for q in range(Q) for x in range(X)], axis=0),
        preferred_element_type=jnp.float32,
    )

    def load(j, group):
        return prod[32 * j : 32 * j + 32, 128 * group : 128 * group + 128]

    for i in range(OCC):
        for g in range(GROUPS):
            paired_ref[32 * i : 32 * i + 32, 128 * g : 128 * g + 128] = (
                load(i, g) - crossed(load, i, g)
            ).astype(jnp.bfloat16)
    turned[...] = paired_ref[...].astype(jnp.float32).T

    def tile(i, group):
        return turned[32 * i : 32 * i + 32, 128 * group : 128 * group + 128]

    slot = slot_of((32, 128))
    out = [tile(i, g) for i, g in full_tiles()]
    for q in range(GROUPS):
        out.append(jnp.where(slot == 0, pltpu.roll(tile(4 * q + 2, q), HALF, 1), tile(4 * q, q)))
    out.append(jnp.where(slot < 2, pltpu.roll(tile(5, 1), 2 * HALF, 1), tile(1, 0)))
    out.append(tile(9, 2))
    for t, value in enumerate(out):
        send_ref[32 * t : 32 * t + 32, :] = value.astype(jnp.bfloat16)


def first_kernel(place_ref, own_ref, far_ref, w_ref, lhs, paired_ref, send_ref, prod, turned):
    core, y, q_own, s_own = place_ref[1], place_ref[2], place_ref[3], place_ref[4]
    for step in range(Y):
        shift = lax.rem(s_own + S - jnp.bitwise_xor(y, STEPS[step]), S)
        k = jnp.bitwise_xor(shift, shift // 2)
        for h in range(H):
            mine, other = own_ref[step, h], far_ref[step, h]
            first = jnp.where(core == 0, mine, other)
            second = jnp.where(core == 0, other, mine)
            at = Q * k + jnp.bitwise_xor(q_own, h)
            lhs[at, :192] = jnp.concatenate([first[:, :64], second[:, :64]], axis=1)
            lhs[at, 192:] = jnp.concatenate([first[:, 64:], second[:, 64:]], axis=1)
    paired_half(place_ref[0], lhs, w_ref, paired_ref, send_ref, prod, turned)


def second_kernel(place_ref, lhs, w_ref, paired_ref, send_ref, prod, turned):
    paired_half(1 - place_ref[0], lhs, w_ref, paired_ref, send_ref, prod, turned)


WORK = [pltpu.VMEM((SIDE, SIDE), jnp.float32), pltpu.VMEM((SIDE, SIDE), jnp.float32)]


def pair_first(place, a_mine, a_other, w_all):
    return pl.pallas_call(
        first_kernel,
        out_shape=(bf16(Q * S, SIDE, 128), bf16(SIDE, SIDE), bf16(TILES * 32, 128)),
        in_specs=[SMEM, VMEM, VMEM, VMEM],
        out_specs=(VMEM, VMEM, VMEM),
        scratch_shapes=WORK,
        compiler_params=PARAMS,
        name="pair_first",
    )(place, a_mine, a_other, w_all)


def pair_second(place, lhs, w_all):
    return pl.pallas_call(
        second_kernel,
        out_shape=(bf16(SIDE, SIDE), bf16(TILES * 32, 128)),
        in_specs=[SMEM, VMEM, VMEM],
        out_specs=(VMEM, VMEM),
        scratch_shapes=WORK,
        compiler_params=PARAMS,
        name="pair_second",
    )(place, lhs, w_all)


def residual_half(half, paired_ref, get_ref, row_key, col_key, order, upper, whole):
    slot = slot_of((32, 128))

    def got(t):
        return get_ref[32 * t : 32 * t + 32, :].astype(jnp.float32)

    def put(i, group, mirrored, floor):
        rows, lanes = slice(32 * i, 32 * i + 32), slice(128 * group, 128 * group + 128)
        diff = paired_ref[rows, lanes].astype(jnp.float32) + mirrored
        if floor >= 0:
            diff = jnp.where(slot > floor, diff, 0.0)
        upper[rows, lanes] = diff

    for t, (i, g) in enumerate(full_tiles()):
        put(i, g, got(t), -1)
    last = [got(15), got(16)]
    for q in range(GROUPS):
        piece = got(12 + q)
        put(4 * q, q, piece, 0)
        put(4 * q + 2, q, pltpu.roll(piece, 3 * HALF, 1), 2)
        put(4 * q + 1, q, (last[0], pltpu.roll(last[0], 2 * HALF, 1), last[1])[q], 1)
        upper[32 * (4 * q + 3) : 32 * (4 * q + 4), 128 * q : 128 * q + 128] = jnp.zeros((32, 128), jnp.float32)

    def load(j, group):
        return upper[32 * j : 32 * j + 32, 128 * group : 128 * group + 128]

    col = jnp.where(half == 0, col_key[0:1, :], col_key[1:2, :])
    for i in range(OCC):
        rows = slice(32 * i, 32 * i + 32)
        for g in range(GROUPS):
            lanes = slice(128 * g, 128 * g + 128)
            if g > i // 4:
                value = load(i, g)
            elif g < i // 4:
                value = -crossed(load, i, g)
            else:
                value = load(i, g) - crossed(load, i, g)
            allowed = row_key[rows, :] == col[:, lanes]
            whole[rows, lanes] = jnp.where(allowed, value, 0.0).astype(jnp.bfloat16)
    return jnp.dot(whole[...], order[...], preferred_element_type=jnp.float32).astype(jnp.bfloat16)


def finish_first_kernel(place_ref, paired_ref, get_ref, row_key, col_key, order, out_ref, upper, whole):
    out_ref[...] = residual_half(place_ref[0], paired_ref, get_ref, row_key, col_key, order, upper, whole)


def finish_second_kernel(place_ref, done_ref, paired_ref, get_ref, row_key, col_key, order, out_ref, upper, whole):
    half = place_ref[0]
    out_ref[:, pl.ds(pl.multiple_of(half * SIDE, 128), SIDE)] = done_ref[...]
    out_ref[:, pl.ds(pl.multiple_of((1 - half) * SIDE, 128), SIDE)] = residual_half(
        1 - half, paired_ref, get_ref, row_key, col_key, order, upper, whole
    )


def finish(kernel, width, name, place, *arrays):
    return pl.pallas_call(
        kernel,
        out_shape=bf16(SIDE, width),
        in_specs=[SMEM] + [VMEM] * len(arrays),
        out_specs=VMEM,
        scratch_shapes=[pltpu.VMEM((SIDE, SIDE), jnp.float32), pltpu.VMEM((SIDE, SIDE), jnp.bfloat16)],
        compiler_params=PARAMS,
        name=name,
    )(place, *arrays)


def on_device(amplitudes, cycle_vertex, occupied_irrep, virtual_irrep):
    r, c = lax.axis_index("row"), lax.axis_index("col")
    place = jnp.stack([r % 2, c % 2, c // 2 % Y, r // (S * X), r // X % S, r, c]).astype(jnp.int32)
    a_own, w_own = pack(amplitudes, cycle_vertex)
    a_far = lax.ppermute(a_own, "col", h_swap())
    w_far = lax.ppermute(w_own, "row", q_swap())
    low = c < Y * CORE
    a_two = jnp.stack([jnp.where(low, a_own, a_far), jnp.where(low, a_far, a_own)])
    w_two = jnp.stack([w_own, w_far])
    w_z = jnp.stack([w_two] + [lax.ppermute(w_two, "row", s_shift(k)) for k in STEPS[1:]])
    w_z, a_two = lax.optimization_barrier((w_z, a_two))
    w_all = lax.all_to_all(
        jnp.broadcast_to(w_z[None], (X, S, Q, 32, 2 * SIDE)), "row", 0, 0, tiled=True, axis_index_groups=x_groups()
    )
    a_pair = jnp.stack([a_two, lax.ppermute(a_two, "col", y_swap(1))])
    a_mine = jnp.concatenate([a_pair, lax.ppermute(a_pair, "col", y_swap(2))])
    a_other = lax.ppermute(a_mine, "col", core_swap())
    row_key, col_key, order = keys(place, occupied_irrep, virtual_irrep)
    lhs, paired0, send0 = pair_first(place, a_mine, a_other, w_all)
    get0 = lax.ppermute(send0, ("row", "col"), mirror_perm(0))
    paired1, send1 = pair_second(place, lhs, w_all)
    get1 = lax.ppermute(send1, ("row", "col"), mirror_perm(1))
    done = finish(finish_first_kernel, SIDE, "finish_first", place, paired0, get0, row_key, col_key, order)
    result = finish(
        finish_second_kernel, 2 * SIDE, "finish_second", place, done, paired1, get1, row_key, col_key, order
    )
    return result.reshape(OCC, WA, WB * OCC)


def solution(mesh):
    return jax.shard_map(
        on_device,
        mesh=mesh,
        in_specs=(P(None, "row", "col"), P(None, "row", "col"), P(), P()),
        out_specs=P(None, "row", "col"),
        check_vma=False,
    )
```

time: 515 us -> 98.7 us (0.19)
  the two profiles are of different devices: /device:TPU:8 before, /device:TPU:129 now
where the time goes in v3:
time: 98.7 us; the launch traced here: 98.2 us
  starting transfers between devices  55.6 us (56%)
  waiting for transfers between devices  31.1 us (32%)
  Pallas kernels  7.9 us (8%)
  local copies, waits for them, and re-layouts  3.24 us (3%)
    ppermute x1, waiting for transfers between devices, on_device(): get0 = lax.ppermute(send0, ('row', 'col'), mirror_perm(0))  17.2 us
    ppermute x1, starting transfers between devices, on_device(): a_far = lax.ppermute(a_own, 'col', h_swap())  13.9 us
    ppermute x1, starting transfers between devices, on_device(): get0 = lax.ppermute(send0, ('row', 'col'), mirror_perm(0))  10.4 us
    ppermute x3, starting transfers between devices, on_device(): lax.ppermute(w_two, 'row', s_shift(k))  9 us
    ppermute x1, starting transfers between devices, on_device(): a_other = lax.ppermute(a_mine, 'col', core_swap())  5.72 us
    ppermute x3, waiting for transfers between devices, on_device(): lax.ppermute(w_two, 'row', s_shift(k))  5.32 us
    ppermute x1, starting transfers between devices, on_device(): a_mine = jnp.concatenate([a_pair, lax.ppermute(a_pair, 'col', y_swap(2))])  4.64 us
    all_to_all x1, starting transfers between devices, on_device(): lax.all_to_all(jnp.broadcast_to(w_z[None], (X, S, Q, 32, 2 * SIDE)), 'row...  4.01 us
  transfers between devices with their start and end apart: 11, of which 7 were waited for; matrix products, arithmetic and copies ran while one was open for 0% of the time, Pallas kernels for 4%

profile of v3, /device:TPU:129, one launch (start us, length us, event | category | flops | bytes accessed | tf_op | source)
XLA Modules:
  0.0 98.2 jit_solution(11060192473048043592)
XLA Ops:
  0.0 0.9 copy-done
  0.9 0.9 copy-done.1
  1.8 0.4 pack.1
  2.2 1.9 %collective-permute-start = (bf16[32,768]{1,0:T(8,128)(2,1)S(1)}, bf16[32,768]{1,0:T(8,128)(2,1)S(1)}, u32[]{:S(2)}, u32[]{:S(2)}) collective-permute-start(bf16[32,768]{1,0:T(8,128)(2,1)S(1)} %get-tuple-element.17), channel_id=1, source_target_pairs={{0,256},{16,272},{32,288},{48,304},{64,320},{80,336},{96,352},{112... | collective-permute-start | bytes 147464 | tf_op jit(solution)/shard_map/ppermute | solution.py:300
  4.1 13.9 %collective-permute-start.4 = (bf16[192,128]{1,0:T(8,128)(2,1)S(1)}, bf16[192,128]{1,0:T(8,128)(2,1)S(1)}, u32[]{:S(2)}, u32[]{:S(2)}) collective-permute-start(bf16[192,128]{1,0:T(8,128)(2,1)S(1)} %get-tuple-element.18), channel_id=1, source_target_pairs={{0,8},{1,9},{2,10},{3,11},{4,12},{5,13},{6,14},{7,15},{8,0},{9,1},... | collective-permute-start | bytes 147464 | tf_op jit(solution)/shard_map/ppermute | solution.py:299
  18.0 2.6 %collective-permute-start.1 = (bf16[2,32,768]{2,1,0:T(8,128)(2,1)S(1)}, bf16[2,32,768]{2,1,0:T(8,128)(2,1)S(1)}, u32[]{:S(2)}, u32[]{:S(2)}) collective-permute-start(bf16[2,32,768]{2,1,0:T(8,128)(2,1)S(1)} %get-tuple-element.32), channel_id=1, source_target_pairs={{0,64},{16,80},{32,96},{48,112},{64,128},{80,144},{96,160},{112,17... | collective-permute-start | bytes 294920 | tf_op jit(solution)/shard_map/ppermute | solution.py:304
  20.7 4.4 %collective-permute-start.2 = (bf16[2,32,768]{2,1,0:T(8,128)(2,1)S(1)}, bf16[2,32,768]{2,1,0:T(8,128)(2,1)S(1)}, u32[]{:S(2)}, u32[]{:S(2)}) collective-permute-start(bf16[2,32,768]{2,1,0:T(8,128)(2,1)S(1)} %get-tuple-element.32), channel_id=1, source_target_pairs={{0,192},{16,208},{32,224},{48,240},{64,0},{80,16},{96,32},{112,48}... | collective-permute-start | bytes 294920 | tf_op jit(solution)/shard_map/ppermute | solution.py:304
  25.1 1.9 %collective-permute-start.3 = (bf16[2,32,768]{2,1,0:T(8,128)(2,1)S(1)}, bf16[2,32,768]{2,1,0:T(8,128)(2,1)S(1)}, u32[]{:S(2)}, u32[]{:S(2)}) collective-permute-start(bf16[2,32,768]{2,1,0:T(8,128)(2,1)S(1)} %get-tuple-element.32), channel_id=1, source_target_pairs={{0,128},{16,144},{32,160},{48,176},{64,192},{80,208},{96,224},{112... | collective-permute-start | bytes 294920 | tf_op jit(solution)/shard_map/ppermute | solution.py:304
  27.1 0.0 collective-permute-done.4
  27.1 0.8 collective-permute-done.2
  27.9 4.5 %collective-permute-done.3 = bf16[2,32,768]{2,1,0:T(8,128)(2,1)S(1)} collective-permute-done((bf16[2,32,768]{2,1,0:T(8,128)(2,1)S(1)}, bf16[2,32,768]{2,1,0:T(8,128)(2,1)S(1)}, u32[]{:S(2)}, u32[]{:S(2)}) %collective-permute-start.3) | collective-permute-done | bytes 98336 | tf_op jit(solution)/shard_map/ppermute | solution.py:304
  32.4 0.1 pad_maximum_fusion
  32.5 1.4 %broadcast_in_dim.2 = bf16[4,4,2,32,768]{4,3,2,1,0:T(8,128)(2,1)} broadcast(bf16[4,2,32,768]{3,2,1,0:T(8,128)(2,1)S(1)} %pad_maximum_fusion), dimensions={1,2,3,4} | broadcast | bytes 1966080 | tf_op jit(solution)/shard_map/broadcast_in_dim | solution.py:307
  33.8 4.0 %all-to-all-start = ((bf16[4,4,2,32,768]{4,3,2,1,0:T(8,128)(2,1)}), bf16[4,4,2,32,768]{4,3,2,1,0:T(8,128)(2,1)S(1)}, u32[]{:S(2)}, u32[]{:S(2)}) async-start(bf16[4,4,2,32,768]{4,3,2,1,0:T(8,128)(2,1)} %broadcast_in_dim.2), calls=%async_computation | async-start | bytes 3145728 | tf_op jit(solution)/shard_map/all_to_all | solution.py:306
  37.9 3.2 %collective-permute-start.5 = (bf16[2,192,128]{2,1,0:T(8,128)(2,1)S(1)}, bf16[2,192,128]{2,1,0:T(8,128)(2,1)S(1)}, u32[]{:S(2)}, u32[]{:S(2)}) collective-permute-start(bf16[2,192,128]{2,1,0:T(8,128)(2,1)S(1)} %pad_maximum_fusion.4), channel_id=1, source_target_pairs={{0,2},{1,3},{2,0},{3,1},{4,6},{5,7},{6,4},{7,5},{8,10},{9,11},{10,... | collective-permute-start | bytes 294920 | tf_op jit(solution)/shard_map/ppermute | solution.py:309
  41.1 2.4 %collective-permute-done.5 = bf16[2,192,128]{2,1,0:T(8,128)(2,1)S(1)} collective-permute-done((bf16[2,192,128]{2,1,0:T(8,128)(2,1)S(1)}, bf16[2,192,128]{2,1,0:T(8,128)(2,1)S(1)}, u32[]{:S(2)}, u32[]{:S(2)}) %collective-permute-start.5) | collective-permute-done | bytes 98336 | tf_op jit(solution)/shard_map/ppermute | solution.py:309
  43.5 4.6 %collective-permute-start.6 = (bf16[2,2,192,128]{3,2,1,0:T(8,128)(2,1)S(1)}, bf16[2,2,192,128]{3,2,1,0:T(8,128)(2,1)S(1)}, u32[]{:S(2)}, u32[]{:S(2)}) collective-permute-start(bf16[2,2,192,128]{3,2,1,0:T(8,128)(2,1)S(1)} %pad_maximum_fusion.2), channel_id=1, source_target_pairs={{0,6},{1,7},{2,4},{3,5},{4,2},{5,3},{6,0},{7,1},{8,14},{9,15},{10,... | collective-permute-start | bytes 589832 | tf_op jit(solution)/shard_map/ppermute | solution.py:310
  48.2 3.3 %collective-permute-done.6 = bf16[2,2,192,128]{3,2,1,0:T(8,128)(2,1)S(1)} collective-permute-done((bf16[2,2,192,128]{3,2,1,0:T(8,128)(2,1)S(1)}, bf16[2,2,192,128]{3,2,1,0:T(8,128)(2,1)S(1)}, u32[]{:S(2)}, u32[]{:S(2)}) %collective-permute-start.6) | collective-permute-done | bytes 196640 | tf_op jit(solution)/shard_map/ppermute | solution.py:310
  51.6 5.7 %collective-permute-start.7 = (bf16[4,2,192,128]{3,2,1,0:T(8,128)(2,1)S(1)}, bf16[4,2,192,128]{3,2,1,0:T(8,128)(2,1)S(1)}, u32[]{:S(2)}, u32[]{:S(2)}) collective-permute-start(bf16[4,2,192,128]{3,2,1,0:T(8,128)(2,1)S(1)} %pad_maximum_fusion.1.own_ref), channel_id=1, source_target_pairs={{0,1},{1,0},{2,3},{3,2},{4,5},{5,4},{6,7},{7,6},{8,9},{9,8},{10,11... | collective-permute-start | bytes 1179656 | tf_op jit(solution)/shard_map/ppermute | solution.py:311
  57.4 0.1 stack.73.place_ref
  57.5 1.2 %collective-permute-done.7.far_ref = bf16[4,2,192,128]{3,2,1,0:T(8,128)(2,1)S(1)} collective-permute-done((bf16[4,2,192,128]{3,2,1,0:T(8,128)(2,1)S(1)}, bf16[4,2,192,128]{3,2,1,0:T(8,128)(2,1)S(1)}, u32[]{:S(2)}, u32[]{:S(2)}) %collective-permute-start.7) | collective-permute-done | bytes 393248 | tf_op jit(solution)/shard_map/ppermute | solution.py:311
  58.6 1.9 %pair_first.1 = (bf16[8,384,128]{2,1,0:T(8,128)(2,1)S(1)}, bf16[384,384]{1,0:T(8,128)(2,1)S(1)}, bf16[544,128]{1,0:T(8,128)(2,1)S(1)}) custom-call(s32[7]{0:T(128)S(1)} %stack.73.place_ref, bf16[4,2,192,128]{3,2,1,0:T(8,128)(2,1)S(1)} %pad_maximum_fusion.1.own_ref, bf16[4,2,192,128]{3,2,1,0:T(8,128)(2,1)S(1)} %collective-permute-done.7.far_ref, ...), custom_call_target="tpu_custom_call" | custom-call | tf_op jit(solution)/shard_map/pair_first/pallas_call | solution.py:206
  60.6 0.0 copy-start.2
  60.6 0.0 copy-start.3
  60.6 10.4 %collective-permute-start.8 = (bf16[544,128]{1,0:T(8,128)(2,1)S(1)}, bf16[544,128]{1,0:T(8,128)(2,1)S(1)}, u32[]{:S(2)}, u32[]{:S(2)}) collective-permute-start(bf16[544,128]{1,0:T(8,128)(2,1)S(1)} %get-tuple-element.22), channel_id=1, source_target_pairs={{0,0},{1,32},{2,64},{3,96},{4,128},{5,160},{6,192},{7,224},{8,256}... | collective-permute-start | bytes 417800 | tf_op jit(solution)/shard_map/ppermute | solution.py:314
  71.0 1.7 %pair_second.1 = (bf16[384,384]{1,0:T(8,128)(2,1)S(1)}, bf16[544,128]{1,0:T(8,128)(2,1)S(1)}) custom-call(s32[7]{0:T(128)S(1)} %stack.73.place_ref, bf16[8,384,128]{2,1,0:T(8,128)(2,1)S(1)} %get-tuple-element.26.lhs, bf16[4,4,2,32,768]{4,3,2,1,0:T(8,128)(2,1)S(1)} %all-to-all-done.w_ref), custom_call_target="tpu_custom_call" | custom-call | tf_op jit(solution)/shard_map/pair_second/pallas_call | solution.py:218
  72.7 2.8 %collective-permute-start.9 = (bf16[544,128]{1,0:T(8,128)(2,1)S(1)}, bf16[544,128]{1,0:T(8,128)(2,1)S(1)}, u32[]{:S(2)}, u32[]{:S(2)}) collective-permute-start(bf16[544,128]{1,0:T(8,128)(2,1)S(1)} %get-tuple-element.28), channel_id=1, source_target_pairs={{0,16},{1,48},{2,80},{3,112},{4,144},{5,176},{6,208},{7,240},{8,27... | collective-permute-start | bytes 417800 | tf_op jit(solution)/shard_map/ppermute | solution.py:316
  75.5 0.8 keys.1
  76.2 17.2 %collective-permute-done.8.get_ref = bf16[544,128]{1,0:T(8,128)(2,1)S(1)} collective-permute-done((bf16[544,128]{1,0:T(8,128)(2,1)S(1)}, bf16[544,128]{1,0:T(8,128)(2,1)S(1)}, u32[]{:S(2)}, u32[]{:S(2)}) %collective-permute-start.8) | collective-permute-done | bytes 139296 | tf_op jit(solution)/shard_map/ppermute | solution.py:314
  93.5 1.2 %finish_first.1.done_ref = bf16[384,384]{1,0:T(8,128)(2,1)S(1)} custom-call(s32[7]{0:T(128)S(1)} %stack.73.place_ref, bf16[384,384]{1,0:T(8,128)(2,1)S(1)} %get-tuple-element.21.paired_ref, bf16[544,128]{1,0:T(8,128)(2,1)S(1)} %collective-permute-done.8.get_ref, s32[384,128]{1,0:T(8,128)S(1)} %get-tuple-element.23.row_key, ...), custom_call_target="tpu_custom_call" | custom-call | tf_op jit(solution)/shard_map/finish_first/pallas_call | solution.py:284
  94.6 1.6 %collective-permute-done.9.get_ref = bf16[544,128]{1,0:T(8,128)(2,1)S(1)} collective-permute-done((bf16[544,128]{1,0:T(8,128)(2,1)S(1)}, bf16[544,128]{1,0:T(8,128)(2,1)S(1)}, u32[]{:S(2)}, u32[]{:S(2)}) %collective-permute-start.9) | collective-permute-done | bytes 139296 | tf_op jit(solution)/shard_map/ppermute | solution.py:316
  96.2 2.0 %finish_second.1 = bf16[384,768]{1,0:T(8,128)(2,1)} custom-call(s32[7]{0:T(128)S(1)} %stack.73.place_ref, bf16[384,384]{1,0:T(8,128)(2,1)S(1)} %finish_first.1.done_ref, bf16[384,384]{1,0:T(8,128)(2,1)S(1)} %get-tuple-element.27.paired_ref, bf16[544,128]{1,0:T(8,128)(2,1)S(1)} %collective-permute-done.9.get_ref, s32[384,128]{1,0:T(8,128)S(1)} %get-tuple-element.23.row_key, ...), custom_call_target="tpu_custom_call" | custom-call | tf_op jit(solution)/shard_map/finish_second/pallas_call | solution.py:284
  (12 shorter events, 0.1 us)
Async XLA Ops:
  0.0 0.9 copy-start
  0.9 0.9 copy-start.1
  2.2 15.8 %collective-permute-start = (bf16[32,768]{1,0:T(8,128)(2,1)S(1)}, bf16[32,768]{1,0:T(8,128)(2,1)S(1)}, u32[]{:S(2)}, u32[]{:S(2)}) collective-permute-start(bf16[32,768]{1,0:T(8,128)(2,1)S(1)} %get-tuple-element.17), channel_id=1, source_target_pairs={{0,256},{16,272},{32,288},{48,304},{64,320},{80,336},{96,352},{112... | collective-permute-start | bytes 147464 | tf_op jit(solution)/shard_map/ppermute | solution.py:300
  4.1 23.0 %collective-permute-start.4 = (bf16[192,128]{1,0:T(8,128)(2,1)S(1)}, bf16[192,128]{1,0:T(8,128)(2,1)S(1)}, u32[]{:S(2)}, u32[]{:S(2)}) collective-permute-start(bf16[192,128]{1,0:T(8,128)(2,1)S(1)} %get-tuple-element.18), channel_id=1, source_target_pairs={{0,8},{1,9},{2,10},{3,11},{4,12},{5,13},{6,14},{7,15},{8,0},{9,1},... | collective-permute-start | bytes 147464 | tf_op jit(solution)/shard_map/ppermute | solution.py:299
  18.0 9.1 %collective-permute-start.1 = (bf16[2,32,768]{2,1,0:T(8,128)(2,1)S(1)}, bf16[2,32,768]{2,1,0:T(8,128)(2,1)S(1)}, u32[]{:S(2)}, u32[]{:S(2)}) collective-permute-start(bf16[2,32,768]{2,1,0:T(8,128)(2,1)S(1)} %get-tuple-element.32), channel_id=1, source_target_pairs={{0,64},{16,80},{32,96},{48,112},{64,128},{80,144},{96,160},{112,17... | collective-permute-start | bytes 294920 | tf_op jit(solution)/shard_map/ppermute | solution.py:304
  20.7 7.2 %collective-permute-start.2 = (bf16[2,32,768]{2,1,0:T(8,128)(2,1)S(1)}, bf16[2,32,768]{2,1,0:T(8,128)(2,1)S(1)}, u32[]{:S(2)}, u32[]{:S(2)}) collective-permute-start(bf16[2,32,768]{2,1,0:T(8,128)(2,1)S(1)} %get-tuple-element.32), channel_id=1, source_target_pairs={{0,192},{16,208},{32,224},{48,240},{64,0},{80,16},{96,32},{112,48}... | collective-permute-start | bytes 294920 | tf_op jit(solution)/shard_map/ppermute | solution.py:304
  25.1 7.3 %collective-permute-start.3 = (bf16[2,32,768]{2,1,0:T(8,128)(2,1)S(1)}, bf16[2,32,768]{2,1,0:T(8,128)(2,1)S(1)}, u32[]{:S(2)}, u32[]{:S(2)}) collective-permute-start(bf16[2,32,768]{2,1,0:T(8,128)(2,1)S(1)} %get-tuple-element.32), channel_id=1, source_target_pairs={{0,128},{16,144},{32,160},{48,176},{64,192},{80,208},{96,224},{112... | collective-permute-start | bytes 294920 | tf_op jit(solution)/shard_map/ppermute | solution.py:304
  33.8 24.8 %all-to-all-start = ((bf16[4,4,2,32,768]{4,3,2,1,0:T(8,128)(2,1)}), bf16[4,4,2,32,768]{4,3,2,1,0:T(8,128)(2,1)S(1)}, u32[]{:S(2)}, u32[]{:S(2)}) async-start(bf16[4,4,2,32,768]{4,3,2,1,0:T(8,128)(2,1)} %broadcast_in_dim.2), calls=%async_computation | async-start | bytes 3145728 | tf_op jit(solution)/shard_map/all_to_all | solution.py:306
  37.9 5.6 %collective-permute-start.5 = (bf16[2,192,128]{2,1,0:T(8,128)(2,1)S(1)}, bf16[2,192,128]{2,1,0:T(8,128)(2,1)S(1)}, u32[]{:S(2)}, u32[]{:S(2)}) collective-permute-start(bf16[2,192,128]{2,1,0:T(8,128)(2,1)S(1)} %pad_maximum_fusion.4), channel_id=1, source_target_pairs={{0,2},{1,3},{2,0},{3,1},{4,6},{5,7},{6,4},{7,5},{8,10},{9,11},{10,... | collective-permute-start | bytes 294920 | tf_op jit(solution)/shard_map/ppermute | solution.py:309
  43.5 8.0 %collective-permute-start.6 = (bf16[2,2,192,128]{3,2,1,0:T(8,128)(2,1)S(1)}, bf16[2,2,192,128]{3,2,1,0:T(8,128)(2,1)S(1)}, u32[]{:S(2)}, u32[]{:S(2)}) collective-permute-start(bf16[2,2,192,128]{3,2,1,0:T(8,128)(2,1)S(1)} %pad_maximum_fusion.2), channel_id=1, source_target_pairs={{0,6},{1,7},{2,4},{3,5},{4,2},{5,3},{6,0},{7,1},{8,14},{9,15},{10,... | collective-permute-start | bytes 589832 | tf_op jit(solution)/shard_map/ppermute | solution.py:310
  51.6 7.1 %collective-permute-start.7 = (bf16[4,2,192,128]{3,2,1,0:T(8,128)(2,1)S(1)}, bf16[4,2,192,128]{3,2,1,0:T(8,128)(2,1)S(1)}, u32[]{:S(2)}, u32[]{:S(2)}) collective-permute-start(bf16[4,2,192,128]{3,2,1,0:T(8,128)(2,1)S(1)} %pad_maximum_fusion.1.own_ref), channel_id=1, source_target_pairs={{0,1},{1,0},{2,3},{3,2},{4,5},{5,4},{6,7},{7,6},{8,9},{9,8},{10,11... | collective-permute-start | bytes 1179656 | tf_op jit(solution)/shard_map/ppermute | solution.py:311
  60.6 14.9 %copy-start.2 = (s32[1024]{0:T(1024)S(1)}, s32[1024]{0:T(1024)}, u32[]{:S(2)}) copy-start(s32[1024]{0:T(1024)} %param.7) | copy-start | bytes 12292
  60.6 14.9 %copy-start.3 = (s32[12]{0:T(128)S(1)}, s32[12]{0:T(128)}, u32[]{:S(2)}) copy-start(s32[12]{0:T(128)} %occ_ref.1) | copy-start | bytes 148
  60.6 32.9 %collective-permute-start.8 = (bf16[544,128]{1,0:T(8,128)(2,1)S(1)}, bf16[544,128]{1,0:T(8,128)(2,1)S(1)}, u32[]{:S(2)}, u32[]{:S(2)}) collective-permute-start(bf16[544,128]{1,0:T(8,128)(2,1)S(1)} %get-tuple-element.22), channel_id=1, source_target_pairs={{0,0},{1,32},{2,64},{3,96},{4,128},{5,160},{6,192},{7,224},{8,256}... | collective-permute-start | bytes 417800 | tf_op jit(solution)/shard_map/ppermute | solution.py:314
  72.7 23.5 %collective-permute-start.9 = (bf16[544,128]{1,0:T(8,128)(2,1)S(1)}, bf16[544,128]{1,0:T(8,128)(2,1)S(1)}, u32[]{:S(2)}, u32[]{:S(2)}) collective-permute-start(bf16[544,128]{1,0:T(8,128)(2,1)S(1)} %get-tuple-element.28), channel_id=1, source_target_pairs={{0,16},{1,48},{2,80},{3,112},{4,144},{5,176},{6,208},{7,240},{8,27... | collective-permute-start | bytes 417800 | tf_op jit(solution)/shard_map/ppermute | solution.py:316

commit v4 on v3

--- a/solution.py
+++ b/solution.py
@@ -1,3 +1,5 @@
+import functools
+
 import jax
 import jax.numpy as jnp
 from jax import lax
@@ -14,6 +16,7 @@
 SIDE = OCC * 32
 TILES = 17
 STEPS = (0, 1, 3, 2)
+PARTS = [slice(r, r + 96) for r in range(0, SIDE, 96)]
 VMEM = pl.BlockSpec(memory_space=pltpu.VMEM)
 SMEM = pl.BlockSpec(memory_space=pltpu.SMEM)
 HBM = pl.BlockSpec(memory_space=pltpu.HBM)
@@ -41,7 +44,7 @@
 
 
 def y_swap(step):
-    return [(c, c ^ (2 if step == 1 else 6)) for c in range(COLS)]
+    return [(c, c ^ (CORE * step)) for c in range(COLS)]
 
 
 def core_swap():
@@ -75,14 +78,7 @@
     return [(i, g) for i in range(OCC) for g in range(i // 4 + 1, GROUPS)]
 
 
-def pack_kernel(a_hbm, w_hbm, a_out, w_out, a_ref, w_ref, sem):
-    copies = [pltpu.make_async_copy(w_hbm, w_ref, sem.at[0]), pltpu.make_async_copy(a_hbm, a_ref, sem.at[1])]
-    for copy in copies:
-        copy.start()
-    for copy in copies:
-        copy.wait()
-    for i in range(OCC // 2):
-        a_out[32 * i : 32 * i + 32, :] = jnp.concatenate([a_ref[i], a_ref[i + 6]], axis=1)
+def pack_w_kernel(w_ref, w_out):
     for g in range(GROUPS):
         block = [w_ref[4 * g + s].astype(jnp.float32) for s in range(4)]
         for half in range(2):
@@ -91,20 +87,46 @@
             w_out[:, lane : lane + 128] = cut.astype(jnp.bfloat16)
 
 
-def pack(amplitudes, cycle_vertex):
-    return pl.pallas_call(
-        pack_kernel,
-        out_shape=(bf16(192, 128), bf16(32, 2 * SIDE)),
-        in_specs=[HBM, HBM],
-        out_specs=(VMEM, VMEM),
-        scratch_shapes=[
-            pltpu.VMEM(amplitudes.shape, jnp.bfloat16),
-            pltpu.VMEM(cycle_vertex.shape, jnp.bfloat16),
-            pltpu.SemaphoreType.DMA((2,)),
-        ],
-        compiler_params=PARAMS,
-        name="pack",
-    )(amplitudes, cycle_vertex)
+def pack_a_kernel(a_ref, a_out):
+    for i in range(OCC // 2):
+        a_out[32 * i : 32 * i + 32, :] = jnp.concatenate([a_ref[i], a_ref[i + 6]], axis=1)
+
+
+def pack(kernel, shape, name, array):
+    return pl.pallas_call(
+        kernel,
+        out_shape=bf16(*shape),
+        in_specs=[VMEM],
+        out_specs=VMEM,
+        compiler_params=PARAMS,
+        name=name,
+    )(array)
+
+
+def spread_kernel(first, count, *refs):
+    blocks, out, sem = refs[-count - 2 : -2], refs[-2], refs[-1]
+    copies = [
+        pltpu.make_async_copy(blocks[k], out.at[x, first + k], sem.at[count * x + k])
+        for x in range(X) for k in range(count)
+    ]
+    for copy in copies:
+        copy.start()
+    for copy in copies:
+        copy.wait()
+
+
+def spread(first, blocks, begun, name):
+    count = len(blocks)
+    return pl.pallas_call(
+        functools.partial(spread_kernel, first, count),
+        out_shape=bf16(X, S, *blocks[0].shape),
+        in_specs=[HBM] * len(begun) + [VMEM] * count,
+        out_specs=HBM,
+        scratch_shapes=[pltpu.SemaphoreType.DMA((count * X,))],
+        input_output_aliases={0: 0} if begun else {},
+        compiler_params=PARAMS,
+        name=name,
+    )(*begun, *blocks)
 
 
 def keys_kernel(place_ref, occ_ref, virt_ref, row_key, col_key, order):
@@ -265,28 +287,42 @@
                 value = load(i, g) - crossed(load, i, g)
             allowed = row_key[rows, :] == col[:, lanes]
             whole[rows, lanes] = jnp.where(allowed, value, 0.0).astype(jnp.bfloat16)
-    return jnp.dot(whole[...], order[...], preferred_element_type=jnp.float32).astype(jnp.bfloat16)
-
-
-def finish_first_kernel(place_ref, paired_ref, get_ref, row_key, col_key, order, out_ref, upper, whole):
-    out_ref[...] = residual_half(place_ref[0], paired_ref, get_ref, row_key, col_key, order, upper, whole)
-
-
-def finish_second_kernel(place_ref, done_ref, paired_ref, get_ref, row_key, col_key, order, out_ref, upper, whole):
+    for rows in PARTS:
+        yield rows, jnp.dot(whole[rows, :], order[...], preferred_element_type=jnp.float32).astype(jnp.bfloat16)
+
+
+def half_lanes(half):
+    return pl.ds(pl.multiple_of(half * SIDE, 128), SIDE)
+
+
+def finish_first_kernel(place_ref, paired_ref, get_ref, row_key, col_key, order, done_ref, upper, whole):
+    for rows, value in residual_half(place_ref[0], paired_ref, get_ref, row_key, col_key, order, upper, whole):
+        done_ref[rows, :] = value
+
+
+def finish_second_kernel(
+    place_ref, done_ref, paired_ref, get_ref, row_key, col_key, order, out_ref, upper, whole, result, sem
+):
     half = place_ref[0]
-    out_ref[:, pl.ds(pl.multiple_of(half * SIDE, 128), SIDE)] = done_ref[...]
-    out_ref[:, pl.ds(pl.multiple_of((1 - half) * SIDE, 128), SIDE)] = residual_half(
-        1 - half, paired_ref, get_ref, row_key, col_key, order, upper, whole
-    )
-
-
-def finish(kernel, width, name, place, *arrays):
+    copies = [pltpu.make_async_copy(done_ref, out_ref.at[:, half_lanes(half)], sem.at[len(PARTS)])]
+    copies[0].start()
+    for rows, value in residual_half(1 - half, paired_ref, get_ref, row_key, col_key, order, upper, whole):
+        result[rows, :] = value
+        copies.append(
+            pltpu.make_async_copy(result.at[rows], out_ref.at[rows, half_lanes(1 - half)], sem.at[len(copies) - 1])
+        )
+        copies[-1].start()
+    for copy in copies:
+        copy.wait()
+
+
+def finish(kernel, width, out_space, scratch, name, place, *arrays):
     return pl.pallas_call(
         kernel,
         out_shape=bf16(SIDE, width),
         in_specs=[SMEM] + [VMEM] * len(arrays),
-        out_specs=VMEM,
-        scratch_shapes=[pltpu.VMEM((SIDE, SIDE), jnp.float32), pltpu.VMEM((SIDE, SIDE), jnp.bfloat16)],
+        out_specs=out_space,
+        scratch_shapes=[pltpu.VMEM((SIDE, SIDE), jnp.float32), pltpu.VMEM((SIDE, SIDE), jnp.bfloat16)] + scratch,
         compiler_params=PARAMS,
         name=name,
     )(place, *arrays)
@@ -295,28 +331,32 @@
 def on_device(amplitudes, cycle_vertex, occupied_irrep, virtual_irrep):
     r, c = lax.axis_index("row"), lax.axis_index("col")
     place = jnp.stack([r % 2, c % 2, c // 2 % Y, r // (S * X), r // X % S, r, c]).astype(jnp.int32)
-    a_own, w_own = pack(amplitudes, cycle_vertex)
+    w_own = pack(pack_w_kernel, (32, 2 * SIDE), "pack_w", cycle_vertex)
+    a_own = pack(pack_a_kernel, (192, 128), "pack_a", amplitudes)
     a_far = lax.ppermute(a_own, "col", h_swap())
     w_far = lax.ppermute(w_own, "row", q_swap())
     low = c < Y * CORE
     a_two = jnp.stack([jnp.where(low, a_own, a_far), jnp.where(low, a_far, a_own)])
     w_two = jnp.stack([w_own, w_far])
-    w_z = jnp.stack([w_two] + [lax.ppermute(w_two, "row", s_shift(k)) for k in STEPS[1:]])
-    w_z, a_two = lax.optimization_barrier((w_z, a_two))
-    w_all = lax.all_to_all(
-        jnp.broadcast_to(w_z[None], (X, S, Q, 32, 2 * SIDE)), "row", 0, 0, tiled=True, axis_index_groups=x_groups()
-    )
-    a_pair = jnp.stack([a_two, lax.ppermute(a_two, "col", y_swap(1))])
-    a_mine = jnp.concatenate([a_pair, lax.ppermute(a_pair, "col", y_swap(2))])
+    w_s = [lax.ppermute(w_two, "row", s_shift(k)) for k in STEPS[1:]]
+    w_s[0], a_two = lax.optimization_barrier((w_s[0], a_two))
+    a_next = lax.ppermute(a_two, "col", y_swap(1))
+    w_wide = spread(0, [w_two] + w_s[:2], (), "spread_first")
+    w_s, w_wide, a_two, a_next = lax.optimization_barrier((w_s, w_wide, a_two, a_next))
+    w_wide = spread(S - 1, w_s[2:], (w_wide,), "spread_last")
+    w_all = lax.all_to_all(w_wide, "row", 0, 0, tiled=True, axis_index_groups=x_groups())
+    a_mine = jnp.stack([a_two, a_next] + [lax.ppermute(a_two, "col", y_swap(k)) for k in STEPS[2:]])
     a_other = lax.ppermute(a_mine, "col", core_swap())
     row_key, col_key, order = keys(place, occupied_irrep, virtual_irrep)
     lhs, paired0, send0 = pair_first(place, a_mine, a_other, w_all)
     get0 = lax.ppermute(send0, ("row", "col"), mirror_perm(0))
     paired1, send1 = pair_second(place, lhs, w_all)
     get1 = lax.ppermute(send1, ("row", "col"), mirror_perm(1))
-    done = finish(finish_first_kernel, SIDE, "finish_first", place, paired0, get0, row_key, col_key, order)
+    keep = (row_key, col_key, order)
+    done = finish(finish_first_kernel, SIDE, VMEM, [], "finish_first", place, paired0, get0, *keep)
+    last = [pltpu.VMEM((SIDE, SIDE), jnp.bfloat16), pltpu.SemaphoreType.DMA((len(PARTS) + 1,))]
     result = finish(
-        finish_second_kernel, 2 * SIDE, "finish_second", place, done, paired1, get1, row_key, col_key, order
+        finish_second_kernel, 2 * SIDE, HBM, last, "finish_second", place, done, paired1, get1, *keep
     )
     return result.reshape(OCC, WA, WB * OCC)
 

time: 98.7 us -> 95.9 us (0.972)
  the two profiles are of different devices: /device:TPU:129 before, /device:TPU:134 now
where the time goes in v4:
time: 95.9 us; the launch traced here: 95.4 us
  starting transfers between devices  55.6 us (58%)
  waiting for transfers between devices  27.9 us (29%)
  Pallas kernels  9.56 us (10%)
  local copies, waits for them, and re-layouts  1.88 us (2%)
    ppermute x1, waiting for transfers between devices, on_device(): get0 = lax.ppermute(send0, ('row', 'col'), mirror_perm(0))  17.7 us
    ppermute x1, starting transfers between devices, on_device(): a_far = lax.ppermute(a_own, 'col', h_swap())  14.5 us
    ppermute x3, starting transfers between devices, on_device(): w_s = [lax.ppermute(w_two, 'row', s_shift(k)) for k in STEPS[1:]]  9.56 us
    ppermute x2, starting transfers between devices, on_device(): lax.ppermute(a_two, 'col', y_swap(k))  7.45 us
    ppermute x1, starting transfers between devices, on_device(): get0 = lax.ppermute(send0, ('row', 'col'), mirror_perm(0))  6.63 us
    ppermute x2, waiting for transfers between devices, on_device(): lax.ppermute(a_two, 'col', y_swap(k))  5.47 us
    ppermute x1, starting transfers between devices, on_device(): get1 = lax.ppermute(send1, ('row', 'col'), mirror_perm(1))  5.36 us
    all_to_all x1, starting transfers between devices, on_device(): lax.all_to_all(w_wide, 'row', 0, 0, tiled=True, axis_index_groups=x_group...  4.78 us
  transfers between devices with their start and end apart: 12, of which 7 were waited for; matrix products, arithmetic and copies ran while one was open for 0% of the time, Pallas kernels for 5%

profile of v4, /device:TPU:134, one launch (start us, length us, event | category | flops | bytes accessed | tf_op | source)
XLA Modules:
  0.0 95.4 jit_solution(9066517641183337881)
XLA Ops:
  0.0 0.9 copy-done
  0.9 0.1 pack_w.1
  1.0 1.9 %collective-permute-start = (bf16[32,768]{1,0:T(8,128)(2,1)S(1)}, bf16[32,768]{1,0:T(8,128)(2,1)S(1)}, u32[]{:S(2)}, u32[]{:S(2)}) collective-permute-start(bf16[32,768]{1,0:T(8,128)(2,1)S(1)} %pack_w.1), channel_id=1, source_target_pairs={{0,256},{16,272},{32,288},{48,304},{64,320},{80,336},{96,352},{112... | collective-permute-start | bytes 147464 | tf_op jit(solution)/shard_map/ppermute | solution.py:337
  2.9 0.9 copy-done.1
  3.8 0.1 pack_a.1
  3.9 14.5 %collective-permute-start.2 = (bf16[192,128]{1,0:T(8,128)(2,1)S(1)}, bf16[192,128]{1,0:T(8,128)(2,1)S(1)}, u32[]{:S(2)}, u32[]{:S(2)}) collective-permute-start(bf16[192,128]{1,0:T(8,128)(2,1)S(1)} %pack_a.1), channel_id=1, source_target_pairs={{0,8},{1,9},{2,10},{3,11},{4,12},{5,13},{6,14},{7,15},{8,0},{9,1},... | collective-permute-start | bytes 147464 | tf_op jit(solution)/shard_map/ppermute | solution.py:336
  18.4 2.9 %collective-permute-start.1 = (bf16[2,32,768]{2,1,0:T(8,128)(2,1)S(1)}, bf16[2,32,768]{2,1,0:T(8,128)(2,1)S(1)}, u32[]{:S(2)}, u32[]{:S(2)}) collective-permute-start(bf16[2,32,768]{2,1,0:T(8,128)(2,1)S(1)} %pad_maximum_fusion.1.refs_0_), channel_id=1, source_target_pairs={{0,64},{16,80},{32,96},{48,112},{64,128},{80,144},{96,160},{112,17... | collective-permute-start | bytes 294920 | tf_op jit(solution)/shard_map/ppermute | solution.py:341
  21.3 4.7 %collective-permute-start.3 = (bf16[2,32,768]{2,1,0:T(8,128)(2,1)S(1)}, bf16[2,32,768]{2,1,0:T(8,128)(2,1)S(1)}, u32[]{:S(2)}, u32[]{:S(2)}) collective-permute-start(bf16[2,32,768]{2,1,0:T(8,128)(2,1)S(1)} %pad_maximum_fusion.1.refs_0_), channel_id=1, source_target_pairs={{0,192},{16,208},{32,224},{48,240},{64,0},{80,16},{96,32},{112,48}... | collective-permute-start | bytes 294920 | tf_op jit(solution)/shard_map/ppermute | solution.py:341
  26.1 1.9 %collective-permute-start.4 = (bf16[2,32,768]{2,1,0:T(8,128)(2,1)S(1)}, bf16[2,32,768]{2,1,0:T(8,128)(2,1)S(1)}, u32[]{:S(2)}, u32[]{:S(2)}) collective-permute-start(bf16[2,32,768]{2,1,0:T(8,128)(2,1)S(1)} %pad_maximum_fusion.1.refs_0_), channel_id=1, source_target_pairs={{0,128},{16,144},{32,160},{48,176},{64,192},{80,208},{96,224},{112... | collective-permute-start | bytes 294920 | tf_op jit(solution)/shard_map/ppermute | solution.py:341
  28.1 3.5 %collective-permute-start.5 = (bf16[2,192,128]{2,1,0:T(8,128)(2,1)S(1)}, bf16[2,192,128]{2,1,0:T(8,128)(2,1)S(1)}, u32[]{:S(2)}, u32[]{:S(2)}) collective-permute-start(bf16[2,192,128]{2,1,0:T(8,128)(2,1)S(1)} %pad_maximum_fusion.2), channel_id=1, source_target_pairs={{0,2},{1,3},{2,0},{3,1},{4,6},{5,7},{6,4},{7,5},{8,10},{9,11},{10,... | collective-permute-start | bytes 294920 | tf_op jit(solution)/shard_map/ppermute | solution.py:343
  31.6 1.2 %spread_first.1.refs_0_ = bf16[4,4,2,32,768]{4,3,2,1,0:T(8,128)(2,1)} custom-call(bf16[2,32,768]{2,1,0:T(8,128)(2,1)S(1)} %pad_maximum_fusion.1.refs_0_, bf16[2,32,768]{2,1,0:T(8,128)(2,1)S(1)} %collective-permute-done.1.refs_1_, bf16[2,32,768]{2,1,0:T(8,128)(2,1)S(1)} %collective-permute-done.3.refs_2_), custom_call_target="tpu_custom_call" | custom-call | tf_op jit(solution)/shard_map/spread_first/pallas_call | solution.py:120
  32.7 0.7 collective-permute-done.4.refs_1_
  33.5 1.1 %collective-permute-done.5 = bf16[2,192,128]{2,1,0:T(8,128)(2,1)S(1)} collective-permute-done((bf16[2,192,128]{2,1,0:T(8,128)(2,1)S(1)}, bf16[2,192,128]{2,1,0:T(8,128)(2,1)S(1)}, u32[]{:S(2)}, u32[]{:S(2)}) %collective-permute-start.5) | collective-permute-done | bytes 98336 | tf_op jit(solution)/shard_map/ppermute | solution.py:343
  34.6 0.8 spread_last.1
  35.4 4.8 %all-to-all-start = ((bf16[4,4,2,32,768]{4,3,2,1,0:T(8,128)(2,1)}), bf16[4,4,2,32,768]{4,3,2,1,0:T(8,128)(2,1)S(1)}, u32[]{:S(2)}, u32[]{:S(2)}) async-start(bf16[4,4,2,32,768]{4,3,2,1,0:T(8,128)(2,1)} %spread_last.1), calls=%async_computation | async-start | bytes 3145728 | tf_op jit(solution)/shard_map/all_to_all | solution.py:347
  40.2 4.9 %collective-permute-start.6 = (bf16[2,192,128]{2,1,0:T(8,128)(2,1)S(1)}, bf16[2,192,128]{2,1,0:T(8,128)(2,1)S(1)}, u32[]{:S(2)}, u32[]{:S(2)}) collective-permute-start(bf16[2,192,128]{2,1,0:T(8,128)(2,1)S(1)} %pad_maximum_fusion.2), channel_id=1, source_target_pairs={{0,6},{1,7},{2,4},{3,5},{4,2},{5,3},{6,0},{7,1},{8,14},{9,15},{10,... | collective-permute-start | bytes 294920 | tf_op jit(solution)/shard_map/ppermute | solution.py:348
  45.1 2.5 %collective-permute-start.7 = (bf16[2,192,128]{2,1,0:T(8,128)(2,1)S(1)}, bf16[2,192,128]{2,1,0:T(8,128)(2,1)S(1)}, u32[]{:S(2)}, u32[]{:S(2)}) collective-permute-start(bf16[2,192,128]{2,1,0:T(8,128)(2,1)S(1)} %pad_maximum_fusion.2), channel_id=1, source_target_pairs={{0,4},{1,5},{2,6},{3,7},{4,0},{5,1},{6,2},{7,3},{8,12},{9,13},{10,... | collective-permute-start | bytes 294920 | tf_op jit(solution)/shard_map/ppermute | solution.py:348
  47.6 0.3 collective-permute-done.6
  47.9 5.2 %collective-permute-done.7 = bf16[2,192,128]{2,1,0:T(8,128)(2,1)S(1)} collective-permute-done((bf16[2,192,128]{2,1,0:T(8,128)(2,1)S(1)}, bf16[2,192,128]{2,1,0:T(8,128)(2,1)S(1)}, u32[]{:S(2)}, u32[]{:S(2)}) %collective-permute-start.7) | collective-permute-done | bytes 98336 | tf_op jit(solution)/shard_map/ppermute | solution.py:348
  53.1 0.1 pad_maximum_fusion.own_ref
  53.2 1.9 %collective-permute-start.8 = (bf16[4,2,192,128]{3,2,1,0:T(8,128)(2,1)S(1)}, bf16[4,2,192,128]{3,2,1,0:T(8,128)(2,1)S(1)}, u32[]{:S(2)}, u32[]{:S(2)}) collective-permute-start(bf16[4,2,192,128]{3,2,1,0:T(8,128)(2,1)S(1)} %pad_maximum_fusion.own_ref), channel_id=1, source_target_pairs={{0,1},{1,0},{2,3},{3,2},{4,5},{5,4},{6,7},{7,6},{8,9},{9,8},{10,11... | collective-permute-start | bytes 1179656 | tf_op jit(solution)/shard_map/ppermute | solution.py:349
  55.2 0.1 stack.64.place_ref
  55.2 1.5 %collective-permute-done.8.far_ref = bf16[4,2,192,128]{3,2,1,0:T(8,128)(2,1)S(1)} collective-permute-done((bf16[4,2,192,128]{3,2,1,0:T(8,128)(2,1)S(1)}, bf16[4,2,192,128]{3,2,1,0:T(8,128)(2,1)S(1)}, u32[]{:S(2)}, u32[]{:S(2)}) %collective-permute-start.8) | collective-permute-done | bytes 393248 | tf_op jit(solution)/shard_map/ppermute | solution.py:349
  56.8 1.9 %pair_first.1 = (bf16[8,384,128]{2,1,0:T(8,128)(2,1)S(1)}, bf16[384,384]{1,0:T(8,128)(2,1)S(1)}, bf16[544,128]{1,0:T(8,128)(2,1)S(1)}) custom-call(s32[7]{0:T(128)S(1)} %stack.64.place_ref, bf16[4,2,192,128]{3,2,1,0:T(8,128)(2,1)S(1)} %pad_maximum_fusion.own_ref, bf16[4,2,192,128]{3,2,1,0:T(8,128)(2,1)S(1)} %collective-permute-done.8.far_ref, ...), custom_call_target="tpu_custom_call" | custom-call | tf_op jit(solution)/shard_map/pair_first/pallas_call | solution.py:228
  58.7 6.6 %collective-permute-start.9 = (bf16[544,128]{1,0:T(8,128)(2,1)S(1)}, bf16[544,128]{1,0:T(8,128)(2,1)S(1)}, u32[]{:S(2)}, u32[]{:S(2)}) collective-permute-start(bf16[544,128]{1,0:T(8,128)(2,1)S(1)} %get-tuple-element.26), channel_id=1, source_target_pairs={{0,0},{1,32},{2,64},{3,96},{4,128},{5,160},{6,192},{7,224},{8,256}... | collective-permute-start | bytes 417800 | tf_op jit(solution)/shard_map/ppermute | solution.py:352
  65.4 1.7 %pair_second.1 = (bf16[384,384]{1,0:T(8,128)(2,1)S(1)}, bf16[544,128]{1,0:T(8,128)(2,1)S(1)}) custom-call(s32[7]{0:T(128)S(1)} %stack.64.place_ref, bf16[8,384,128]{2,1,0:T(8,128)(2,1)S(1)} %get-tuple-element.30.lhs, bf16[4,4,2,32,768]{4,3,2,1,0:T(8,128)(2,1)S(1)} %all-to-all-done.w_ref), custom_call_target="tpu_custom_call" | custom-call | tf_op jit(solution)/shard_map/pair_second/pallas_call | solution.py:240
  67.1 5.4 %collective-permute-start.10 = (bf16[544,128]{1,0:T(8,128)(2,1)S(1)}, bf16[544,128]{1,0:T(8,128)(2,1)S(1)}, u32[]{:S(2)}, u32[]{:S(2)}) collective-permute-start(bf16[544,128]{1,0:T(8,128)(2,1)S(1)} %get-tuple-element.32), channel_id=1, source_target_pairs={{0,16},{1,48},{2,80},{3,112},{4,144},{5,176},{6,208},{7,240},{8,27... | collective-permute-start | bytes 417800 | tf_op jit(solution)/shard_map/ppermute | solution.py:354
  72.5 0.8 keys.1
  73.2 17.7 %collective-permute-done.9.get_ref = bf16[544,128]{1,0:T(8,128)(2,1)S(1)} collective-permute-done((bf16[544,128]{1,0:T(8,128)(2,1)S(1)}, bf16[544,128]{1,0:T(8,128)(2,1)S(1)}, u32[]{:S(2)}, u32[]{:S(2)}) %collective-permute-start.9) | collective-permute-done | bytes 139296 | tf_op jit(solution)/shard_map/ppermute | solution.py:352
  90.9 1.2 %finish_first.1.done_ref = bf16[384,384]{1,0:T(8,128)(2,1)S(1)} custom-call(s32[7]{0:T(128)S(1)} %stack.64.place_ref, bf16[384,384]{1,0:T(8,128)(2,1)S(1)} %get-tuple-element.25.paired_ref, bf16[544,128]{1,0:T(8,128)(2,1)S(1)} %collective-permute-done.9.get_ref, s32[384,128]{1,0:T(8,128)S(1)} %get-tuple-element.27.row_key, ...), custom_call_target="tpu_custom_call" | custom-call | tf_op jit(solution)/shard_map/finish_first/pallas_call | solution.py:320
  92.1 1.5 %collective-permute-done.10.get_ref = bf16[544,128]{1,0:T(8,128)(2,1)S(1)} collective-permute-done((bf16[544,128]{1,0:T(8,128)(2,1)S(1)}, bf16[544,128]{1,0:T(8,128)(2,1)S(1)}, u32[]{:S(2)}, u32[]{:S(2)}) %collective-permute-start.10) | collective-permute-done | bytes 139296 | tf_op jit(solution)/shard_map/ppermute | solution.py:354
  93.5 1.9 %finish_second.1 = bf16[384,768]{1,0:T(8,128)(2,1)} custom-call(s32[7]{0:T(128)S(1)} %stack.64.place_ref, bf16[384,384]{1,0:T(8,128)(2,1)S(1)} %finish_first.1.done_ref, bf16[384,384]{1,0:T(8,128)(2,1)S(1)} %get-tuple-element.31.paired_ref, bf16[544,128]{1,0:T(8,128)(2,1)S(1)} %collective-permute-done.10.get_ref, s32[384,128]{1,0:T(8,128)S(1)} %get-tuple-element.27.row_key, ...), custom_call_target="tpu_custom_call" | custom-call | tf_op jit(solution)/shard_map/finish_second/pallas_call | solution.py:320
  (14 shorter events, 0.1 us)
Async XLA Ops:
  0.0 0.9 copy-start
  1.0 17.4 %collective-permute-start = (bf16[32,768]{1,0:T(8,128)(2,1)S(1)}, bf16[32,768]{1,0:T(8,128)(2,1)S(1)}, u32[]{:S(2)}, u32[]{:S(2)}) collective-permute-start(bf16[32,768]{1,0:T(8,128)(2,1)S(1)} %pack_w.1), channel_id=1, source_target_pairs={{0,256},{16,272},{32,288},{48,304},{64,320},{80,336},{96,352},{112... | collective-permute-start | bytes 147464 | tf_op jit(solution)/shard_map/ppermute | solution.py:337
  2.9 0.9 copy-start.1
  3.9 24.1 %collective-permute-start.2 = (bf16[192,128]{1,0:T(8,128)(2,1)S(1)}, bf16[192,128]{1,0:T(8,128)(2,1)S(1)}, u32[]{:S(2)}, u32[]{:S(2)}) collective-permute-start(bf16[192,128]{1,0:T(8,128)(2,1)S(1)} %pack_a.1), channel_id=1, source_target_pairs={{0,8},{1,9},{2,10},{3,11},{4,12},{5,13},{6,14},{7,15},{8,0},{9,1},... | collective-permute-start | bytes 147464 | tf_op jit(solution)/shard_map/ppermute | solution.py:336
  18.4 9.6 %collective-permute-start.1 = (bf16[2,32,768]{2,1,0:T(8,128)(2,1)S(1)}, bf16[2,32,768]{2,1,0:T(8,128)(2,1)S(1)}, u32[]{:S(2)}, u32[]{:S(2)}) collective-permute-start(bf16[2,32,768]{2,1,0:T(8,128)(2,1)S(1)} %pad_maximum_fusion.1.refs_0_), channel_id=1, source_target_pairs={{0,64},{16,80},{32,96},{48,112},{64,128},{80,144},{96,160},{112,17... | collective-permute-start | bytes 294920 | tf_op jit(solution)/shard_map/ppermute | solution.py:341
  21.3 10.2 %collective-permute-start.3 = (bf16[2,32,768]{2,1,0:T(8,128)(2,1)S(1)}, bf16[2,32,768]{2,1,0:T(8,128)(2,1)S(1)}, u32[]{:S(2)}, u32[]{:S(2)}) collective-permute-start(bf16[2,32,768]{2,1,0:T(8,128)(2,1)S(1)} %pad_maximum_fusion.1.refs_0_), channel_id=1, source_target_pairs={{0,192},{16,208},{32,224},{48,240},{64,0},{80,16},{96,32},{112,48}... | collective-permute-start | bytes 294920 | tf_op jit(solution)/shard_map/ppermute | solution.py:341
  26.1 7.4 %collective-permute-start.4 = (bf16[2,32,768]{2,1,0:T(8,128)(2,1)S(1)}, bf16[2,32,768]{2,1,0:T(8,128)(2,1)S(1)}, u32[]{:S(2)}, u32[]{:S(2)}) collective-permute-start(bf16[2,32,768]{2,1,0:T(8,128)(2,1)S(1)} %pad_maximum_fusion.1.refs_0_), channel_id=1, source_target_pairs={{0,128},{16,144},{32,160},{48,176},{64,192},{80,208},{96,224},{112... | collective-permute-start | bytes 294920 | tf_op jit(solution)/shard_map/ppermute | solution.py:341
  28.1 6.5 %collective-permute-start.5 = (bf16[2,192,128]{2,1,0:T(8,128)(2,1)S(1)}, bf16[2,192,128]{2,1,0:T(8,128)(2,1)S(1)}, u32[]{:S(2)}, u32[]{:S(2)}) collective-permute-start(bf16[2,192,128]{2,1,0:T(8,128)(2,1)S(1)} %pad_maximum_fusion.2), channel_id=1, source_target_pairs={{0,2},{1,3},{2,0},{3,1},{4,6},{5,7},{6,4},{7,5},{8,10},{9,11},{10,... | collective-permute-start | bytes 294920 | tf_op jit(solution)/shard_map/ppermute | solution.py:343
  35.4 21.4 %all-to-all-start = ((bf16[4,4,2,32,768]{4,3,2,1,0:T(8,128)(2,1)}), bf16[4,4,2,32,768]{4,3,2,1,0:T(8,128)(2,1)S(1)}, u32[]{:S(2)}, u32[]{:S(2)}) async-start(bf16[4,4,2,32,768]{4,3,2,1,0:T(8,128)(2,1)} %spread_last.1), calls=%async_computation | async-start | bytes 3145728 | tf_op jit(solution)/shard_map/all_to_all | solution.py:347
  40.2 7.7 %collective-permute-start.6 = (bf16[2,192,128]{2,1,0:T(8,128)(2,1)S(1)}, bf16[2,192,128]{2,1,0:T(8,128)(2,1)S(1)}, u32[]{:S(2)}, u32[]{:S(2)}) collective-permute-start(bf16[2,192,128]{2,1,0:T(8,128)(2,1)S(1)} %pad_maximum_fusion.2), channel_id=1, source_target_pairs={{0,6},{1,7},{2,4},{3,5},{4,2},{5,3},{6,0},{7,1},{8,14},{9,15},{10,... | collective-permute-start | bytes 294920 | tf_op jit(solution)/shard_map/ppermute | solution.py:348
  45.1 8.0 %collective-permute-start.7 = (bf16[2,192,128]{2,1,0:T(8,128)(2,1)S(1)}, bf16[2,192,128]{2,1,0:T(8,128)(2,1)S(1)}, u32[]{:S(2)}, u32[]{:S(2)}) collective-permute-start(bf16[2,192,128]{2,1,0:T(8,128)(2,1)S(1)} %pad_maximum_fusion.2), channel_id=1, source_target_pairs={{0,4},{1,5},{2,6},{3,7},{4,0},{5,1},{6,2},{7,3},{8,12},{9,13},{10,... | collective-permute-start | bytes 294920 | tf_op jit(solution)/shard_map/ppermute | solution.py:348
  53.2 3.6 %collective-permute-start.8 = (bf16[4,2,192,128]{3,2,1,0:T(8,128)(2,1)S(1)}, bf16[4,2,192,128]{3,2,1,0:T(8,128)(2,1)S(1)}, u32[]{:S(2)}, u32[]{:S(2)}) collective-permute-start(bf16[4,2,192,128]{3,2,1,0:T(8,128)(2,1)S(1)} %pad_maximum_fusion.own_ref), channel_id=1, source_target_pairs={{0,1},{1,0},{2,3},{3,2},{4,5},{5,4},{6,7},{7,6},{8,9},{9,8},{10,11... | collective-permute-start | bytes 1179656 | tf_op jit(solution)/shard_map/ppermute | solution.py:349
  58.7 13.7 %copy-start.2 = (s32[1024]{0:T(1024)S(1)}, s32[1024]{0:T(1024)}, u32[]{:S(2)}) copy-start(s32[1024]{0:T(1024)} %param.7) | copy-start | bytes 12292
  58.7 13.7 %copy-start.3 = (s32[12]{0:T(128)S(1)}, s32[12]{0:T(128)}, u32[]{:S(2)}) copy-start(s32[12]{0:T(128)} %occ_ref.1) | copy-start | bytes 148
  58.7 32.1 %collective-permute-start.9 = (bf16[544,128]{1,0:T(8,128)(2,1)S(1)}, bf16[544,128]{1,0:T(8,128)(2,1)S(1)}, u32[]{:S(2)}, u32[]{:S(2)}) collective-permute-start(bf16[544,128]{1,0:T(8,128)(2,1)S(1)} %get-tuple-element.26), channel_id=1, source_target_pairs={{0,0},{1,32},{2,64},{3,96},{4,128},{5,160},{6,192},{7,224},{8,256}... | collective-permute-start | bytes 417800 | tf_op jit(solution)/shard_map/ppermute | solution.py:352
  67.1 26.4 %collective-permute-start.10 = (bf16[544,128]{1,0:T(8,128)(2,1)S(1)}, bf16[544,128]{1,0:T(8,128)(2,1)S(1)}, u32[]{:S(2)}, u32[]{:S(2)}) collective-permute-start(bf16[544,128]{1,0:T(8,128)(2,1)S(1)} %get-tuple-element.32), channel_id=1, source_target_pairs={{0,16},{1,48},{2,80},{3,112},{4,144},{5,176},{6,208},{7,240},{8,27... | collective-permute-start | bytes 417800 | tf_op jit(solution)/shard_map/ppermute | solution.py:354

commit v5 on v4

--- a/solution.py
+++ b/solution.py
@@ -14,7 +14,7 @@
 HALF = 32
 GROUPS = OCC // 4
 SIDE = OCC * 32
-TILES = 17
+SENT = 16 * 32 + 16
 STEPS = (0, 1, 3, 2)
 PARTS = [slice(r, r + 96) for r in range(0, SIDE, 96)]
 VMEM = pl.BlockSpec(memory_space=pltpu.VMEM)
@@ -197,9 +197,11 @@
     for q in range(GROUPS):
         out.append(jnp.where(slot == 0, pltpu.roll(tile(4 * q + 2, q), HALF, 1), tile(4 * q, q)))
     out.append(jnp.where(slot < 2, pltpu.roll(tile(5, 1), 2 * HALF, 1), tile(1, 0)))
-    out.append(tile(9, 2))
     for t, value in enumerate(out):
         send_ref[32 * t : 32 * t + 32, :] = value.astype(jnp.bfloat16)
+    rest = tile(9, 2)
+    rest = jnp.where(slot[:16] < 2, pltpu.roll(rest[16:], 2 * HALF, 1), rest[:16])
+    send_ref[SENT - 16 :, :] = rest.astype(jnp.bfloat16)
 
 
 def first_kernel(place_ref, own_ref, far_ref, w_ref, lhs, paired_ref, send_ref, prod, turned):
@@ -227,7 +229,7 @@
 def pair_first(place, a_mine, a_other, w_all):
     return pl.pallas_call(
         first_kernel,
-        out_shape=(bf16(Q * S, SIDE, 128), bf16(SIDE, SIDE), bf16(TILES * 32, 128)),
+        out_shape=(bf16(Q * S, SIDE, 128), bf16(SIDE, SIDE), bf16(SENT, 128)),
         in_specs=[SMEM, VMEM, VMEM, VMEM],
         out_specs=(VMEM, VMEM, VMEM),
         scratch_shapes=WORK,
@@ -239,7 +241,7 @@
 def pair_second(place, lhs, w_all):
     return pl.pallas_call(
         second_kernel,
-        out_shape=(bf16(SIDE, SIDE), bf16(TILES * 32, 128)),
+        out_shape=(bf16(SIDE, SIDE), bf16(SENT, 128)),
         in_specs=[SMEM, VMEM, VMEM],
         out_specs=(VMEM, VMEM),
         scratch_shapes=WORK,
@@ -263,7 +265,8 @@
 
     for t, (i, g) in enumerate(full_tiles()):
         put(i, g, got(t), -1)
-    last = [got(15), got(16)]
+    rest = get_ref[SENT - 16 :, :].astype(jnp.float32)
+    last = [got(15), jnp.concatenate([rest, pltpu.roll(rest, 2 * HALF, 1)], axis=0)]
     for q in range(GROUPS):
         piece = got(12 + q)
         put(4 * q, q, piece, 0)

time: 95.9 us -> 95.1 us (level)
  the two profiles are of different devices: /device:TPU:134 before, /device:TPU:129 now
where the time goes in v5:
time: 95.1 us; the launch traced here: 94.6 us
  starting transfers between devices  58.7 us (62%)
  waiting for transfers between devices  24.1 us (25%)
  Pallas kernels  9.57 us (10%)
  local copies, waits for them, and re-layouts  1.88 us (2%)
    ppermute x1, waiting for transfers between devices, on_device(): get0 = lax.ppermute(send0, ('row', 'col'), mirror_perm(0))  16.1 us
    ppermute x1, starting transfers between devices, on_device(): a_far = lax.ppermute(a_own, 'col', h_swap())  13.9 us
    ppermute x3, starting transfers between devices, on_device(): w_s = [lax.ppermute(w_two, 'row', s_shift(k)) for k in STEPS[1:]]  9 us
    ppermute x1, starting transfers between devices, on_device(): get0 = lax.ppermute(send0, ('row', 'col'), mirror_perm(0))  8.94 us
    ppermute x2, starting transfers between devices, on_device(): lax.ppermute(a_two, 'col', y_swap(k))  6.89 us
    ppermute x1, starting transfers between devices, on_device(): a_other = lax.ppermute(a_mine, 'col', core_swap())  6.56 us
    ppermute x2, waiting for transfers between devices, on_device(): lax.ppermute(a_two, 'col', y_swap(k))  4.59 us
    ppermute x1, starting transfers between devices, on_device(): get1 = lax.ppermute(send1, ('row', 'col'), mirror_perm(1))  4.24 us
  transfers between devices with their start and end apart: 12, of which 5 were waited for; matrix products, arithmetic and copies ran while one was open for 0% of the time, Pallas kernels for 5%

profile of v5, /device:TPU:129, one launch (start us, length us, event | category | flops | bytes accessed | tf_op | source)
XLA Modules:
  0.0 94.6 jit_solution(16522446320016740306)
XLA Ops:
  0.0 0.9 copy-done
  0.9 0.1 pack_w.1
  1.0 1.9 %collective-permute-start = (bf16[32,768]{1,0:T(8,128)(2,1)S(1)}, bf16[32,768]{1,0:T(8,128)(2,1)S(1)}, u32[]{:S(2)}, u32[]{:S(2)}) collective-permute-start(bf16[32,768]{1,0:T(8,128)(2,1)S(1)} %pack_w.1), channel_id=1, source_target_pairs={{0,256},{16,272},{32,288},{48,304},{64,320},{80,336},{96,352},{112... | collective-permute-start | bytes 147464 | tf_op jit(solution)/shard_map/ppermute | solution.py:340
  2.9 0.9 copy-done.1
  3.8 0.1 pack_a.1
  3.9 13.9 %collective-permute-start.2 = (bf16[192,128]{1,0:T(8,128)(2,1)S(1)}, bf16[192,128]{1,0:T(8,128)(2,1)S(1)}, u32[]{:S(2)}, u32[]{:S(2)}) collective-permute-start(bf16[192,128]{1,0:T(8,128)(2,1)S(1)} %pack_a.1), channel_id=1, source_target_pairs={{0,8},{1,9},{2,10},{3,11},{4,12},{5,13},{6,14},{7,15},{8,0},{9,1},... | collective-permute-start | bytes 147464 | tf_op jit(solution)/shard_map/ppermute | solution.py:339
  17.9 2.6 %collective-permute-start.1 = (bf16[2,32,768]{2,1,0:T(8,128)(2,1)S(1)}, bf16[2,32,768]{2,1,0:T(8,128)(2,1)S(1)}, u32[]{:S(2)}, u32[]{:S(2)}) collective-permute-start(bf16[2,32,768]{2,1,0:T(8,128)(2,1)S(1)} %pad_maximum_fusion.1.refs_0_), channel_id=1, source_target_pairs={{0,64},{16,80},{32,96},{48,112},{64,128},{80,144},{96,160},{112,17... | collective-permute-start | bytes 294920 | tf_op jit(solution)/shard_map/ppermute | solution.py:344
  20.5 4.4 %collective-permute-start.3 = (bf16[2,32,768]{2,1,0:T(8,128)(2,1)S(1)}, bf16[2,32,768]{2,1,0:T(8,128)(2,1)S(1)}, u32[]{:S(2)}, u32[]{:S(2)}) collective-permute-start(bf16[2,32,768]{2,1,0:T(8,128)(2,1)S(1)} %pad_maximum_fusion.1.refs_0_), channel_id=1, source_target_pairs={{0,192},{16,208},{32,224},{48,240},{64,0},{80,16},{96,32},{112,48}... | collective-permute-start | bytes 294920 | tf_op jit(solution)/shard_map/ppermute | solution.py:344
  25.0 1.9 %collective-permute-start.4 = (bf16[2,32,768]{2,1,0:T(8,128)(2,1)S(1)}, bf16[2,32,768]{2,1,0:T(8,128)(2,1)S(1)}, u32[]{:S(2)}, u32[]{:S(2)}) collective-permute-start(bf16[2,32,768]{2,1,0:T(8,128)(2,1)S(1)} %pad_maximum_fusion.1.refs_0_), channel_id=1, source_target_pairs={{0,128},{16,144},{32,160},{48,176},{64,192},{80,208},{96,224},{112... | collective-permute-start | bytes 294920 | tf_op jit(solution)/shard_map/ppermute | solution.py:344
  26.9 3.2 %collective-permute-start.5 = (bf16[2,192,128]{2,1,0:T(8,128)(2,1)S(1)}, bf16[2,192,128]{2,1,0:T(8,128)(2,1)S(1)}, u32[]{:S(2)}, u32[]{:S(2)}) collective-permute-start(bf16[2,192,128]{2,1,0:T(8,128)(2,1)S(1)} %pad_maximum_fusion.2), channel_id=1, source_target_pairs={{0,2},{1,3},{2,0},{3,1},{4,6},{5,7},{6,4},{7,5},{8,10},{9,11},{10,... | collective-permute-start | bytes 294920 | tf_op jit(solution)/shard_map/ppermute | solution.py:346
  30.2 1.2 %spread_first.1.refs_0_ = bf16[4,4,2,32,768]{4,3,2,1,0:T(8,128)(2,1)} custom-call(bf16[2,32,768]{2,1,0:T(8,128)(2,1)S(1)} %pad_maximum_fusion.1.refs_0_, bf16[2,32,768]{2,1,0:T(8,128)(2,1)S(1)} %collective-permute-done.1.refs_1_, bf16[2,32,768]{2,1,0:T(8,128)(2,1)S(1)} %collective-permute-done.3.refs_2_), custom_call_target="tpu_custom_call" | custom-call | tf_op jit(solution)/shard_map/spread_first/pallas_call | solution.py:120
  31.3 0.9 collective-permute-done.4.refs_1_
  32.3 0.0 collective-permute-done.5
  32.3 0.8 spread_last.1
  33.1 4.0 %all-to-all-start = ((bf16[4,4,2,32,768]{4,3,2,1,0:T(8,128)(2,1)}), bf16[4,4,2,32,768]{4,3,2,1,0:T(8,128)(2,1)S(1)}, u32[]{:S(2)}, u32[]{:S(2)}) async-start(bf16[4,4,2,32,768]{4,3,2,1,0:T(8,128)(2,1)} %spread_last.1), calls=%async_computation | async-start | bytes 3145728 | tf_op jit(solution)/shard_map/all_to_all | solution.py:350
  37.1 4.6 %collective-permute-start.6 = (bf16[2,192,128]{2,1,0:T(8,128)(2,1)S(1)}, bf16[2,192,128]{2,1,0:T(8,128)(2,1)S(1)}, u32[]{:S(2)}, u32[]{:S(2)}) collective-permute-start(bf16[2,192,128]{2,1,0:T(8,128)(2,1)S(1)} %pad_maximum_fusion.2), channel_id=1, source_target_pairs={{0,6},{1,7},{2,4},{3,5},{4,2},{5,3},{6,0},{7,1},{8,14},{9,15},{10,... | collective-permute-start | bytes 294920 | tf_op jit(solution)/shard_map/ppermute | solution.py:351
  41.8 2.3 %collective-permute-start.7 = (bf16[2,192,128]{2,1,0:T(8,128)(2,1)S(1)}, bf16[2,192,128]{2,1,0:T(8,128)(2,1)S(1)}, u32[]{:S(2)}, u32[]{:S(2)}) collective-permute-start(bf16[2,192,128]{2,1,0:T(8,128)(2,1)S(1)} %pad_maximum_fusion.2), channel_id=1, source_target_pairs={{0,4},{1,5},{2,6},{3,7},{4,0},{5,1},{6,2},{7,3},{8,12},{9,13},{10,... | collective-permute-start | bytes 294920 | tf_op jit(solution)/shard_map/ppermute | solution.py:351
  44.1 4.6 %collective-permute-done.7 = bf16[2,192,128]{2,1,0:T(8,128)(2,1)S(1)} collective-permute-done((bf16[2,192,128]{2,1,0:T(8,128)(2,1)S(1)}, bf16[2,192,128]{2,1,0:T(8,128)(2,1)S(1)}, u32[]{:S(2)}, u32[]{:S(2)}) %collective-permute-start.7) | collective-permute-done | bytes 98336 | tf_op jit(solution)/shard_map/ppermute | solution.py:351
  48.6 0.1 pad_maximum_fusion.own_ref
  48.7 6.6 %collective-permute-start.8 = (bf16[4,2,192,128]{3,2,1,0:T(8,128)(2,1)S(1)}, bf16[4,2,192,128]{3,2,1,0:T(8,128)(2,1)S(1)}, u32[]{:S(2)}, u32[]{:S(2)}) collective-permute-start(bf16[4,2,192,128]{3,2,1,0:T(8,128)(2,1)S(1)} %pad_maximum_fusion.own_ref), channel_id=1, source_target_pairs={{0,1},{1,0},{2,3},{3,2},{4,5},{5,4},{6,7},{7,6},{8,9},{9,8},{10,11... | collective-permute-start | bytes 1179656 | tf_op jit(solution)/shard_map/ppermute | solution.py:352
  55.3 0.1 stack.64.place_ref
  55.4 1.2 %collective-permute-done.8.far_ref = bf16[4,2,192,128]{3,2,1,0:T(8,128)(2,1)S(1)} collective-permute-done((bf16[4,2,192,128]{3,2,1,0:T(8,128)(2,1)S(1)}, bf16[4,2,192,128]{3,2,1,0:T(8,128)(2,1)S(1)}, u32[]{:S(2)}, u32[]{:S(2)}) %collective-permute-start.8) | collective-permute-done | bytes 393248 | tf_op jit(solution)/shard_map/ppermute | solution.py:352
  56.6 1.9 %pair_first.1 = (bf16[8,384,128]{2,1,0:T(8,128)(2,1)S(1)}, bf16[384,384]{1,0:T(8,128)(2,1)S(1)}, bf16[528,128]{1,0:T(8,128)(2,1)S(1)}) custom-call(s32[7]{0:T(128)S(1)} %stack.64.place_ref, bf16[4,2,192,128]{3,2,1,0:T(8,128)(2,1)S(1)} %pad_maximum_fusion.own_ref, bf16[4,2,192,128]{3,2,1,0:T(8,128)(2,1)S(1)} %collective-permute-done.8.far_ref, ...), custom_call_target="tpu_custom_call" | custom-call | tf_op jit(solution)/shard_map/pair_first/pallas_call | solution.py:230
  58.5 0.0 copy-start.2
  58.6 8.9 %collective-permute-start.9 = (bf16[528,128]{1,0:T(8,128)(2,1)S(1)}, bf16[528,128]{1,0:T(8,128)(2,1)S(1)}, u32[]{:S(2)}, u32[]{:S(2)}) collective-permute-start(bf16[528,128]{1,0:T(8,128)(2,1)S(1)} %get-tuple-element.26), channel_id=1, source_target_pairs={{0,0},{1,32},{2,64},{3,96},{4,128},{5,160},{6,192},{7,224},{8,256}... | collective-permute-start | bytes 405512 | tf_op jit(solution)/shard_map/ppermute | solution.py:355
  67.5 1.7 %pair_second.1 = (bf16[384,384]{1,0:T(8,128)(2,1)S(1)}, bf16[528,128]{1,0:T(8,128)(2,1)S(1)}) custom-call(s32[7]{0:T(128)S(1)} %stack.64.place_ref, bf16[8,384,128]{2,1,0:T(8,128)(2,1)S(1)} %get-tuple-element.30.lhs, bf16[4,4,2,32,768]{4,3,2,1,0:T(8,128)(2,1)S(1)} %all-to-all-done.w_ref), custom_call_target="tpu_custom_call" | custom-call | tf_op jit(solution)/shard_map/pair_second/pallas_call | solution.py:242
  69.2 4.2 %collective-permute-start.10 = (bf16[528,128]{1,0:T(8,128)(2,1)S(1)}, bf16[528,128]{1,0:T(8,128)(2,1)S(1)}, u32[]{:S(2)}, u32[]{:S(2)}) collective-permute-start(bf16[528,128]{1,0:T(8,128)(2,1)S(1)} %get-tuple-element.32), channel_id=1, source_target_pairs={{0,16},{1,48},{2,80},{3,112},{4,144},{5,176},{6,208},{7,240},{8,27... | collective-permute-start | bytes 405512 | tf_op jit(solution)/shard_map/ppermute | solution.py:357
  73.5 0.8 keys.1
  74.2 16.1 %collective-permute-done.9.get_ref = bf16[528,128]{1,0:T(8,128)(2,1)S(1)} collective-permute-done((bf16[528,128]{1,0:T(8,128)(2,1)S(1)}, bf16[528,128]{1,0:T(8,128)(2,1)S(1)}, u32[]{:S(2)}, u32[]{:S(2)}) %collective-permute-start.9) | collective-permute-done | bytes 135200 | tf_op jit(solution)/shard_map/ppermute | solution.py:355
  90.3 1.2 %finish_first.1.done_ref = bf16[384,384]{1,0:T(8,128)(2,1)S(1)} custom-call(s32[7]{0:T(128)S(1)} %stack.64.place_ref, bf16[384,384]{1,0:T(8,128)(2,1)S(1)} %get-tuple-element.25.paired_ref, bf16[528,128]{1,0:T(8,128)(2,1)S(1)} %collective-permute-done.9.get_ref, s32[384,128]{1,0:T(8,128)S(1)} %get-tuple-element.27.row_key, ...), custom_call_target="tpu_custom_call" | custom-call | tf_op jit(solution)/shard_map/finish_first/pallas_call | solution.py:323
  91.5 1.3 %collective-permute-done.10.get_ref = bf16[528,128]{1,0:T(8,128)(2,1)S(1)} collective-permute-done((bf16[528,128]{1,0:T(8,128)(2,1)S(1)}, bf16[528,128]{1,0:T(8,128)(2,1)S(1)}, u32[]{:S(2)}, u32[]{:S(2)}) %collective-permute-start.10) | collective-permute-done | bytes 135200 | tf_op jit(solution)/shard_map/ppermute | solution.py:357
  92.7 1.9 %finish_second.1 = bf16[384,768]{1,0:T(8,128)(2,1)} custom-call(s32[7]{0:T(128)S(1)} %stack.64.place_ref, bf16[384,384]{1,0:T(8,128)(2,1)S(1)} %finish_first.1.done_ref, bf16[384,384]{1,0:T(8,128)(2,1)S(1)} %get-tuple-element.31.paired_ref, bf16[528,128]{1,0:T(8,128)(2,1)S(1)} %collective-permute-done.10.get_ref, s32[384,128]{1,0:T(8,128)S(1)} %get-tuple-element.27.row_key, ...), custom_call_target="tpu_custom_call" | custom-call | tf_op jit(solution)/shard_map/finish_second/pallas_call | solution.py:323
  (14 shorter events, 0.1 us)
Async XLA Ops:
  0.0 0.9 copy-start
  1.0 16.8 %collective-permute-start = (bf16[32,768]{1,0:T(8,128)(2,1)S(1)}, bf16[32,768]{1,0:T(8,128)(2,1)S(1)}, u32[]{:S(2)}, u32[]{:S(2)}) collective-permute-start(bf16[32,768]{1,0:T(8,128)(2,1)S(1)} %pack_w.1), channel_id=1, source_target_pairs={{0,256},{16,272},{32,288},{48,304},{64,320},{80,336},{96,352},{112... | collective-permute-start | bytes 147464 | tf_op jit(solution)/shard_map/ppermute | solution.py:340
  2.9 0.9 copy-start.1
  3.9 23.0 %collective-permute-start.2 = (bf16[192,128]{1,0:T(8,128)(2,1)S(1)}, bf16[192,128]{1,0:T(8,128)(2,1)S(1)}, u32[]{:S(2)}, u32[]{:S(2)}) collective-permute-start(bf16[192,128]{1,0:T(8,128)(2,1)S(1)} %pack_a.1), channel_id=1, source_target_pairs={{0,8},{1,9},{2,10},{3,11},{4,12},{5,13},{6,14},{7,15},{8,0},{9,1},... | collective-permute-start | bytes 147464 | tf_op jit(solution)/shard_map/ppermute | solution.py:339
  17.9 9.1 %collective-permute-start.1 = (bf16[2,32,768]{2,1,0:T(8,128)(2,1)S(1)}, bf16[2,32,768]{2,1,0:T(8,128)(2,1)S(1)}, u32[]{:S(2)}, u32[]{:S(2)}) collective-permute-start(bf16[2,32,768]{2,1,0:T(8,128)(2,1)S(1)} %pad_maximum_fusion.1.refs_0_), channel_id=1, source_target_pairs={{0,64},{16,80},{32,96},{48,112},{64,128},{80,144},{96,160},{112,17... | collective-permute-start | bytes 294920 | tf_op jit(solution)/shard_map/ppermute | solution.py:344
  20.5 9.6 %collective-permute-start.3 = (bf16[2,32,768]{2,1,0:T(8,128)(2,1)S(1)}, bf16[2,32,768]{2,1,0:T(8,128)(2,1)S(1)}, u32[]{:S(2)}, u32[]{:S(2)}) collective-permute-start(bf16[2,32,768]{2,1,0:T(8,128)(2,1)S(1)} %pad_maximum_fusion.1.refs_0_), channel_id=1, source_target_pairs={{0,192},{16,208},{32,224},{48,240},{64,0},{80,16},{96,32},{112,48}... | collective-permute-start | bytes 294920 | tf_op jit(solution)/shard_map/ppermute | solution.py:344
  25.0 7.3 %collective-permute-start.4 = (bf16[2,32,768]{2,1,0:T(8,128)(2,1)S(1)}, bf16[2,32,768]{2,1,0:T(8,128)(2,1)S(1)}, u32[]{:S(2)}, u32[]{:S(2)}) collective-permute-start(bf16[2,32,768]{2,1,0:T(8,128)(2,1)S(1)} %pad_maximum_fusion.1.refs_0_), channel_id=1, source_target_pairs={{0,128},{16,144},{32,160},{48,176},{64,192},{80,208},{96,224},{112... | collective-permute-start | bytes 294920 | tf_op jit(solution)/shard_map/ppermute | solution.py:344
  26.9 5.4 %collective-permute-start.5 = (bf16[2,192,128]{2,1,0:T(8,128)(2,1)S(1)}, bf16[2,192,128]{2,1,0:T(8,128)(2,1)S(1)}, u32[]{:S(2)}, u32[]{:S(2)}) collective-permute-start(bf16[2,192,128]{2,1,0:T(8,128)(2,1)S(1)} %pad_maximum_fusion.2), channel_id=1, source_target_pairs={{0,2},{1,3},{2,0},{3,1},{4,6},{5,7},{6,4},{7,5},{8,10},{9,11},{10,... | collective-permute-start | bytes 294920 | tf_op jit(solution)/shard_map/ppermute | solution.py:346
  33.1 23.5 %all-to-all-start = ((bf16[4,4,2,32,768]{4,3,2,1,0:T(8,128)(2,1)}), bf16[4,4,2,32,768]{4,3,2,1,0:T(8,128)(2,1)S(1)}, u32[]{:S(2)}, u32[]{:S(2)}) async-start(bf16[4,4,2,32,768]{4,3,2,1,0:T(8,128)(2,1)} %spread_last.1), calls=%async_computation | async-start | bytes 3145728 | tf_op jit(solution)/shard_map/all_to_all | solution.py:350
  37.1 6.9 %collective-permute-start.6 = (bf16[2,192,128]{2,1,0:T(8,128)(2,1)S(1)}, bf16[2,192,128]{2,1,0:T(8,128)(2,1)S(1)}, u32[]{:S(2)}, u32[]{:S(2)}) collective-permute-start(bf16[2,192,128]{2,1,0:T(8,128)(2,1)S(1)} %pad_maximum_fusion.2), channel_id=1, source_target_pairs={{0,6},{1,7},{2,4},{3,5},{4,2},{5,3},{6,0},{7,1},{8,14},{9,15},{10,... | collective-permute-start | bytes 294920 | tf_op jit(solution)/shard_map/ppermute | solution.py:351
  41.8 6.9 %collective-permute-start.7 = (bf16[2,192,128]{2,1,0:T(8,128)(2,1)S(1)}, bf16[2,192,128]{2,1,0:T(8,128)(2,1)S(1)}, u32[]{:S(2)}, u32[]{:S(2)}) collective-permute-start(bf16[2,192,128]{2,1,0:T(8,128)(2,1)S(1)} %pad_maximum_fusion.2), channel_id=1, source_target_pairs={{0,4},{1,5},{2,6},{3,7},{4,0},{5,1},{6,2},{7,3},{8,12},{9,13},{10,... | collective-permute-start | bytes 294920 | tf_op jit(solution)/shard_map/ppermute | solution.py:351
  48.7 7.9 %collective-permute-start.8 = (bf16[4,2,192,128]{3,2,1,0:T(8,128)(2,1)S(1)}, bf16[4,2,192,128]{3,2,1,0:T(8,128)(2,1)S(1)}, u32[]{:S(2)}, u32[]{:S(2)}) collective-permute-start(bf16[4,2,192,128]{3,2,1,0:T(8,128)(2,1)S(1)} %pad_maximum_fusion.own_ref), channel_id=1, source_target_pairs={{0,1},{1,0},{2,3},{3,2},{4,5},{5,4},{6,7},{7,6},{8,9},{9,8},{10,11... | collective-permute-start | bytes 1179656 | tf_op jit(solution)/shard_map/ppermute | solution.py:352
  58.5 14.9 %copy-start.2 = (s32[1024]{0:T(1024)S(1)}, s32[1024]{0:T(1024)}, u32[]{:S(2)}) copy-start(s32[1024]{0:T(1024)} %param.7) | copy-start | bytes 12292
  58.5 14.9 %copy-start.3 = (s32[12]{0:T(128)S(1)}, s32[12]{0:T(128)}, u32[]{:S(2)}) copy-start(s32[12]{0:T(128)} %occ_ref.1) | copy-start | bytes 148
  58.6 31.7 %collective-permute-start.9 = (bf16[528,128]{1,0:T(8,128)(2,1)S(1)}, bf16[528,128]{1,0:T(8,128)(2,1)S(1)}, u32[]{:S(2)}, u32[]{:S(2)}) collective-permute-start(bf16[528,128]{1,0:T(8,128)(2,1)S(1)} %get-tuple-element.26), channel_id=1, source_target_pairs={{0,0},{1,32},{2,64},{3,96},{4,128},{5,160},{6,192},{7,224},{8,256}... | collective-permute-start | bytes 405512 | tf_op jit(solution)/shard_map/ppermute | solution.py:355
  69.2 23.6 %collective-permute-start.10 = (bf16[528,128]{1,0:T(8,128)(2,1)S(1)}, bf16[528,128]{1,0:T(8,128)(2,1)S(1)}, u32[]{:S(2)}, u32[]{:S(2)}) collective-permute-start(bf16[528,128]{1,0:T(8,128)(2,1)S(1)} %get-tuple-element.32), channel_id=1, source_target_pairs={{0,16},{1,48},{2,80},{3,112},{4,144},{5,176},{6,208},{7,240},{8,27... | collective-permute-start | bytes 405512 | tf_op jit(solution)/shard_map/ppermute | solution.py:357

commit v6 on v5

--- a/solution.py
+++ b/solution.py
@@ -187,7 +187,10 @@
             paired_ref[32 * i : 32 * i + 32, 128 * g : 128 * g + 128] = (
                 load(i, g) - crossed(load, i, g)
             ).astype(jnp.bfloat16)
-    turned[...] = paired_ref[...].astype(jnp.float32).T
+    for block in range(GROUPS):
+        for g in range(block + 1):
+            down, across = slice(128 * block, 128 * block + 128), slice(128 * g, 128 * g + 128)
+            turned[across, down] = paired_ref[down, across].astype(jnp.float32).T
 
     def tile(i, group):
         return turned[32 * i : 32 * i + 32, 128 * group : 128 * group + 128]
@@ -207,7 +210,7 @@
 def first_kernel(place_ref, own_ref, far_ref, w_ref, lhs, paired_ref, send_ref, prod, turned):
     core, y, q_own, s_own = place_ref[1], place_ref[2], place_ref[3], place_ref[4]
     for step in range(Y):
-        shift = lax.rem(s_own + S - jnp.bitwise_xor(y, STEPS[step]), S)
+        shift = lax.rem(s_own + S - jnp.bitwise_xor(y, step), S)
         k = jnp.bitwise_xor(shift, shift // 2)
         for h in range(H):
             mine, other = own_ref[step, h], far_ref[step, h]
@@ -278,20 +281,20 @@
         return upper[32 * j : 32 * j + 32, 128 * group : 128 * group + 128]
 
     col = jnp.where(half == 0, col_key[0:1, :], col_key[1:2, :])
-    for i in range(OCC):
-        rows = slice(32 * i, 32 * i + 32)
-        for g in range(GROUPS):
-            lanes = slice(128 * g, 128 * g + 128)
-            if g > i // 4:
-                value = load(i, g)
-            elif g < i // 4:
-                value = -crossed(load, i, g)
-            else:
-                value = load(i, g) - crossed(load, i, g)
-            allowed = row_key[rows, :] == col[:, lanes]
-            whole[rows, lanes] = jnp.where(allowed, value, 0.0).astype(jnp.bfloat16)
-    for rows in PARTS:
-        yield rows, jnp.dot(whole[rows, :], order[...], preferred_element_type=jnp.float32).astype(jnp.bfloat16)
+    for part in PARTS:
+        for i in range(part.start // 32, part.stop // 32):
+            rows = slice(32 * i, 32 * i + 32)
+            for g in range(GROUPS):
+                lanes = slice(128 * g, 128 * g + 128)
+                if g > i // 4:
+                    value = load(i, g)
+                elif g < i // 4:
+                    value = -crossed(load, i, g)
+                else:
+                    value = load(i, g) - crossed(load, i, g)
+                allowed = row_key[rows, :] == col[:, lanes]
+                whole[rows, lanes] = jnp.where(allowed, value, 0.0).astype(jnp.bfloat16)
+        yield part, jnp.dot(whole[part, :], order[...], preferred_element_type=jnp.float32).astype(jnp.bfloat16)
 
 
 def half_lanes(half):
@@ -348,7 +351,7 @@
     w_s, w_wide, a_two, a_next = lax.optimization_barrier((w_s, w_wide, a_two, a_next))
     w_wide = spread(S - 1, w_s[2:], (w_wide,), "spread_last")
     w_all = lax.all_to_all(w_wide, "row", 0, 0, tiled=True, axis_index_groups=x_groups())
-    a_mine = jnp.stack([a_two, a_next] + [lax.ppermute(a_two, "col", y_swap(k)) for k in STEPS[2:]])
+    a_mine = jnp.stack([a_two, a_next] + [lax.ppermute(a_two, "col", y_swap(k)) for k in (2, 3)])
     a_other = lax.ppermute(a_mine, "col", core_swap())
     row_key, col_key, order = keys(place, occupied_irrep, virtual_irrep)
     lhs, paired0, send0 = pair_first(place, a_mine, a_other, w_all)

time: 95.1 us -> 95.1 us (level)
  the two profiles are of different devices: /device:TPU:129 before, /device:TPU:134 now
where the time goes in v6:
time: 95.1 us; the launch traced here: 94.5 us
  starting transfers between devices  56.2 us (59%)
  waiting for transfers between devices  26.5 us (28%)
  Pallas kernels  9.59 us (10%)
  local copies, waits for them, and re-layouts  1.88 us (2%)
    ppermute x1, waiting for transfers between devices, on_device(): get0 = lax.ppermute(send0, ('row', 'col'), mirror_perm(0))  17 us
    ppermute x1, starting transfers between devices, on_device(): a_far = lax.ppermute(a_own, 'col', h_swap())  14.5 us
    ppermute x3, starting transfers between devices, on_device(): w_s = [lax.ppermute(w_two, 'row', s_shift(k)) for k in STEPS[1:]]  9.56 us
    ppermute x2, starting transfers between devices, on_device(): lax.ppermute(a_two, 'col', y_swap(k))  8.05 us
    ppermute x1, starting transfers between devices, on_device(): get0 = lax.ppermute(send0, ('row', 'col'), mirror_perm(0))  6.63 us
    ppermute x1, starting transfers between devices, on_device(): get1 = lax.ppermute(send1, ('row', 'col'), mirror_perm(1))  5.37 us
    all_to_all x1, starting transfers between devices, on_device(): lax.all_to_all(w_wide, 'row', 0, 0, tiled=True, axis_index_groups=x_group...  4.78 us
    ppermute x2, waiting for transfers between devices, on_device(): lax.ppermute(a_two, 'col', y_swap(k))  4.74 us
  transfers between devices with their start and end apart: 12, of which 6 were waited for; matrix products, arithmetic and copies ran while one was open for 0% of the time, Pallas kernels for 5%

profile of v6, /device:TPU:134, one launch (start us, length us, event | category | flops | bytes accessed | tf_op | source)
XLA Modules:
  0.0 94.5 jit_solution(5051814760820648856)
XLA Ops:
  0.0 0.9 copy-done
  0.9 0.1 pack_w.1
  1.0 1.9 %collective-permute-start = (bf16[32,768]{1,0:T(8,128)(2,1)S(1)}, bf16[32,768]{1,0:T(8,128)(2,1)S(1)}, u32[]{:S(2)}, u32[]{:S(2)}) collective-permute-start(bf16[32,768]{1,0:T(8,128)(2,1)S(1)} %pack_w.1), channel_id=1, source_target_pairs={{0,256},{16,272},{32,288},{48,304},{64,320},{80,336},{96,352},{112... | collective-permute-start | bytes 147464 | tf_op jit(solution)/shard_map/ppermute | solution.py:343
  2.9 0.9 copy-done.1
  3.8 0.1 pack_a.1
  3.9 14.5 %collective-permute-start.2 = (bf16[192,128]{1,0:T(8,128)(2,1)S(1)}, bf16[192,128]{1,0:T(8,128)(2,1)S(1)}, u32[]{:S(2)}, u32[]{:S(2)}) collective-permute-start(bf16[192,128]{1,0:T(8,128)(2,1)S(1)} %pack_a.1), channel_id=1, source_target_pairs={{0,8},{1,9},{2,10},{3,11},{4,12},{5,13},{6,14},{7,15},{8,0},{9,1},... | collective-permute-start | bytes 147464 | tf_op jit(solution)/shard_map/ppermute | solution.py:342
  18.4 2.9 %collective-permute-start.1 = (bf16[2,32,768]{2,1,0:T(8,128)(2,1)S(1)}, bf16[2,32,768]{2,1,0:T(8,128)(2,1)S(1)}, u32[]{:S(2)}, u32[]{:S(2)}) collective-permute-start(bf16[2,32,768]{2,1,0:T(8,128)(2,1)S(1)} %pad_maximum_fusion.1.refs_0_), channel_id=1, source_target_pairs={{0,64},{16,80},{32,96},{48,112},{64,128},{80,144},{96,160},{112,17... | collective-permute-start | bytes 294920 | tf_op jit(solution)/shard_map/ppermute | solution.py:347
  21.3 4.7 %collective-permute-start.3 = (bf16[2,32,768]{2,1,0:T(8,128)(2,1)S(1)}, bf16[2,32,768]{2,1,0:T(8,128)(2,1)S(1)}, u32[]{:S(2)}, u32[]{:S(2)}) collective-permute-start(bf16[2,32,768]{2,1,0:T(8,128)(2,1)S(1)} %pad_maximum_fusion.1.refs_0_), channel_id=1, source_target_pairs={{0,192},{16,208},{32,224},{48,240},{64,0},{80,16},{96,32},{112,48}... | collective-permute-start | bytes 294920 | tf_op jit(solution)/shard_map/ppermute | solution.py:347
  26.1 1.9 %collective-permute-start.4 = (bf16[2,32,768]{2,1,0:T(8,128)(2,1)S(1)}, bf16[2,32,768]{2,1,0:T(8,128)(2,1)S(1)}, u32[]{:S(2)}, u32[]{:S(2)}) collective-permute-start(bf16[2,32,768]{2,1,0:T(8,128)(2,1)S(1)} %pad_maximum_fusion.1.refs_0_), channel_id=1, source_target_pairs={{0,128},{16,144},{32,160},{48,176},{64,192},{80,208},{96,224},{112... | collective-permute-start | bytes 294920 | tf_op jit(solution)/shard_map/ppermute | solution.py:347
  28.1 3.5 %collective-permute-start.5 = (bf16[2,192,128]{2,1,0:T(8,128)(2,1)S(1)}, bf16[2,192,128]{2,1,0:T(8,128)(2,1)S(1)}, u32[]{:S(2)}, u32[]{:S(2)}) collective-permute-start(bf16[2,192,128]{2,1,0:T(8,128)(2,1)S(1)} %pad_maximum_fusion.2), channel_id=1, source_target_pairs={{0,2},{1,3},{2,0},{3,1},{4,6},{5,7},{6,4},{7,5},{8,10},{9,11},{10,... | collective-permute-start | bytes 294920 | tf_op jit(solution)/shard_map/ppermute | solution.py:349
  31.6 1.2 %spread_first.1.refs_0_ = bf16[4,4,2,32,768]{4,3,2,1,0:T(8,128)(2,1)} custom-call(bf16[2,32,768]{2,1,0:T(8,128)(2,1)S(1)} %pad_maximum_fusion.1.refs_0_, bf16[2,32,768]{2,1,0:T(8,128)(2,1)S(1)} %collective-permute-done.1.refs_1_, bf16[2,32,768]{2,1,0:T(8,128)(2,1)S(1)} %collective-permute-done.3.refs_2_), custom_call_target="tpu_custom_call" | custom-call | tf_op jit(solution)/shard_map/spread_first/pallas_call | solution.py:120
  32.7 0.7 collective-permute-done.4.refs_1_
  33.5 1.1 %collective-permute-done.5 = bf16[2,192,128]{2,1,0:T(8,128)(2,1)S(1)} collective-permute-done((bf16[2,192,128]{2,1,0:T(8,128)(2,1)S(1)}, bf16[2,192,128]{2,1,0:T(8,128)(2,1)S(1)}, u32[]{:S(2)}, u32[]{:S(2)}) %collective-permute-start.5) | collective-permute-done | bytes 98336 | tf_op jit(solution)/shard_map/ppermute | solution.py:349
  34.6 0.8 spread_last.1
  35.4 4.8 %all-to-all-start = ((bf16[4,4,2,32,768]{4,3,2,1,0:T(8,128)(2,1)}), bf16[4,4,2,32,768]{4,3,2,1,0:T(8,128)(2,1)S(1)}, u32[]{:S(2)}, u32[]{:S(2)}) async-start(bf16[4,4,2,32,768]{4,3,2,1,0:T(8,128)(2,1)} %spread_last.1), calls=%async_computation | async-start | bytes 3145728 | tf_op jit(solution)/shard_map/all_to_all | solution.py:353
  40.2 5.1 %collective-permute-start.6 = (bf16[2,192,128]{2,1,0:T(8,128)(2,1)S(1)}, bf16[2,192,128]{2,1,0:T(8,128)(2,1)S(1)}, u32[]{:S(2)}, u32[]{:S(2)}) collective-permute-start(bf16[2,192,128]{2,1,0:T(8,128)(2,1)S(1)} %pad_maximum_fusion.2), channel_id=1, source_target_pairs={{0,4},{1,5},{2,6},{3,7},{4,0},{5,1},{6,2},{7,3},{8,12},{9,13},{10,... | collective-permute-start | bytes 294920 | tf_op jit(solution)/shard_map/ppermute | solution.py:354
  45.3 3.0 %collective-permute-start.7 = (bf16[2,192,128]{2,1,0:T(8,128)(2,1)S(1)}, bf16[2,192,128]{2,1,0:T(8,128)(2,1)S(1)}, u32[]{:S(2)}, u32[]{:S(2)}) collective-permute-start(bf16[2,192,128]{2,1,0:T(8,128)(2,1)S(1)} %pad_maximum_fusion.2), channel_id=1, source_target_pairs={{0,6},{1,7},{2,4},{3,5},{4,2},{5,3},{6,0},{7,1},{8,14},{9,15},{10,... | collective-permute-start | bytes 294920 | tf_op jit(solution)/shard_map/ppermute | solution.py:354
  48.2 4.7 %collective-permute-done.7 = bf16[2,192,128]{2,1,0:T(8,128)(2,1)S(1)} collective-permute-done((bf16[2,192,128]{2,1,0:T(8,128)(2,1)S(1)}, bf16[2,192,128]{2,1,0:T(8,128)(2,1)S(1)}, u32[]{:S(2)}, u32[]{:S(2)}) %collective-permute-start.7) | collective-permute-done | bytes 98336 | tf_op jit(solution)/shard_map/ppermute | solution.py:354
  53.0 0.1 pad_maximum_fusion.own_ref
  53.0 1.9 %collective-permute-start.8 = (bf16[4,2,192,128]{3,2,1,0:T(8,128)(2,1)S(1)}, bf16[4,2,192,128]{3,2,1,0:T(8,128)(2,1)S(1)}, u32[]{:S(2)}, u32[]{:S(2)}) collective-permute-start(bf16[4,2,192,128]{3,2,1,0:T(8,128)(2,1)S(1)} %pad_maximum_fusion.own_ref), channel_id=1, source_target_pairs={{0,1},{1,0},{2,3},{3,2},{4,5},{5,4},{6,7},{7,6},{8,9},{9,8},{10,11... | collective-permute-start | bytes 1179656 | tf_op jit(solution)/shard_map/ppermute | solution.py:355
  55.0 0.1 stack.64.place_ref
  55.1 1.5 %collective-permute-done.8.far_ref = bf16[4,2,192,128]{3,2,1,0:T(8,128)(2,1)S(1)} collective-permute-done((bf16[4,2,192,128]{3,2,1,0:T(8,128)(2,1)S(1)}, bf16[4,2,192,128]{3,2,1,0:T(8,128)(2,1)S(1)}, u32[]{:S(2)}, u32[]{:S(2)}) %collective-permute-start.8) | collective-permute-done | bytes 393248 | tf_op jit(solution)/shard_map/ppermute | solution.py:355
  56.7 1.9 %pair_first.1 = (bf16[8,384,128]{2,1,0:T(8,128)(2,1)S(1)}, bf16[384,384]{1,0:T(8,128)(2,1)S(1)}, bf16[528,128]{1,0:T(8,128)(2,1)S(1)}) custom-call(s32[7]{0:T(128)S(1)} %stack.64.place_ref, bf16[4,2,192,128]{3,2,1,0:T(8,128)(2,1)S(1)} %pad_maximum_fusion.own_ref, bf16[4,2,192,128]{3,2,1,0:T(8,128)(2,1)S(1)} %collective-permute-done.8.far_ref, ...), custom_call_target="tpu_custom_call" | custom-call | tf_op jit(solution)/shard_map/pair_first/pallas_call | solution.py:233
  58.6 0.0 copy-start.2
  58.6 6.6 %collective-permute-start.9 = (bf16[528,128]{1,0:T(8,128)(2,1)S(1)}, bf16[528,128]{1,0:T(8,128)(2,1)S(1)}, u32[]{:S(2)}, u32[]{:S(2)}) collective-permute-start(bf16[528,128]{1,0:T(8,128)(2,1)S(1)} %get-tuple-element.26), channel_id=1, source_target_pairs={{0,0},{1,32},{2,64},{3,96},{4,128},{5,160},{6,192},{7,224},{8,256}... | collective-permute-start | bytes 405512 | tf_op jit(solution)/shard_map/ppermute | solution.py:358
  65.3 1.7 %pair_second.1 = (bf16[384,384]{1,0:T(8,128)(2,1)S(1)}, bf16[528,128]{1,0:T(8,128)(2,1)S(1)}) custom-call(s32[7]{0:T(128)S(1)} %stack.64.place_ref, bf16[8,384,128]{2,1,0:T(8,128)(2,1)S(1)} %get-tuple-element.30.lhs, bf16[4,4,2,32,768]{4,3,2,1,0:T(8,128)(2,1)S(1)} %all-to-all-done.w_ref), custom_call_target="tpu_custom_call" | custom-call | tf_op jit(solution)/shard_map/pair_second/pallas_call | solution.py:245
  67.0 5.4 %collective-permute-start.10 = (bf16[528,128]{1,0:T(8,128)(2,1)S(1)}, bf16[528,128]{1,0:T(8,128)(2,1)S(1)}, u32[]{:S(2)}, u32[]{:S(2)}) collective-permute-start(bf16[528,128]{1,0:T(8,128)(2,1)S(1)} %get-tuple-element.32), channel_id=1, source_target_pairs={{0,16},{1,48},{2,80},{3,112},{4,144},{5,176},{6,208},{7,240},{8,27... | collective-permute-start | bytes 405512 | tf_op jit(solution)/shard_map/ppermute | solution.py:360
  72.4 0.8 keys.1
  73.1 17.0 %collective-permute-done.9.get_ref = bf16[528,128]{1,0:T(8,128)(2,1)S(1)} collective-permute-done((bf16[528,128]{1,0:T(8,128)(2,1)S(1)}, bf16[528,128]{1,0:T(8,128)(2,1)S(1)}, u32[]{:S(2)}, u32[]{:S(2)}) %collective-permute-start.9) | collective-permute-done | bytes 135200 | tf_op jit(solution)/shard_map/ppermute | solution.py:358
  90.1 1.2 %finish_first.1.done_ref = bf16[384,384]{1,0:T(8,128)(2,1)S(1)} custom-call(s32[7]{0:T(128)S(1)} %stack.64.place_ref, bf16[384,384]{1,0:T(8,128)(2,1)S(1)} %get-tuple-element.25.paired_ref, bf16[528,128]{1,0:T(8,128)(2,1)S(1)} %collective-permute-done.9.get_ref, s32[384,128]{1,0:T(8,128)S(1)} %get-tuple-element.27.row_key, ...), custom_call_target="tpu_custom_call" | custom-call | tf_op jit(solution)/shard_map/finish_first/pallas_call | solution.py:326
  91.3 1.3 %collective-permute-done.10.get_ref = bf16[528,128]{1,0:T(8,128)(2,1)S(1)} collective-permute-done((bf16[528,128]{1,0:T(8,128)(2,1)S(1)}, bf16[528,128]{1,0:T(8,128)(2,1)S(1)}, u32[]{:S(2)}, u32[]{:S(2)}) %collective-permute-start.10) | collective-permute-done | bytes 135200 | tf_op jit(solution)/shard_map/ppermute | solution.py:360
  92.7 1.9 %finish_second.1 = bf16[384,768]{1,0:T(8,128)(2,1)} custom-call(s32[7]{0:T(128)S(1)} %stack.64.place_ref, bf16[384,384]{1,0:T(8,128)(2,1)S(1)} %finish_first.1.done_ref, bf16[384,384]{1,0:T(8,128)(2,1)S(1)} %get-tuple-element.31.paired_ref, bf16[528,128]{1,0:T(8,128)(2,1)S(1)} %collective-permute-done.10.get_ref, s32[384,128]{1,0:T(8,128)S(1)} %get-tuple-element.27.row_key, ...), custom_call_target="tpu_custom_call" | custom-call | tf_op jit(solution)/shard_map/finish_second/pallas_call | solution.py:326
  (14 shorter events, 0.1 us)
Async XLA Ops:
  0.0 0.9 copy-start
  1.0 17.4 %collective-permute-start = (bf16[32,768]{1,0:T(8,128)(2,1)S(1)}, bf16[32,768]{1,0:T(8,128)(2,1)S(1)}, u32[]{:S(2)}, u32[]{:S(2)}) collective-permute-start(bf16[32,768]{1,0:T(8,128)(2,1)S(1)} %pack_w.1), channel_id=1, source_target_pairs={{0,256},{16,272},{32,288},{48,304},{64,320},{80,336},{96,352},{112... | collective-permute-start | bytes 147464 | tf_op jit(solution)/shard_map/ppermute | solution.py:343
  2.9 0.9 copy-start.1
  3.9 24.1 %collective-permute-start.2 = (bf16[192,128]{1,0:T(8,128)(2,1)S(1)}, bf16[192,128]{1,0:T(8,128)(2,1)S(1)}, u32[]{:S(2)}, u32[]{:S(2)}) collective-permute-start(bf16[192,128]{1,0:T(8,128)(2,1)S(1)} %pack_a.1), channel_id=1, source_target_pairs={{0,8},{1,9},{2,10},{3,11},{4,12},{5,13},{6,14},{7,15},{8,0},{9,1},... | collective-permute-start | bytes 147464 | tf_op jit(solution)/shard_map/ppermute | solution.py:342
  18.4 9.6 %collective-permute-start.1 = (bf16[2,32,768]{2,1,0:T(8,128)(2,1)S(1)}, bf16[2,32,768]{2,1,0:T(8,128)(2,1)S(1)}, u32[]{:S(2)}, u32[]{:S(2)}) collective-permute-start(bf16[2,32,768]{2,1,0:T(8,128)(2,1)S(1)} %pad_maximum_fusion.1.refs_0_), channel_id=1, source_target_pairs={{0,64},{16,80},{32,96},{48,112},{64,128},{80,144},{96,160},{112,17... | collective-permute-start | bytes 294920 | tf_op jit(solution)/shard_map/ppermute | solution.py:347
  21.3 10.2 %collective-permute-start.3 = (bf16[2,32,768]{2,1,0:T(8,128)(2,1)S(1)}, bf16[2,32,768]{2,1,0:T(8,128)(2,1)S(1)}, u32[]{:S(2)}, u32[]{:S(2)}) collective-permute-start(bf16[2,32,768]{2,1,0:T(8,128)(2,1)S(1)} %pad_maximum_fusion.1.refs_0_), channel_id=1, source_target_pairs={{0,192},{16,208},{32,224},{48,240},{64,0},{80,16},{96,32},{112,48}... | collective-permute-start | bytes 294920 | tf_op jit(solution)/shard_map/ppermute | solution.py:347
  26.1 7.4 %collective-permute-start.4 = (bf16[2,32,768]{2,1,0:T(8,128)(2,1)S(1)}, bf16[2,32,768]{2,1,0:T(8,128)(2,1)S(1)}, u32[]{:S(2)}, u32[]{:S(2)}) collective-permute-start(bf16[2,32,768]{2,1,0:T(8,128)(2,1)S(1)} %pad_maximum_fusion.1.refs_0_), channel_id=1, source_target_pairs={{0,128},{16,144},{32,160},{48,176},{64,192},{80,208},{96,224},{112... | collective-permute-start | bytes 294920 | tf_op jit(solution)/shard_map/ppermute | solution.py:347
  28.1 6.5 %collective-permute-start.5 = (bf16[2,192,128]{2,1,0:T(8,128)(2,1)S(1)}, bf16[2,192,128]{2,1,0:T(8,128)(2,1)S(1)}, u32[]{:S(2)}, u32[]{:S(2)}) collective-permute-start(bf16[2,192,128]{2,1,0:T(8,128)(2,1)S(1)} %pad_maximum_fusion.2), channel_id=1, source_target_pairs={{0,2},{1,3},{2,0},{3,1},{4,6},{5,7},{6,4},{7,5},{8,10},{9,11},{10,... | collective-permute-start | bytes 294920 | tf_op jit(solution)/shard_map/ppermute | solution.py:349
  35.4 21.3 %all-to-all-start = ((bf16[4,4,2,32,768]{4,3,2,1,0:T(8,128)(2,1)}), bf16[4,4,2,32,768]{4,3,2,1,0:T(8,128)(2,1)S(1)}, u32[]{:S(2)}, u32[]{:S(2)}) async-start(bf16[4,4,2,32,768]{4,3,2,1,0:T(8,128)(2,1)} %spread_last.1), calls=%async_computation | async-start | bytes 3145728 | tf_op jit(solution)/shard_map/all_to_all | solution.py:353
  40.2 8.1 %collective-permute-start.6 = (bf16[2,192,128]{2,1,0:T(8,128)(2,1)S(1)}, bf16[2,192,128]{2,1,0:T(8,128)(2,1)S(1)}, u32[]{:S(2)}, u32[]{:S(2)}) collective-permute-start(bf16[2,192,128]{2,1,0:T(8,128)(2,1)S(1)} %pad_maximum_fusion.2), channel_id=1, source_target_pairs={{0,4},{1,5},{2,6},{3,7},{4,0},{5,1},{6,2},{7,3},{8,12},{9,13},{10,... | collective-permute-start | bytes 294920 | tf_op jit(solution)/shard_map/ppermute | solution.py:354
  45.3 7.7 %collective-permute-start.7 = (bf16[2,192,128]{2,1,0:T(8,128)(2,1)S(1)}, bf16[2,192,128]{2,1,0:T(8,128)(2,1)S(1)}, u32[]{:S(2)}, u32[]{:S(2)}) collective-permute-start(bf16[2,192,128]{2,1,0:T(8,128)(2,1)S(1)} %pad_maximum_fusion.2), channel_id=1, source_target_pairs={{0,6},{1,7},{2,4},{3,5},{4,2},{5,3},{6,0},{7,1},{8,14},{9,15},{10,... | collective-permute-start | bytes 294920 | tf_op jit(solution)/shard_map/ppermute | solution.py:354
  53.0 3.6 %collective-permute-start.8 = (bf16[4,2,192,128]{3,2,1,0:T(8,128)(2,1)S(1)}, bf16[4,2,192,128]{3,2,1,0:T(8,128)(2,1)S(1)}, u32[]{:S(2)}, u32[]{:S(2)}) collective-permute-start(bf16[4,2,192,128]{3,2,1,0:T(8,128)(2,1)S(1)} %pad_maximum_fusion.own_ref), channel_id=1, source_target_pairs={{0,1},{1,0},{2,3},{3,2},{4,5},{5,4},{6,7},{7,6},{8,9},{9,8},{10,11... | collective-permute-start | bytes 1179656 | tf_op jit(solution)/shard_map/ppermute | solution.py:355
  58.6 13.7 %copy-start.2 = (s32[1024]{0:T(1024)S(1)}, s32[1024]{0:T(1024)}, u32[]{:S(2)}) copy-start(s32[1024]{0:T(1024)} %param.7) | copy-start | bytes 12292
  58.6 13.7 %copy-start.3 = (s32[12]{0:T(128)S(1)}, s32[12]{0:T(128)}, u32[]{:S(2)}) copy-start(s32[12]{0:T(128)} %occ_ref.1) | copy-start | bytes 148
  58.6 31.5 %collective-permute-start.9 = (bf16[528,128]{1,0:T(8,128)(2,1)S(1)}, bf16[528,128]{1,0:T(8,128)(2,1)S(1)}, u32[]{:S(2)}, u32[]{:S(2)}) collective-permute-start(bf16[528,128]{1,0:T(8,128)(2,1)S(1)} %get-tuple-element.26), channel_id=1, source_target_pairs={{0,0},{1,32},{2,64},{3,96},{4,128},{5,160},{6,192},{7,224},{8,256}... | collective-permute-start | bytes 405512 | tf_op jit(solution)/shard_map/ppermute | solution.py:358
  67.0 25.7 %collective-permute-start.10 = (bf16[528,128]{1,0:T(8,128)(2,1)S(1)}, bf16[528,128]{1,0:T(8,128)(2,1)S(1)}, u32[]{:S(2)}, u32[]{:S(2)}) collective-permute-start(bf16[528,128]{1,0:T(8,128)(2,1)S(1)} %get-tuple-element.32), channel_id=1, source_target_pairs={{0,16},{1,48},{2,80},{3,112},{4,144},{5,176},{6,208},{7,240},{8,27... | collective-permute-start | bytes 405512 | tf_op jit(solution)/shard_map/ppermute | solution.py:360

commit v7 on v5

--- a/solution.py
+++ b/solution.py
@@ -207,7 +207,7 @@
 def first_kernel(place_ref, own_ref, far_ref, w_ref, lhs, paired_ref, send_ref, prod, turned):
     core, y, q_own, s_own = place_ref[1], place_ref[2], place_ref[3], place_ref[4]
     for step in range(Y):
-        shift = lax.rem(s_own + S - jnp.bitwise_xor(y, STEPS[step]), S)
+        shift = lax.rem(s_own + S - jnp.bitwise_xor(y, step), S)
         k = jnp.bitwise_xor(shift, shift // 2)
         for h in range(H):
             mine, other = own_ref[step, h], far_ref[step, h]
@@ -348,7 +348,7 @@
     w_s, w_wide, a_two, a_next = lax.optimization_barrier((w_s, w_wide, a_two, a_next))
     w_wide = spread(S - 1, w_s[2:], (w_wide,), "spread_last")
     w_all = lax.all_to_all(w_wide, "row", 0, 0, tiled=True, axis_index_groups=x_groups())
-    a_mine = jnp.stack([a_two, a_next] + [lax.ppermute(a_two, "col", y_swap(k)) for k in STEPS[2:]])
+    a_mine = jnp.stack([a_two, a_next] + [lax.ppermute(a_two, "col", y_swap(k)) for k in (2, 3)])
     a_other = lax.ppermute(a_mine, "col", core_swap())
     row_key, col_key, order = keys(place, occupied_irrep, virtual_irrep)
     lhs, paired0, send0 = pair_first(place, a_mine, a_other, w_all)

time: 95.1 us -> 95.1 us (level)
  the two profiles are of different devices: /device:TPU:129 before, /device:TPU:134 now
where the time goes in v7:
time: 95.1 us; the launch traced here: 94.5 us
  starting transfers between devices  56.2 us (59%)
  waiting for transfers between devices  26.5 us (28%)
  Pallas kernels  9.58 us (10%)
  local copies, waits for them, and re-layouts  1.88 us (2%)
    ppermute x1, waiting for transfers between devices, on_device(): get0 = lax.ppermute(send0, ('row', 'col'), mirror_perm(0))  17 us
    ppermute x1, starting transfers between devices, on_device(): a_far = lax.ppermute(a_own, 'col', h_swap())  14.5 us
    ppermute x3, starting transfers between devices, on_device(): w_s = [lax.ppermute(w_two, 'row', s_shift(k)) for k in STEPS[1:]]  9.56 us
    ppermute x2, starting transfers between devices, on_device(): lax.ppermute(a_two, 'col', y_swap(k))  8.05 us
    ppermute x1, starting transfers between devices, on_device(): get0 = lax.ppermute(send0, ('row', 'col'), mirror_perm(0))  6.63 us
    ppermute x1, starting transfers between devices, on_device(): get1 = lax.ppermute(send1, ('row', 'col'), mirror_perm(1))  5.36 us
    all_to_all x1, starting transfers between devices, on_device(): lax.all_to_all(w_wide, 'row', 0, 0, tiled=True, axis_index_groups=x_group...  4.78 us
    ppermute x2, waiting for transfers between devices, on_device(): lax.ppermute(a_two, 'col', y_swap(k))  4.74 us
  transfers between devices with their start and end apart: 12, of which 6 were waited for; matrix products, arithmetic and copies ran while one was open for 0% of the time, Pallas kernels for 5%

profile of v7, /device:TPU:134, one launch (start us, length us, event | category | flops | bytes accessed | tf_op | source)
XLA Modules:
  0.0 94.5 jit_solution(12365754414271320544)
XLA Ops:
  0.0 0.9 copy-done
  0.9 0.1 pack_w.1
  1.0 1.9 %collective-permute-start = (bf16[32,768]{1,0:T(8,128)(2,1)S(1)}, bf16[32,768]{1,0:T(8,128)(2,1)S(1)}, u32[]{:S(2)}, u32[]{:S(2)}) collective-permute-start(bf16[32,768]{1,0:T(8,128)(2,1)S(1)} %pack_w.1), channel_id=1, source_target_pairs={{0,256},{16,272},{32,288},{48,304},{64,320},{80,336},{96,352},{112... | collective-permute-start | bytes 147464 | tf_op jit(solution)/shard_map/ppermute | solution.py:340
  2.9 0.9 copy-done.1
  3.8 0.1 pack_a.1
  3.9 14.5 %collective-permute-start.2 = (bf16[192,128]{1,0:T(8,128)(2,1)S(1)}, bf16[192,128]{1,0:T(8,128)(2,1)S(1)}, u32[]{:S(2)}, u32[]{:S(2)}) collective-permute-start(bf16[192,128]{1,0:T(8,128)(2,1)S(1)} %pack_a.1), channel_id=1, source_target_pairs={{0,8},{1,9},{2,10},{3,11},{4,12},{5,13},{6,14},{7,15},{8,0},{9,1},... | collective-permute-start | bytes 147464 | tf_op jit(solution)/shard_map/ppermute | solution.py:339
  18.4 2.9 %collective-permute-start.1 = (bf16[2,32,768]{2,1,0:T(8,128)(2,1)S(1)}, bf16[2,32,768]{2,1,0:T(8,128)(2,1)S(1)}, u32[]{:S(2)}, u32[]{:S(2)}) collective-permute-start(bf16[2,32,768]{2,1,0:T(8,128)(2,1)S(1)} %pad_maximum_fusion.1.refs_0_), channel_id=1, source_target_pairs={{0,64},{16,80},{32,96},{48,112},{64,128},{80,144},{96,160},{112,17... | collective-permute-start | bytes 294920 | tf_op jit(solution)/shard_map/ppermute | solution.py:344
  21.3 4.7 %collective-permute-start.3 = (bf16[2,32,768]{2,1,0:T(8,128)(2,1)S(1)}, bf16[2,32,768]{2,1,0:T(8,128)(2,1)S(1)}, u32[]{:S(2)}, u32[]{:S(2)}) collective-permute-start(bf16[2,32,768]{2,1,0:T(8,128)(2,1)S(1)} %pad_maximum_fusion.1.refs_0_), channel_id=1, source_target_pairs={{0,192},{16,208},{32,224},{48,240},{64,0},{80,16},{96,32},{112,48}... | collective-permute-start | bytes 294920 | tf_op jit(solution)/shard_map/ppermute | solution.py:344
  26.1 1.9 %collective-permute-start.4 = (bf16[2,32,768]{2,1,0:T(8,128)(2,1)S(1)}, bf16[2,32,768]{2,1,0:T(8,128)(2,1)S(1)}, u32[]{:S(2)}, u32[]{:S(2)}) collective-permute-start(bf16[2,32,768]{2,1,0:T(8,128)(2,1)S(1)} %pad_maximum_fusion.1.refs_0_), channel_id=1, source_target_pairs={{0,128},{16,144},{32,160},{48,176},{64,192},{80,208},{96,224},{112... | collective-permute-start | bytes 294920 | tf_op jit(solution)/shard_map/ppermute | solution.py:344
  28.1 3.5 %collective-permute-start.5 = (bf16[2,192,128]{2,1,0:T(8,128)(2,1)S(1)}, bf16[2,192,128]{2,1,0:T(8,128)(2,1)S(1)}, u32[]{:S(2)}, u32[]{:S(2)}) collective-permute-start(bf16[2,192,128]{2,1,0:T(8,128)(2,1)S(1)} %pad_maximum_fusion.2), channel_id=1, source_target_pairs={{0,2},{1,3},{2,0},{3,1},{4,6},{5,7},{6,4},{7,5},{8,10},{9,11},{10,... | collective-permute-start | bytes 294920 | tf_op jit(solution)/shard_map/ppermute | solution.py:346
  31.6 1.2 %spread_first.1.refs_0_ = bf16[4,4,2,32,768]{4,3,2,1,0:T(8,128)(2,1)} custom-call(bf16[2,32,768]{2,1,0:T(8,128)(2,1)S(1)} %pad_maximum_fusion.1.refs_0_, bf16[2,32,768]{2,1,0:T(8,128)(2,1)S(1)} %collective-permute-done.1.refs_1_, bf16[2,32,768]{2,1,0:T(8,128)(2,1)S(1)} %collective-permute-done.3.refs_2_), custom_call_target="tpu_custom_call" | custom-call | tf_op jit(solution)/shard_map/spread_first/pallas_call | solution.py:120
  32.7 0.7 collective-permute-done.4.refs_1_
  33.5 1.1 %collective-permute-done.5 = bf16[2,192,128]{2,1,0:T(8,128)(2,1)S(1)} collective-permute-done((bf16[2,192,128]{2,1,0:T(8,128)(2,1)S(1)}, bf16[2,192,128]{2,1,0:T(8,128)(2,1)S(1)}, u32[]{:S(2)}, u32[]{:S(2)}) %collective-permute-start.5) | collective-permute-done | bytes 98336 | tf_op jit(solution)/shard_map/ppermute | solution.py:346
  34.6 0.8 spread_last.1
  35.4 4.8 %all-to-all-start = ((bf16[4,4,2,32,768]{4,3,2,1,0:T(8,128)(2,1)}), bf16[4,4,2,32,768]{4,3,2,1,0:T(8,128)(2,1)S(1)}, u32[]{:S(2)}, u32[]{:S(2)}) async-start(bf16[4,4,2,32,768]{4,3,2,1,0:T(8,128)(2,1)} %spread_last.1), calls=%async_computation | async-start | bytes 3145728 | tf_op jit(solution)/shard_map/all_to_all | solution.py:350
  40.2 5.1 %collective-permute-start.6 = (bf16[2,192,128]{2,1,0:T(8,128)(2,1)S(1)}, bf16[2,192,128]{2,1,0:T(8,128)(2,1)S(1)}, u32[]{:S(2)}, u32[]{:S(2)}) collective-permute-start(bf16[2,192,128]{2,1,0:T(8,128)(2,1)S(1)} %pad_maximum_fusion.2), channel_id=1, source_target_pairs={{0,4},{1,5},{2,6},{3,7},{4,0},{5,1},{6,2},{7,3},{8,12},{9,13},{10,... | collective-permute-start | bytes 294920 | tf_op jit(solution)/shard_map/ppermute | solution.py:351
  45.3 3.0 %collective-permute-start.7 = (bf16[2,192,128]{2,1,0:T(8,128)(2,1)S(1)}, bf16[2,192,128]{2,1,0:T(8,128)(2,1)S(1)}, u32[]{:S(2)}, u32[]{:S(2)}) collective-permute-start(bf16[2,192,128]{2,1,0:T(8,128)(2,1)S(1)} %pad_maximum_fusion.2), channel_id=1, source_target_pairs={{0,6},{1,7},{2,4},{3,5},{4,2},{5,3},{6,0},{7,1},{8,14},{9,15},{10,... | collective-permute-start | bytes 294920 | tf_op jit(solution)/shard_map/ppermute | solution.py:351
  48.2 4.7 %collective-permute-done.7 = bf16[2,192,128]{2,1,0:T(8,128)(2,1)S(1)} collective-permute-done((bf16[2,192,128]{2,1,0:T(8,128)(2,1)S(1)}, bf16[2,192,128]{2,1,0:T(8,128)(2,1)S(1)}, u32[]{:S(2)}, u32[]{:S(2)}) %collective-permute-start.7) | collective-permute-done | bytes 98336 | tf_op jit(solution)/shard_map/ppermute | solution.py:351
  53.0 0.1 pad_maximum_fusion.own_ref
  53.0 1.9 %collective-permute-start.8 = (bf16[4,2,192,128]{3,2,1,0:T(8,128)(2,1)S(1)}, bf16[4,2,192,128]{3,2,1,0:T(8,128)(2,1)S(1)}, u32[]{:S(2)}, u32[]{:S(2)}) collective-permute-start(bf16[4,2,192,128]{3,2,1,0:T(8,128)(2,1)S(1)} %pad_maximum_fusion.own_ref), channel_id=1, source_target_pairs={{0,1},{1,0},{2,3},{3,2},{4,5},{5,4},{6,7},{7,6},{8,9},{9,8},{10,11... | collective-permute-start | bytes 1179656 | tf_op jit(solution)/shard_map/ppermute | solution.py:352
  55.0 0.1 stack.64.place_ref
  55.1 1.5 %collective-permute-done.8.far_ref = bf16[4,2,192,128]{3,2,1,0:T(8,128)(2,1)S(1)} collective-permute-done((bf16[4,2,192,128]{3,2,1,0:T(8,128)(2,1)S(1)}, bf16[4,2,192,128]{3,2,1,0:T(8,128)(2,1)S(1)}, u32[]{:S(2)}, u32[]{:S(2)}) %collective-permute-start.8) | collective-permute-done | bytes 393248 | tf_op jit(solution)/shard_map/ppermute | solution.py:352
  56.7 1.9 %pair_first.1 = (bf16[8,384,128]{2,1,0:T(8,128)(2,1)S(1)}, bf16[384,384]{1,0:T(8,128)(2,1)S(1)}, bf16[528,128]{1,0:T(8,128)(2,1)S(1)}) custom-call(s32[7]{0:T(128)S(1)} %stack.64.place_ref, bf16[4,2,192,128]{3,2,1,0:T(8,128)(2,1)S(1)} %pad_maximum_fusion.own_ref, bf16[4,2,192,128]{3,2,1,0:T(8,128)(2,1)S(1)} %collective-permute-done.8.far_ref, ...), custom_call_target="tpu_custom_call" | custom-call | tf_op jit(solution)/shard_map/pair_first/pallas_call | solution.py:230
  58.6 0.0 copy-start.3
  58.6 6.6 %collective-permute-start.9 = (bf16[528,128]{1,0:T(8,128)(2,1)S(1)}, bf16[528,128]{1,0:T(8,128)(2,1)S(1)}, u32[]{:S(2)}, u32[]{:S(2)}) collective-permute-start(bf16[528,128]{1,0:T(8,128)(2,1)S(1)} %get-tuple-element.26), channel_id=1, source_target_pairs={{0,0},{1,32},{2,64},{3,96},{4,128},{5,160},{6,192},{7,224},{8,256}... | collective-permute-start | bytes 405512 | tf_op jit(solution)/shard_map/ppermute | solution.py:355
  65.3 1.7 %pair_second.1 = (bf16[384,384]{1,0:T(8,128)(2,1)S(1)}, bf16[528,128]{1,0:T(8,128)(2,1)S(1)}) custom-call(s32[7]{0:T(128)S(1)} %stack.64.place_ref, bf16[8,384,128]{2,1,0:T(8,128)(2,1)S(1)} %get-tuple-element.30.lhs, bf16[4,4,2,32,768]{4,3,2,1,0:T(8,128)(2,1)S(1)} %all-to-all-done.w_ref), custom_call_target="tpu_custom_call" | custom-call | tf_op jit(solution)/shard_map/pair_second/pallas_call | solution.py:242
  67.0 5.4 %collective-permute-start.10 = (bf16[528,128]{1,0:T(8,128)(2,1)S(1)}, bf16[528,128]{1,0:T(8,128)(2,1)S(1)}, u32[]{:S(2)}, u32[]{:S(2)}) collective-permute-start(bf16[528,128]{1,0:T(8,128)(2,1)S(1)} %get-tuple-element.32), channel_id=1, source_target_pairs={{0,16},{1,48},{2,80},{3,112},{4,144},{5,176},{6,208},{7,240},{8,27... | collective-permute-start | bytes 405512 | tf_op jit(solution)/shard_map/ppermute | solution.py:357
  72.3 0.8 keys.1
  73.1 17.0 %collective-permute-done.9.get_ref = bf16[528,128]{1,0:T(8,128)(2,1)S(1)} collective-permute-done((bf16[528,128]{1,0:T(8,128)(2,1)S(1)}, bf16[528,128]{1,0:T(8,128)(2,1)S(1)}, u32[]{:S(2)}, u32[]{:S(2)}) %collective-permute-start.9) | collective-permute-done | bytes 135200 | tf_op jit(solution)/shard_map/ppermute | solution.py:355
  90.1 1.2 %finish_first.1.done_ref = bf16[384,384]{1,0:T(8,128)(2,1)S(1)} custom-call(s32[7]{0:T(128)S(1)} %stack.64.place_ref, bf16[384,384]{1,0:T(8,128)(2,1)S(1)} %get-tuple-element.25.paired_ref, bf16[528,128]{1,0:T(8,128)(2,1)S(1)} %collective-permute-done.9.get_ref, s32[384,128]{1,0:T(8,128)S(1)} %get-tuple-element.27.row_key, ...), custom_call_target="tpu_custom_call" | custom-call | tf_op jit(solution)/shard_map/finish_first/pallas_call | solution.py:323
  91.3 1.3 %collective-permute-done.10.get_ref = bf16[528,128]{1,0:T(8,128)(2,1)S(1)} collective-permute-done((bf16[528,128]{1,0:T(8,128)(2,1)S(1)}, bf16[528,128]{1,0:T(8,128)(2,1)S(1)}, u32[]{:S(2)}, u32[]{:S(2)}) %collective-permute-start.10) | collective-permute-done | bytes 135200 | tf_op jit(solution)/shard_map/ppermute | solution.py:357
  92.7 1.9 %finish_second.1 = bf16[384,768]{1,0:T(8,128)(2,1)} custom-call(s32[7]{0:T(128)S(1)} %stack.64.place_ref, bf16[384,384]{1,0:T(8,128)(2,1)S(1)} %finish_first.1.done_ref, bf16[384,384]{1,0:T(8,128)(2,1)S(1)} %get-tuple-element.31.paired_ref, bf16[528,128]{1,0:T(8,128)(2,1)S(1)} %collective-permute-done.10.get_ref, s32[384,128]{1,0:T(8,128)S(1)} %get-tuple-element.27.row_key, ...), custom_call_target="tpu_custom_call" | custom-call | tf_op jit(solution)/shard_map/finish_second/pallas_call | solution.py:323
  (14 shorter events, 0.1 us)
Async XLA Ops:
  0.0 0.9 copy-start
  1.0 17.4 %collective-permute-start = (bf16[32,768]{1,0:T(8,128)(2,1)S(1)}, bf16[32,768]{1,0:T(8,128)(2,1)S(1)}, u32[]{:S(2)}, u32[]{:S(2)}) collective-permute-start(bf16[32,768]{1,0:T(8,128)(2,1)S(1)} %pack_w.1), channel_id=1, source_target_pairs={{0,256},{16,272},{32,288},{48,304},{64,320},{80,336},{96,352},{112... | collective-permute-start | bytes 147464 | tf_op jit(solution)/shard_map/ppermute | solution.py:340
  2.9 0.9 copy-start.1
  3.9 24.1 %collective-permute-start.2 = (bf16[192,128]{1,0:T(8,128)(2,1)S(1)}, bf16[192,128]{1,0:T(8,128)(2,1)S(1)}, u32[]{:S(2)}, u32[]{:S(2)}) collective-permute-start(bf16[192,128]{1,0:T(8,128)(2,1)S(1)} %pack_a.1), channel_id=1, source_target_pairs={{0,8},{1,9},{2,10},{3,11},{4,12},{5,13},{6,14},{7,15},{8,0},{9,1},... | collective-permute-start | bytes 147464 | tf_op jit(solution)/shard_map/ppermute | solution.py:339
  18.4 9.6 %collective-permute-start.1 = (bf16[2,32,768]{2,1,0:T(8,128)(2,1)S(1)}, bf16[2,32,768]{2,1,0:T(8,128)(2,1)S(1)}, u32[]{:S(2)}, u32[]{:S(2)}) collective-permute-start(bf16[2,32,768]{2,1,0:T(8,128)(2,1)S(1)} %pad_maximum_fusion.1.refs_0_), channel_id=1, source_target_pairs={{0,64},{16,80},{32,96},{48,112},{64,128},{80,144},{96,160},{112,17... | collective-permute-start | bytes 294920 | tf_op jit(solution)/shard_map/ppermute | solution.py:344
  21.3 10.2 %collective-permute-start.3 = (bf16[2,32,768]{2,1,0:T(8,128)(2,1)S(1)}, bf16[2,32,768]{2,1,0:T(8,128)(2,1)S(1)}, u32[]{:S(2)}, u32[]{:S(2)}) collective-permute-start(bf16[2,32,768]{2,1,0:T(8,128)(2,1)S(1)} %pad_maximum_fusion.1.refs_0_), channel_id=1, source_target_pairs={{0,192},{16,208},{32,224},{48,240},{64,0},{80,16},{96,32},{112,48}... | collective-permute-start | bytes 294920 | tf_op jit(solution)/shard_map/ppermute | solution.py:344
  26.1 7.4 %collective-permute-start.4 = (bf16[2,32,768]{2,1,0:T(8,128)(2,1)S(1)}, bf16[2,32,768]{2,1,0:T(8,128)(2,1)S(1)}, u32[]{:S(2)}, u32[]{:S(2)}) collective-permute-start(bf16[2,32,768]{2,1,0:T(8,128)(2,1)S(1)} %pad_maximum_fusion.1.refs_0_), channel_id=1, source_target_pairs={{0,128},{16,144},{32,160},{48,176},{64,192},{80,208},{96,224},{112... | collective-permute-start | bytes 294920 | tf_op jit(solution)/shard_map/ppermute | solution.py:344
  28.1 6.5 %collective-permute-start.5 = (bf16[2,192,128]{2,1,0:T(8,128)(2,1)S(1)}, bf16[2,192,128]{2,1,0:T(8,128)(2,1)S(1)}, u32[]{:S(2)}, u32[]{:S(2)}) collective-permute-start(bf16[2,192,128]{2,1,0:T(8,128)(2,1)S(1)} %pad_maximum_fusion.2), channel_id=1, source_target_pairs={{0,2},{1,3},{2,0},{3,1},{4,6},{5,7},{6,4},{7,5},{8,10},{9,11},{10,... | collective-permute-start | bytes 294920 | tf_op jit(solution)/shard_map/ppermute | solution.py:346
  35.4 21.3 %all-to-all-start = ((bf16[4,4,2,32,768]{4,3,2,1,0:T(8,128)(2,1)}), bf16[4,4,2,32,768]{4,3,2,1,0:T(8,128)(2,1)S(1)}, u32[]{:S(2)}, u32[]{:S(2)}) async-start(bf16[4,4,2,32,768]{4,3,2,1,0:T(8,128)(2,1)} %spread_last.1), calls=%async_computation | async-start | bytes 3145728 | tf_op jit(solution)/shard_map/all_to_all | solution.py:350
  40.2 8.1 %collective-permute-start.6 = (bf16[2,192,128]{2,1,0:T(8,128)(2,1)S(1)}, bf16[2,192,128]{2,1,0:T(8,128)(2,1)S(1)}, u32[]{:S(2)}, u32[]{:S(2)}) collective-permute-start(bf16[2,192,128]{2,1,0:T(8,128)(2,1)S(1)} %pad_maximum_fusion.2), channel_id=1, source_target_pairs={{0,4},{1,5},{2,6},{3,7},{4,0},{5,1},{6,2},{7,3},{8,12},{9,13},{10,... | collective-permute-start | bytes 294920 | tf_op jit(solution)/shard_map/ppermute | solution.py:351
  45.3 7.7 %collective-permute-start.7 = (bf16[2,192,128]{2,1,0:T(8,128)(2,1)S(1)}, bf16[2,192,128]{2,1,0:T(8,128)(2,1)S(1)}, u32[]{:S(2)}, u32[]{:S(2)}) collective-permute-start(bf16[2,192,128]{2,1,0:T(8,128)(2,1)S(1)} %pad_maximum_fusion.2), channel_id=1, source_target_pairs={{0,6},{1,7},{2,4},{3,5},{4,2},{5,3},{6,0},{7,1},{8,14},{9,15},{10,... | collective-permute-start | bytes 294920 | tf_op jit(solution)/shard_map/ppermute | solution.py:351
  53.0 3.6 %collective-permute-start.8 = (bf16[4,2,192,128]{3,2,1,0:T(8,128)(2,1)S(1)}, bf16[4,2,192,128]{3,2,1,0:T(8,128)(2,1)S(1)}, u32[]{:S(2)}, u32[]{:S(2)}) collective-permute-start(bf16[4,2,192,128]{3,2,1,0:T(8,128)(2,1)S(1)} %pad_maximum_fusion.own_ref), channel_id=1, source_target_pairs={{0,1},{1,0},{2,3},{3,2},{4,5},{5,4},{6,7},{7,6},{8,9},{9,8},{10,11... | collective-permute-start | bytes 1179656 | tf_op jit(solution)/shard_map/ppermute | solution.py:352
  58.6 13.7 %copy-start.2 = (s32[1024]{0:T(1024)S(1)}, s32[1024]{0:T(1024)}, u32[]{:S(2)}) copy-start(s32[1024]{0:T(1024)} %param.7) | copy-start | bytes 12292
  58.6 13.7 %copy-start.3 = (s32[12]{0:T(128)S(1)}, s32[12]{0:T(128)}, u32[]{:S(2)}) copy-start(s32[12]{0:T(128)} %occ_ref.1) | copy-start | bytes 148
  58.6 31.5 %collective-permute-start.9 = (bf16[528,128]{1,0:T(8,128)(2,1)S(1)}, bf16[528,128]{1,0:T(8,128)(2,1)S(1)}, u32[]{:S(2)}, u32[]{:S(2)}) collective-permute-start(bf16[528,128]{1,0:T(8,128)(2,1)S(1)} %get-tuple-element.26), channel_id=1, source_target_pairs={{0,0},{1,32},{2,64},{3,96},{4,128},{5,160},{6,192},{7,224},{8,256}... | collective-permute-start | bytes 405512 | tf_op jit(solution)/shard_map/ppermute | solution.py:355
  67.0 25.7 %collective-permute-start.10 = (bf16[528,128]{1,0:T(8,128)(2,1)S(1)}, bf16[528,128]{1,0:T(8,128)(2,1)S(1)}, u32[]{:S(2)}, u32[]{:S(2)}) collective-permute-start(bf16[528,128]{1,0:T(8,128)(2,1)S(1)} %get-tuple-element.32), channel_id=1, source_target_pairs={{0,16},{1,48},{2,80},{3,112},{4,144},{5,176},{6,208},{7,240},{8,27... | collective-permute-start | bytes 405512 | tf_op jit(solution)/shard_map/ppermute | solution.py:357
